TPU v7x, 256 devices: a whole 4x4x8 slice. The times are simulated.
256 devices in a mesh: blk: 64 (over z, x_lo, y), pair: 4 (over x_hi, core).
Axes of the slice: x: 4 (x_hi: 2, x_lo: 2; x = x_hi * 2 + x_lo), y: 4, z: 8, core: 2. Of those that a mesh axis runs over, the one named last changes fastest.
Arguments:
- points: float32 [8, 32768], P(None, ('blk', 'pair')), may hold values from -6 to 6
- lengthscale: float32 [8], replicated, may hold values from 0.8 to 4
- targets: float32 [8, 32768], P(None, ('blk', 'pair')), may hold values from -6 to 6
Outputs:
- residual: float32 [8, 32768], P(None, ('blk', 'pair'))
- direction: float32 [8, 32768], P(None, ('blk', 'pair'))
All inputs are finite; a program needn't handle non-finite values.
Results may differ from a plain program's by a relative error of at most 0.0003.
Values sent between devices are 32-bit elements; how exact they have to be, the bound alone decides.
No kernel may reach another device: no remote copies, remote signals or barrier semaphores. Data moves between devices by JAX's collectives and lax.ppermute only.
A program may use at most 64 MiB of HBM per device.

v0:
```python
import math

import jax
import jax.numpy as jnp
from jax import lax
from jax.sharding import PartitionSpec as P

ITERS = 2


root_five = math.sqrt(5.0)
noise_level = 0.5


def kernel_block(left_pts, left_square, right_pts, right_square):
    inner_part = jnp.dot(
        left_pts.T, right_pts, precision=lax.Precision.HIGHEST, preferred_element_type=jnp.float32
    )
    dist_square = jnp.maximum(left_square[:, None] + right_square[None, :] - 2.0 * inner_part, 0.0)
    scaled_dist = root_five * jnp.sqrt(dist_square)
    return (1.0 + scaled_dist + scaled_dist * scaled_dist / 3.0) * jnp.exp(-scaled_dist)


def squares(residual):
    return lax.psum(jnp.sum(residual * residual, axis=1), ("blk", "pair"))


def per_device(points, lengthscale, targets):
    own_scaled = points / lengthscale[:, None]
    own_square = jnp.sum(own_scaled * own_scaled, axis=0)
    all_scaled = lax.all_gather(own_scaled, ("blk", "pair"), axis=1, tiled=True)
    all_square = jnp.sum(all_scaled * all_scaled, axis=0)
    residual = targets
    direction = targets
    norm_now = squares(residual)
    for iteration in range(ITERS):
        local_block = lax.all_gather(direction, "pair", axis=1, tiled=True)
        kernel_tile = kernel_block(own_scaled, own_square, all_scaled, all_square)
        product = jnp.dot(
            lax.all_gather(local_block, "blk", axis=1, tiled=True),
            kernel_tile.T,
            precision=lax.Precision.HIGHEST,
            preferred_element_type=jnp.float32,
        )
        image_vec = product + noise_level * direction
        curvature = lax.psum(jnp.sum(direction * image_vec, axis=1), ("blk", "pair"))
        step_size = norm_now / curvature
        residual = residual - step_size[:, None] * image_vec
        norm_next = squares(residual)
        direction = residual + (norm_next / norm_now)[:, None] * direction
        norm_now = norm_next
    return (residual, direction)


def solution(mesh):
    placed = (P(None, ("blk", "pair")), P(), P(None, ("blk", "pair")))
    return jax.shard_map(
        per_device,
        mesh=mesh,
        in_specs=placed,
        out_specs=(P(None, ("blk", "pair")), P(None, ("blk", "pair"))),
        check_vma=False,
    )
```

profile of v0, /device:TPU:8, one launch (start us, length us, event | category | flops | bytes accessed | tf_op | source)
XLA Modules:
  0.0 1323.6 jit_solution(10025386335485265388)
XLA Ops:
  7.2 0.0 all-gather.4.cloned.1.call-start
  7.2 1.4 multiply_reduce_fusion.5
  8.6 0.0 all-gather.4.cloned.1.call-update
  8.6 0.0 all-gather.6.cloned.1.call-start
  8.6 8.1 all_gather.16
  16.7 0.0 all-gather.6.cloned.1.call-update
  16.7 0.0 all-gather.8.cloned.1.call-start
  16.8 375.1 %all-gather.4.cloned.1.call-done = f32[8,32768]{1,0:T(8,128)} async-done(((f32[8,128]{1,0:T(8,128)}), f32[8,32768]{1,0:T(8,128)}) %all-gather.4.cloned.1.call-update) | async-done | bytes 1048592 | tf_op jit(solution)/shard_map/all_gather | solution.py:31
  391.9 1.5 multiply_reduce_fusion
  393.4 0.0 copy-start
  393.4 27.2 %exponential_multiply_fusion = f32[128,32768]{1,0:T(8,128)} fusion(f32[8,128]{1,0:T(8,128)} %get-tuple-element.9, f32[8,32768]{1,0:T(8,128)} %all-gather.4.cloned.1.call-done, f32[32768]{0:T(1024)S(1)} %multiply_reduce_fusion, f32[128]{0:T(128)S(1)} %get-tuple-element.8), kind=kOutput, calls=%fused_computation.5 | convolution fusion | flops 448790528 | bytes 17961472 | tf_op jit(solution)/shard_map/dot_general | solution.py:16
  420.6 266.1 %all-gather.6.cloned.1.call-done = f32[8,32768]{1,0:T(8,128)} async-done(((f32[8,512]{1,0:T(8,128)}), f32[8,32768]{1,0:T(8,128)}) %all-gather.6.cloned.1.call-update) | async-done | bytes 1048592 | tf_op jit(solution)/shard_map/all_gather | solution.py:40
  686.7 0.0 copy-done
  686.8 16.3 %multiply_reduce_fusion.4 = (f32[8]{0:T(128)S(1)}, f32[8]{0:T(128)S(1)}, f32[8,128]{1,0:T(8,128)S(1)}) fusion(f32[8,128]{1,0:T(8,128)S(1)} %copy-done, f32[128,32768]{1,0:T(8,128)} %exponential_multiply_fusion, f32[8,32768]{1,0:T(8,128)} %all-gather.6.cloned.1.call-done), kind=kOutput, calls=%fused_computation.17 | convolution fusion | flops 402659328 | bytes 17834048 | tf_op jit(solution)/shard_map/dot_general | solution.py:39
  703.1 75.0 %all-reduce = (f32[8]{0:T(128)S(1)}, f32[8]{0:T(128)S(1)}) all-reduce(f32[8]{0:T(128)S(1)} %get-tuple-element.3, f32[8]{0:T(128)S(1)} %get-tuple-element.2), channel_id=1, replica_groups=mesh['blk'=64,'pair'=4] {'blk','pair'}, use_global_device_ids=true, to_apply=%region_1.0 | all-reduce | flops 16 | bytes 128 | tf_op jit(solution)/shard_map/psum | solution.py:25
  778.1 0.2 multiply_reduce_fusion.3
  778.3 73.4 %psum.37 = f32[8]{0:T(128)S(1)} all-reduce(f32[8]{0:T(128)S(1)} %multiply_reduce_fusion.3), channel_id=1, replica_groups=mesh['blk'=64,'pair'=4] {'blk','pair'}, use_global_device_ids=true, to_apply=%region_7.0 | all-reduce | flops 8 | bytes 64 | tf_op jit(solution)/shard_map/psum | solution.py:25
  851.7 0.1 multiply_add_fusion.1
  851.8 7.1 all_gather.18
  858.9 0.0 all-gather.8.cloned.1.call-update
  858.9 292.6 %all-gather.8.cloned.1.call-done = f32[8,32768]{1,0:T(8,128)} async-done(((f32[8,512]{1,0:T(8,128)}), f32[8,32768]{1,0:T(8,128)}) %all-gather.8.cloned.1.call-update) | async-done | bytes 1048592 | tf_op jit(solution)/shard_map/all_gather | solution.py:40
  1151.5 16.4 %multiply_reduce_fusion.2 = (f32[8]{0:T(128)S(1)}, f32[8,128]{1,0:T(8,128)S(1)}) fusion(f32[8,128]{1,0:T(8,128)S(1)} %multiply_add_fusion.1, f32[8,32768]{1,0:T(8,128)} %all-gather.8.cloned.1.call-done, f32[128,32768]{1,0:T(8,128)} %exponential_multiply_fusion), kind=kOutput, calls=%fused_computation.13 | convolution fusion | flops 402657280 | bytes 17834016 | tf_op jit(solution)/shard_map/dot_general | solution.py:39
  1168.0 74.8 %psum.38 = f32[8]{0:T(128)S(1)} all-reduce(f32[8]{0:T(128)S(1)} %get-tuple-element.11), channel_id=1, replica_groups=mesh['blk'=64,'pair'=4] {'blk','pair'}, use_global_device_ids=true, to_apply=%region_9.0 | all-reduce | flops 8 | bytes 64 | tf_op jit(solution)/shard_map/psum | solution.py:46
  1242.8 0.2 multiply_reduce_fusion.1
  1243.0 0.0 copy-start.1
  1243.0 73.4 %psum.39 = f32[8]{0:T(128)S(1)} all-reduce(f32[8]{0:T(128)S(1)} %get-tuple-element.6), channel_id=1, replica_groups=mesh['blk'=64,'pair'=4] {'blk','pair'}, use_global_device_ids=true, to_apply=%region_11.0 | all-reduce | flops 8 | bytes 64 | tf_op jit(solution)/shard_map/psum | solution.py:25
  1316.4 0.7 multiply_add_fusion
  1317.1 0.0 copy-done.1
  (4 shorter events, 0.0 us)
Async XLA Ops:
  7.2 384.7 %all-gather.4.cloned.1.call-start = ((), (), s32[]{:S(2)}) async-start(), calls=%async_computation | async-start | bytes 1052672 | tf_op jit(solution)/shard_map/all_gather | solution.py:31
  8.6 678.2 %all-gather.6.cloned.1.call-start = ((), (), s32[]{:S(2)}) async-start(), calls=%async_computation.1 | async-start | bytes 1064960 | tf_op jit(solution)/shard_map/all_gather | solution.py:40
  16.7 1134.8 %all-gather.8.cloned.1.call-start = ((), (), s32[]{:S(2)}) async-start(), calls=%async_computation.2 | async-start | bytes 1064960 | tf_op jit(solution)/shard_map/all_gather | solution.py:40
  393.4 293.3 %copy-start = (f32[8,128]{1,0:T(8,128)S(1)}, f32[8,128]{1,0:T(8,128)}, u32[]{:S(2)}) copy-start(f32[8,128]{1,0:T(8,128)} %param.5) | copy-start | bytes 12292
  1243.0 74.1 %copy-start.1 = (f32[8,128]{1,0:T(8,128)}, f32[8,128]{1,0:T(8,128)S(1)}, u32[]{:S(2)}) copy-start(f32[8,128]{1,0:T(8,128)S(1)} %get-tuple-element.7) | copy-start | bytes 12292
Sparse Core Ops, SparseCore 0:
  10.4 381.4 all-gather.3
  393.7 293.0 all-gather.5
  859.0 292.4 all-gather.7
where the time goes:
time: 1330 us; the launch traced here: 1320 us
  waiting for transfers between devices  934 us (70%)
  blocking collectives  312 us (23%)
  matrix products  60 us (5%)
  between operations  13.8 us (1%)
    all_gather x2, waiting for transfers between devices, per_device(): lax.all_gather(local_block, 'blk', axis=1, tiled=True)  559 us
    all_gather x1, waiting for transfers between devices, per_device(): all_scaled = lax.all_gather(own_scaled, ('blk', 'pair'), axis=1, tiled=True)  375 us
    psum x3, blocking collectives, squares(): return lax.psum(jnp.sum(residual * residual, axis=1), ('blk', 'pair'))  222 us
    psum x1, blocking collectives, per_device(): lax.psum(jnp.sum(direction * image_vec, axis=1), ('blk', 'pair'))  74.8 us
    dot_general x2, matrix products, per_device(): jnp.dot(lax.all_gather(local_block, 'blk', axis=1, tiled=True), kernel_ti...  32.7 us
    dot_general x1, matrix products, kernel_block(): jnp.dot(left_pts.T, right_pts, precision=lax.Precision.HIGHEST, preferred...  27.2 us
  transfers between devices with their start and end apart: 3, of which 3 were waited for; matrix products, arithmetic and copies ran while one was open for 2% of the time, Pallas kernels for 0%

commit v1 on v0

v1 whole, which is shorter than its diff:
```python
import math

import jax
import jax.numpy as jnp
from jax import lax
from jax.experimental import pallas as pl
from jax.experimental.pallas import tpu as pltpu
from jax.sharding import Mesh
from jax.sharding import PartitionSpec as P

f32 = jnp.float32
bf16 = jnp.bfloat16
VMEM = pltpu.VMEM

AXES = ("z", "xl", "y", "xh", "core")
SIZES = (8, 2, 4, 2, 2)
ROWG = ("xl", "xh", "core")
COLG = ("z", "y")
NR, NC = 8, 32
OWN = 128
NI, NJ = NR * OWN, NC * OWN
noise_level = 0.5

POINT_SCALE = math.sqrt(5.0 / 3.0)
ROOT3 = math.sqrt(3.0)
EXP_SCALE = -math.sqrt(3.0) * math.log2(math.e)

TI, TJ = 256, 256


def pieces(x):
    first = x.astype(bf16).astype(f32)
    rest = x - first
    second = rest.astype(bf16).astype(f32)
    return first, second, rest - second


def features(x, left):
    x = x * POINT_SCALE
    square = jnp.sum(x * x, axis=0, keepdims=True)
    a, b, c = pieces(x)
    s1, s2, s3 = pieces(square)
    one, zero = jnp.ones_like(square), jnp.zeros_like(square)
    if left:
        tail = [s1, s2, s3, one, one, one, zero, zero]
        parts = [a, a, b, b, a, c]
    else:
        tail = [one, one, one, s1, s2, s3, zero, zero]
        parts = [-2.0 * a, -2.0 * b, -2.0 * a, -2.0 * b, -2.0 * c, -2.0 * a]
    return jnp.concatenate(parts + [jnp.concatenate(tail, 0), jnp.zeros_like(a)], 0)


def matern(tau):
    tau = jnp.maximum(tau, 1e-30)
    s = tau * lax.rsqrt(tau)
    return ((1.0 + tau) + ROOT3 * s) * jnp.exp2(EXP_SCALE * s)


def stacked(values):
    return jnp.concatenate(pieces(values), 0).astype(bf16)


def lanes(ref, first_row, count, start=0):
    return jnp.concatenate(
        [ref[start + k, first_row : first_row + 8, :] for k in range(count)], 1
    )


def total(x):
    return jnp.sum(x, axis=1, keepdims=True)


def first_product(rows_ref, cols_ref, high_ref, low_ref, out_ref):
    left = features(lanes(rows_ref, 0, NR), True).astype(bf16)
    right = features(lanes(cols_ref, 0, NC), False).T.astype(bf16)
    values = stacked(lanes(cols_ref, 8, NC))
    for i in range(0, NI, TI):
        acc = jnp.zeros((24, TI), f32)
        for j in range(0, NJ, TJ):
            tau = jnp.dot(right[j : j + TJ], left[:, i : i + TI], preferred_element_type=f32)
            tile = matern(tau)
            high = tile.astype(bf16)
            low = (tile - high.astype(f32)).astype(bf16)
            high_ref[j : j + TJ, i : i + TI] = high
            low_ref[j : j + TJ, i : i + TI] = low
            part = values[:, j : j + TJ]
            acc = acc + jnp.dot(part, high, preferred_element_type=f32)
            acc = acc + jnp.dot(part, low, preferred_element_type=f32)
        write_partial(out_ref, acc, i)


def write_partial(out_ref, acc, i):
    acc = acc[0:8] + acc[8:16] + acc[16:24]
    for k in range(TI // OWN):
        row = (i // OWN + k) * 8
        for copy in range(NR):
            out_ref[copy, row : row + 8, :] = acc[:, k * OWN : (k + 1) * OWN]


def block_rows(ref):
    out = []
    for k in range(NR):
        acc = ref[0, 8 * k : 8 * k + 8, :]
        for copy in range(1, NR):
            acc = acc + ref[copy, 8 * k : 8 * k + 8, :]
        out.append(acc)
    return out


def at_lanes(columns):
    lane = lax.broadcasted_iota(jnp.int32, (8, OWN), 1)
    out = jnp.zeros((8, OWN), f32)
    for k, column in enumerate(columns):
        out = jnp.where(lane == k, column, out)
    return out


def my_row_block():
    return lax.axis_index("xl") * 4 + lax.axis_index("xh") * 2 + lax.axis_index("core")


def first_image(mine_ref, part_ref, rows_ref, image_ref, out_ref):
    parts = block_rows(part_ref)
    bb = jnp.zeros((8, OWN), f32)
    bw = jnp.zeros((8, OWN), f32)
    for k in range(NR):
        target = rows_ref[k, 8:16, :]
        image = parts[k] + noise_level * target
        image_ref[k] = image
        bb = bb + target * target
        bw = bw + target * image
    own = image_ref[mine_ref[0]]
    scalars = at_lanes([total(bb), total(bw)])
    for copy in range(NC):
        out_ref[copy, 0:8, :] = own
        out_ref[copy, 8:16, :] = scalars


def second_product(cols_ref, image_cols_ref, high_ref, low_ref, out_ref, scalar_ref):
    sums = image_cols_ref[0, 8:16, :]
    for k in range(1, NC):
        sums = sums + image_cols_ref[k, 8:16, :]
    norm = sums[:, 0:1]
    step = norm / sums[:, 1:2]
    residual = lanes(cols_ref, 8, NC) - step * lanes(image_cols_ref, 0, NC)
    norm_part = total(residual * residual)
    values = stacked(residual)
    for i in range(0, NI, TI):
        acc = jnp.dot(values, high_ref[:, i : i + TI], preferred_element_type=f32)
        acc = acc + jnp.dot(values, low_ref[:, i : i + TI], preferred_element_type=f32)
        write_partial(out_ref, acc, i)
    for copy in range(NR):
        out_ref[copy, NI // OWN * 8 :, :] = jnp.broadcast_to(norm_part, (8, OWN))
    scalar_ref[...] = at_lanes([norm, step])


def second_image(mine_ref, part_ref, rows_ref, image_ref, scalar_ref, own_ref, out_ref, keep_ref):
    parts = block_rows(part_ref)
    norm, step = scalar_ref[:, 0:1], scalar_ref[:, 1:2]
    norm_next = part_ref[0, NI // OWN * 8 :, 0:1]
    for copy in range(1, NR):
        norm_next = norm_next + part_ref[copy, NI // OWN * 8 :, 0:1]
    ratio = norm_next / norm
    residuals, images = [], []
    di = jnp.zeros((8, OWN), f32)
    ri = jnp.zeros((8, OWN), f32)
    ii = jnp.zeros((8, OWN), f32)
    for k in range(NR):
        target = rows_ref[k, 8:16, :]
        image0 = image_ref[k]
        residual = target - step * image0
        direction = residual + ratio * target
        image = (parts[k] + noise_level * residual) + ratio * image0
        keep_ref[0, k] = residual
        keep_ref[1, k] = direction
        keep_ref[2, k] = image
        residuals.append(residual)
        images.append(image)
        di = di + direction * image
        ri = ri + residual * image
        ii = ii + image * image
    ii = total(ii)
    guess = total(ri) / jnp.where(ii > 0.0, ii, 1.0)
    ss = jnp.zeros((8, OWN), f32)
    si = jnp.zeros((8, OWN), f32)
    for k in range(NR):
        left = residuals[k] - guess * images[k]
        ss = ss + left * left
        si = si + left * images[k]
    scalars = at_lanes([total(di), guess, total(ss), total(si), ii])
    for copy in range(NC):
        out_ref[copy] = scalars
    own_ref[0] = keep_ref[0, mine_ref[0]]
    own_ref[1] = keep_ref[1, mine_ref[0]]
    own_ref[2] = keep_ref[2, mine_ref[0]]
    own_ref[3] = jnp.broadcast_to(norm_next, (8, OWN))


def finish(own_ref, sums_ref, residual_ref, direction_ref):
    norm = own_ref[3][:, 0:1]
    curvature = sums_ref[0][:, 0:1]
    for k in range(1, NC):
        curvature = curvature + sums_ref[k][:, 0:1]
    step = norm / curvature
    norm_next = jnp.zeros((8, 1), f32)
    for k in range(NC):
        block = sums_ref[k]
        off = step - block[:, 1:2]
        norm_next = norm_next + (block[:, 2:3] + off * (off * block[:, 4:5] - 2.0 * block[:, 3:4]))
    residual = own_ref[0] - step * own_ref[2]
    residual_ref[...] = residual
    direction_ref[...] = residual + (norm_next / norm) * own_ref[1]


def call(kernel, outs, name, args, scratch=(), vmem=48 << 20):
    return pl.pallas_call(
        kernel,
        in_specs=[
            pl.BlockSpec(memory_space=pltpu.SMEM if a.dtype == jnp.int32 else VMEM) for a in args
        ],
        out_specs=[pl.BlockSpec(memory_space=VMEM)] * len(outs),
        out_shape=outs,
        scratch_shapes=scratch,
        compiler_params=pltpu.CompilerParams(vmem_limit_bytes=vmem),
        name=name,
    )(*args)


def shape(*dims):
    return jax.ShapeDtypeStruct(dims, f32)


def per_device(points, lengthscale, targets):
    mine = my_row_block().astype(jnp.int32).reshape(1)
    own = jnp.concatenate([points / lengthscale[:, None], targets], 0)
    rows = lax.all_to_all(jnp.broadcast_to(own, (NR, 16, OWN)), ROWG, 0, 0)
    cols = lax.all_to_all(jnp.broadcast_to(own, (NC, 16, OWN)), COLG, 0, 0)
    tile = VMEM((NJ, NI), bf16)
    high, low, part = call(
        first_product, [tile, tile, shape(NR, NR * 8, OWN)], "first_product", [rows, cols], vmem=40 << 20
    )
    part = lax.all_to_all(part, ROWG, 0, 0)
    image, message = call(
        first_image, [shape(NR, 8, OWN), shape(NC, 16, OWN)], "first_image", [mine, part, rows]
    )
    image_cols = lax.all_to_all(message, COLG, 0, 0)
    high = pltpu.with_memory_space_constraint(high, VMEM)
    low = pltpu.with_memory_space_constraint(low, VMEM)
    part, scalars = call(
        second_product,
        [shape(NR, NR * 8 + 8, OWN), shape(8, OWN)],
        "second_product",
        [cols, image_cols, high, low],
        vmem=40 << 20,
    )
    part = lax.all_to_all(part, ROWG, 0, 0)
    keep, message = call(
        second_image,
        [shape(4, 8, OWN), shape(NC, 8, OWN)],
        "second_image",
        [mine, part, rows, image, scalars],
        scratch=[pltpu.VMEM((3, NR, 8, OWN), f32)],
    )
    sums = lax.all_to_all(message, COLG, 0, 0)
    residual, direction = call(
        finish, [shape(8, OWN), shape(8, OWN)], "finish", [keep, sums]
    )
    return residual, direction


def solution(mesh):
    fine = Mesh(mesh.devices.reshape(SIZES), AXES)
    placed = (P(None, AXES), P(), P(None, AXES))
    return jax.shard_map(
        per_device,
        mesh=fine,
        in_specs=placed,
        out_specs=(P(None, AXES), P(None, AXES)),
        check_vma=False,
    )
```

time: 1330 us -> 119 us (0.09)
  waiting for transfers between devices: 934 us -> 7.17 us
  blocking collectives: 312 us -> 74.2 us
  matrix products: 60 us -> 0 us
  Pallas kernels: 0 us -> 16.2 us
  local copies, waits for them, and re-layouts: 0.01 us -> 14.8 us
    all_gather x3 -> x0, waiting for transfers between devices: 934 us -> none  [the longest x2 559 us: per_device(): lax.all_gather(local_block, 'blk', axis=1, tiled=True)]
    psum x4 -> x0, blocking collectives: 297 us -> none  [the longest x3 222 us: squares(): return lax.psum(jnp.sum(residual * residual, axis=1), ('blk', 'pair'))]
    all_to_all x0 -> x5, blocking collectives: none -> 74.2 us  [the longest x1 22.7 us: per_device(): cols = lax.all_to_all(jnp.broadcast_to(own, (NC, 16, OWN)), COLG, 0, 0)]
    dot_general x3 -> x0, matrix products: 60 us -> none  [the longest x2 32.7 us: per_device(): jnp.dot(lax.all_gather(local_block, 'blk', axis=1, tiled=True), kernel_ti...]
    pallas_call x0 -> x5, Pallas kernels: none -> 16.2 us  [call(): pl.pallas_call(kernel, in_specs=[pl.BlockSpec(memory_space=pltpu.SMEM if...]
    all_gather x2 -> x0, blocking collectives: 15.2 us -> none  [per_device(): local_block = lax.all_gather(direction, 'pair', axis=1, tiled=True)]
    unnamed x4 -> x14, local copies, waits for them, and re-layouts: 0.01 us -> 14.7 us
  transfers between devices with their start and end apart: 3 -> 1, of which waited for: 3 -> 1; matrix products, arithmetic and copies ran while one was open for 2% -> 0% of each run, Pallas kernels for 0% -> 0%
where the time goes in v1:
time: 119 us; the launch traced here: 118 us
  blocking collectives  74.2 us (62%)
  Pallas kernels  16.2 us (14%)
  local copies, waits for them, and re-layouts  14.8 us (12%)
  waiting for transfers between devices  7.17 us (6%)
  starting transfers between devices  3.41 us (3%)
  other arithmetic  1.45 us (1%)
    all_to_all x1, blocking collectives, per_device(): cols = lax.all_to_all(jnp.broadcast_to(own, (NC, 16, OWN)), COLG, 0, 0)  22.7 us
    all_to_all x1, blocking collectives, per_device(): image_cols = lax.all_to_all(message, COLG, 0, 0)  16.5 us
    pallas_call x5, Pallas kernels, call(): pl.pallas_call(kernel, in_specs=[pl.BlockSpec(memory_space=pltpu.SMEM if...  16.2 us
    unnamed x14, local copies, waits for them, and re-layouts  14.7 us
    all_to_all x1, blocking collectives, per_device(): sums = lax.all_to_all(message, COLG, 0, 0)  14.2 us
    all_to_all x1, blocking collectives, per_device(): part = lax.all_to_all(part, ROWG, 0, 0)  11.2 us
    all_to_all x1, blocking collectives, per_device(): rows = lax.all_to_all(jnp.broadcast_to(own, (NR, 16, OWN)), ROWG, 0, 0)  9.64 us
    all_to_all x1, waiting for transfers between devices, per_device(): part = lax.all_to_all(part, ROWG, 0, 0)  7.17 us
  transfers between devices with their start and end apart: 1, of which 1 were waited for; matrix products, arithmetic and copies ran while one was open for 0% of the time, Pallas kernels for 0%

profile of v1, /device:TPU:8, one launch (start us, length us, event | category | flops | bytes accessed | tf_op | source)
XLA Modules:
  0.0 117.9 jit_solution(17363263577550391955)
XLA Ops:
  0.6 0.8 broadcast_divide_fusion
  1.4 0.7 pad_maximum_fusion
  2.1 9.6 %all_to_all.30.rows_ref = f32[8,16,128]{2,1,0:T(8,128)} all-to-all(f32[8,16,128]{2,1,0:T(8,128)S(1)} %broadcast_in_dim.8), channel_id=1, replica_groups=mesh['z'=8,'xl'=2,'y'=4,'xh'=2,'core'=2] {'xl','xh','core'}, dimensions={0} | all-to-all | bytes 131072 | tf_op jit(solution)/shard_map/all_to_all | solution.py:236
  11.8 22.7 %all_to_all.31.cols_ref = f32[32,16,128]{2,1,0:T(8,128)} all-to-all(f32[32,16,128]{2,1,0:T(8,128)S(1)} %broadcast_in_dim.7), channel_id=1, replica_groups=mesh['z'=8,'xl'=2,'y'=4,'xh'=2,'core'=2] {'z','y'}, dimensions={0} | all-to-all | bytes 524288 | tf_op jit(solution)/shard_map/all_to_all | solution.py:237
  34.5 10.0 %first_product.1 = (bf16[4096,1024]{1,0:T(8,128)(2,1)S(1)}, bf16[4096,1024]{1,0:T(8,128)(2,1)S(1)}, f32[8,64,128]{2,1,0:T(8,128)}) custom-call(f32[8,16,128]{2,1,0:T(8,128)} %all_to_all.30.rows_ref, f32[32,16,128]{2,1,0:T(8,128)} %all_to_all.31.cols_ref), custom_call_target="tpu_custom_call" | custom-call | tf_op jit(solution)/shard_map/first_product/pallas_call | solution.py:216
  44.5 0.0 copy-start
  44.5 3.2 %copy-done = bf16[4096,1024]{1,0:T(8,128)(2,1)} copy-done((bf16[4096,1024]{1,0:T(8,128)(2,1)}, bf16[4096,1024]{1,0:T(8,128)(2,1)S(1)}, u32[]{:S(2)}) %copy-start) | copy-done | bytes 8388632
  47.7 0.0 copy-start.2
  47.7 3.2 %copy-done.2 = bf16[4096,1024]{1,0:T(8,128)(2,1)} copy-done((bf16[4096,1024]{1,0:T(8,128)(2,1)}, bf16[4096,1024]{1,0:T(8,128)(2,1)S(1)}, u32[]{:S(2)}) %copy-start.2) | copy-done | bytes 8388632
  50.9 3.4 %all-to-all-start.2 = ((f32[8,64,128]{2,1,0:T(8,128)}), f32[8,64,128]{2,1,0:T(8,128)S(1)}, u32[]{:S(2)}, u32[]{:S(2)}) async-start(f32[8,64,128]{2,1,0:T(8,128)} %get-tuple-element.11), calls=%async_computation.2 | async-start | bytes 524288 | tf_op jit(solution)/shard_map/all_to_all | solution.py:242
  54.3 7.2 %all-to-all-done.2.part_ref = f32[8,64,128]{2,1,0:T(8,128)S(1)} async-done(((f32[8,64,128]{2,1,0:T(8,128)}), f32[8,64,128]{2,1,0:T(8,128)S(1)}, u32[]{:S(2)}, u32[]{:S(2)}) %all-to-all-start.2) | async-done | bytes 262176 | tf_op jit(solution)/shard_map/all_to_all | solution.py:242
  61.5 0.0 copy-start.4
  61.5 0.8 copy-done.4
  62.3 0.1 first_image.1
  62.4 16.5 %all_to_all.32.image_cols_ref = f32[32,16,128]{2,1,0:T(8,128)} all-to-all(f32[32,16,128]{2,1,0:T(8,128)S(1)} %get-tuple-element.12), channel_id=1, replica_groups=mesh['z'=8,'xl'=2,'y'=4,'xh'=2,'core'=2] {'z','y'}, dimensions={0} | all-to-all | bytes 524288 | tf_op jit(solution)/shard_map/all_to_all | solution.py:246
  78.9 0.0 copy-start.1
  78.9 3.4 %copy-done.1 = bf16[4096,1024]{1,0:T(8,128)(2,1)S(1)} copy-done((bf16[4096,1024]{1,0:T(8,128)(2,1)S(1)}, bf16[4096,1024]{1,0:T(8,128)(2,1)}, u32[]{:S(2)}) %copy-start.1) | copy-done | bytes 8388632
  82.3 0.0 copy-start.3
  82.3 3.4 %copy-done.3 = bf16[4096,1024]{1,0:T(8,128)(2,1)S(1)} copy-done((bf16[4096,1024]{1,0:T(8,128)(2,1)S(1)}, bf16[4096,1024]{1,0:T(8,128)(2,1)}, u32[]{:S(2)}) %copy-start.3) | copy-done | bytes 8388632
  85.7 0.0 copy-start.5
  85.7 5.0 %second_product.1 = (f32[8,72,128]{2,1,0:T(8,128)}, f32[8,128]{1,0:T(8,128)}) custom-call(f32[32,16,128]{2,1,0:T(8,128)} %all_to_all.31.cols_ref, f32[32,16,128]{2,1,0:T(8,128)} %all_to_all.32.image_cols_ref, bf16[4096,1024]{1,0:T(8,128)(2,1)S(1)} %copy-done.1, bf16[4096,1024]{1,0:T(8,128)(2,1)S(1)} %copy-done.3), custom_call_target="tpu_custom_call" | custom-call | tf_op jit(solution)/shard_map/second_product/pallas_call | solution.py:216
  90.7 11.2 %all_to_all.33.part_ref = f32[8,72,128]{2,1,0:T(8,128)S(1)} all-to-all(f32[8,72,128]{2,1,0:T(8,128)} %get-tuple-element.15), channel_id=1, replica_groups=mesh['z'=8,'xl'=2,'y'=4,'xh'=2,'core'=2] {'xl','xh','core'}, dimensions={0} | all-to-all | bytes 589824 | tf_op jit(solution)/shard_map/all_to_all | solution.py:256
  101.8 0.0 copy-done.5
  101.8 0.0 copy-start.6
  101.8 0.7 copy-done.6
  102.5 0.3 second_image.1
  102.8 14.2 %all_to_all.34.sums_ref = f32[32,8,128]{2,1,0:T(8,128)S(1)} all-to-all(f32[32,8,128]{2,1,0:T(8,128)S(1)} %get-tuple-element.19), channel_id=1, replica_groups=mesh['z'=8,'xl'=2,'y'=4,'xh'=2,'core'=2] {'z','y'}, dimensions={0} | all-to-all | bytes 262144 | tf_op jit(solution)/shard_map/all_to_all | solution.py:264
  117.0 0.9 finish.1
  (2 shorter events, 0.0 us)
Async XLA Ops:
  44.5 3.2 %copy-start = (bf16[4096,1024]{1,0:T(8,128)(2,1)}, bf16[4096,1024]{1,0:T(8,128)(2,1)S(1)}, u32[]{:S(2)}) copy-start(bf16[4096,1024]{1,0:T(8,128)(2,1)S(1)} %get-tuple-element.13.high_ref) | copy-start | bytes 25165828
  47.7 3.2 %copy-start.2 = (bf16[4096,1024]{1,0:T(8,128)(2,1)}, bf16[4096,1024]{1,0:T(8,128)(2,1)S(1)}, u32[]{:S(2)}) copy-start(bf16[4096,1024]{1,0:T(8,128)(2,1)S(1)} %get-tuple-element.14.low_ref) | copy-start | bytes 25165828
  50.9 10.6 %all-to-all-start.2 = ((f32[8,64,128]{2,1,0:T(8,128)}), f32[8,64,128]{2,1,0:T(8,128)S(1)}, u32[]{:S(2)}, u32[]{:S(2)}) async-start(f32[8,64,128]{2,1,0:T(8,128)} %get-tuple-element.11), calls=%async_computation.2 | async-start | bytes 524288 | tf_op jit(solution)/shard_map/all_to_all | solution.py:242
  61.5 0.8 copy-start.4
  78.9 3.4 %copy-start.1 = (bf16[4096,1024]{1,0:T(8,128)(2,1)S(1)}, bf16[4096,1024]{1,0:T(8,128)(2,1)}, u32[]{:S(2)}) copy-start(bf16[4096,1024]{1,0:T(8,128)(2,1)} %copy-done) | copy-start | bytes 25165828
  82.3 3.4 %copy-start.3 = (bf16[4096,1024]{1,0:T(8,128)(2,1)S(1)}, bf16[4096,1024]{1,0:T(8,128)(2,1)}, u32[]{:S(2)}) copy-start(bf16[4096,1024]{1,0:T(8,128)(2,1)} %copy-done.2) | copy-start | bytes 25165828
  85.7 16.1 %copy-start.5 = (f32[8,16,128]{2,1,0:T(8,128)S(1)}, f32[8,16,128]{2,1,0:T(8,128)}, u32[]{:S(2)}) copy-start(f32[8,16,128]{2,1,0:T(8,128)} %all_to_all.30.rows_ref) | copy-start | bytes 196612
  101.8 0.7 copy-start.6

commit v2 on v1

--- a/solution.py
+++ b/solution.py
@@ -119,7 +119,7 @@
     return lax.axis_index("xl") * 4 + lax.axis_index("xh") * 2 + lax.axis_index("core")
 
 
-def first_image(mine_ref, part_ref, rows_ref, image_ref, out_ref):
+def first_image(part_ref, rows_ref, image_ref, out_ref):
     parts = block_rows(part_ref)
     bb = jnp.zeros((8, OWN), f32)
     bw = jnp.zeros((8, OWN), f32)
@@ -129,7 +129,7 @@
         image_ref[k] = image
         bb = bb + target * target
         bw = bw + target * image
-    own = image_ref[mine_ref[0]]
+    own = image_ref[my_row_block()]
     scalars = at_lanes([total(bb), total(bw)])
     for copy in range(NC):
         out_ref[copy, 0:8, :] = own
@@ -154,7 +154,7 @@
     scalar_ref[...] = at_lanes([norm, step])
 
 
-def second_image(mine_ref, part_ref, rows_ref, image_ref, scalar_ref, own_ref, out_ref, keep_ref):
+def second_image(part_ref, rows_ref, image_ref, scalar_ref, own_ref, out_ref, keep_ref):
     parts = block_rows(part_ref)
     norm, step = scalar_ref[:, 0:1], scalar_ref[:, 1:2]
     norm_next = part_ref[0, NI // OWN * 8 :, 0:1]
@@ -190,9 +190,10 @@
     scalars = at_lanes([total(di), guess, total(ss), total(si), ii])
     for copy in range(NC):
         out_ref[copy] = scalars
-    own_ref[0] = keep_ref[0, mine_ref[0]]
-    own_ref[1] = keep_ref[1, mine_ref[0]]
-    own_ref[2] = keep_ref[2, mine_ref[0]]
+    mine = my_row_block()
+    own_ref[0] = keep_ref[0, mine]
+    own_ref[1] = keep_ref[1, mine]
+    own_ref[2] = keep_ref[2, mine]
     own_ref[3] = jnp.broadcast_to(norm_next, (8, OWN))
 
 
@@ -212,11 +213,11 @@
     direction_ref[...] = residual + (norm_next / norm) * own_ref[1]
 
 
-def call(kernel, outs, name, args, scratch=(), vmem=48 << 20):
+def call(kernel, outs, name, args, scratch=(), vmem=4 << 20):
     return pl.pallas_call(
         kernel,
         in_specs=[
-            pl.BlockSpec(memory_space=pltpu.SMEM if a.dtype == jnp.int32 else VMEM) for a in args
+            pl.BlockSpec(memory_space=VMEM) for _ in args
         ],
         out_specs=[pl.BlockSpec(memory_space=VMEM)] * len(outs),
         out_shape=outs,
@@ -231,17 +232,16 @@
 
 
 def per_device(points, lengthscale, targets):
-    mine = my_row_block().astype(jnp.int32).reshape(1)
     own = jnp.concatenate([points / lengthscale[:, None], targets], 0)
     rows = lax.all_to_all(jnp.broadcast_to(own, (NR, 16, OWN)), ROWG, 0, 0)
     cols = lax.all_to_all(jnp.broadcast_to(own, (NC, 16, OWN)), COLG, 0, 0)
     tile = VMEM((NJ, NI), bf16)
     high, low, part = call(
-        first_product, [tile, tile, shape(NR, NR * 8, OWN)], "first_product", [rows, cols], vmem=40 << 20
+        first_product, [tile, tile, shape(NR, NR * 8, OWN)], "first_product", [rows, cols], vmem=24 << 20
     )
     part = lax.all_to_all(part, ROWG, 0, 0)
     image, message = call(
-        first_image, [shape(NR, 8, OWN), shape(NC, 16, OWN)], "first_image", [mine, part, rows]
+        first_image, [shape(NR, 8, OWN), shape(NC, 16, OWN)], "first_image", [part, rows]
     )
     image_cols = lax.all_to_all(message, COLG, 0, 0)
     high = pltpu.with_memory_space_constraint(high, VMEM)
@@ -251,14 +251,14 @@
         [shape(NR, NR * 8 + 8, OWN), shape(8, OWN)],
         "second_product",
         [cols, image_cols, high, low],
-        vmem=40 << 20,
+        vmem=8 << 20,
     )
     part = lax.all_to_all(part, ROWG, 0, 0)
     keep, message = call(
         second_image,
         [shape(4, 8, OWN), shape(NC, 8, OWN)],
         "second_image",
-        [mine, part, rows, image, scalars],
+        [part, rows, image, scalars],
         scratch=[pltpu.VMEM((3, NR, 8, OWN), f32)],
     )
     sums = lax.all_to_all(message, COLG, 0, 0)

time: 119 us -> 98.6 us (0.83)
  local copies, waits for them, and re-layouts: 14.8 us -> 0.03 us
  blocking collectives: 74.2 us -> 82.7 us
  waiting for transfers between devices: 7.17 us -> 0 us
  Pallas kernels: 16.2 us -> 12.7 us
  starting transfers between devices: 3.41 us -> 0 us
    unnamed x14 -> x0, local copies, waits for them, and re-layouts: 14.7 us -> none
    all_to_all x1 -> x2, blocking collectives: 11.2 us -> 19.9 us  [per_device(): part = lax.all_to_all(part, ROWG, 0, 0)]
    all_to_all x1 -> x0, waiting for transfers between devices: 7.17 us -> none  [per_device(): part = lax.all_to_all(part, ROWG, 0, 0)]
    pallas_call x5, Pallas kernels: 16.2 us -> 12.7 us  [call(): pl.pallas_call(kernel, in_specs=[pl.BlockSpec(memory_space=VMEM) for _ in...]
    all_to_all x1 -> x0, starting transfers between devices: 3.41 us -> none  [per_device(): part = lax.all_to_all(part, ROWG, 0, 0)]
  transfers between devices with their start and end apart: 1 -> 0, of which waited for: 1 -> 0; matrix products, arithmetic and copies ran while one was open for 0% -> 0% of each run, Pallas kernels for 0% -> 0%
where the time goes in v2:
time: 98.6 us; the launch traced here: 97.5 us
  blocking collectives  82.7 us (84%)
  Pallas kernels  12.7 us (13%)
  other arithmetic  1.45 us (1%)
    all_to_all x1, blocking collectives, per_device(): cols = lax.all_to_all(jnp.broadcast_to(own, (NC, 16, OWN)), COLG, 0, 0)  22.6 us
    all_to_all x2, blocking collectives, per_device(): part = lax.all_to_all(part, ROWG, 0, 0)  19.9 us
    all_to_all x1, blocking collectives, per_device(): image_cols = lax.all_to_all(message, COLG, 0, 0)  16.4 us
    all_to_all x1, blocking collectives, per_device(): sums = lax.all_to_all(message, COLG, 0, 0)  14.2 us
    pallas_call x5, Pallas kernels, call(): pl.pallas_call(kernel, in_specs=[pl.BlockSpec(memory_space=VMEM) for _ in...  12.7 us
    all_to_all x1, blocking collectives, per_device(): rows = lax.all_to_all(jnp.broadcast_to(own, (NR, 16, OWN)), ROWG, 0, 0)  9.53 us

profile of v2, /device:TPU:8, one launch (start us, length us, event | category | flops | bytes accessed | tf_op | source)
XLA Modules:
  0.0 97.5 jit_solution(15352415218090407638)
XLA Ops:
  0.6 0.8 broadcast_divide_fusion
  1.4 0.7 pad_maximum_fusion
  2.1 9.5 %all_to_all.30.rows_ref = f32[8,16,128]{2,1,0:T(8,128)S(1)} all-to-all(f32[8,16,128]{2,1,0:T(8,128)S(1)} %broadcast_in_dim.8), channel_id=1, replica_groups=mesh['z'=8,'xl'=2,'y'=4,'xh'=2,'core'=2] {'xl','xh','core'}, dimensions={0} | all-to-all | bytes 131072 | tf_op jit(solution)/shard_map/all_to_all | solution.py:236
  11.6 22.6 %all_to_all.31.cols_ref = f32[32,16,128]{2,1,0:T(8,128)S(1)} all-to-all(f32[32,16,128]{2,1,0:T(8,128)S(1)} %broadcast_in_dim.7), channel_id=1, replica_groups=mesh['z'=8,'xl'=2,'y'=4,'xh'=2,'core'=2] {'z','y'}, dimensions={0} | all-to-all | bytes 524288 | tf_op jit(solution)/shard_map/all_to_all | solution.py:237
  34.3 8.2 %first_product.1 = (bf16[4096,1024]{1,0:T(8,128)(2,1)S(1)}, bf16[4096,1024]{1,0:T(8,128)(2,1)S(1)}, f32[8,64,128]{2,1,0:T(8,128)S(1)}) custom-call(f32[8,16,128]{2,1,0:T(8,128)S(1)} %all_to_all.30.rows_ref, f32[32,16,128]{2,1,0:T(8,128)S(1)} %all_to_all.31.cols_ref), custom_call_target="tpu_custom_call" | custom-call | tf_op jit(solution)/shard_map/first_product/pallas_call | solution.py:217
  42.5 9.7 %all_to_all.32.part_ref = f32[8,64,128]{2,1,0:T(8,128)S(1)} all-to-all(f32[8,64,128]{2,1,0:T(8,128)S(1)} %get-tuple-element.11), channel_id=1, replica_groups=mesh['z'=8,'xl'=2,'y'=4,'xh'=2,'core'=2] {'xl','xh','core'}, dimensions={0} | all-to-all | bytes 524288 | tf_op jit(solution)/shard_map/all_to_all | solution.py:242
  52.2 0.1 first_image.1
  52.3 16.4 %all_to_all.33.image_cols_ref = f32[32,16,128]{2,1,0:T(8,128)S(1)} all-to-all(f32[32,16,128]{2,1,0:T(8,128)S(1)} %get-tuple-element.12), channel_id=1, replica_groups=mesh['z'=8,'xl'=2,'y'=4,'xh'=2,'core'=2] {'z','y'}, dimensions={0} | all-to-all | bytes 524288 | tf_op jit(solution)/shard_map/all_to_all | solution.py:246
  68.7 3.2 %second_product.1 = (f32[8,72,128]{2,1,0:T(8,128)S(1)}, f32[8,128]{1,0:T(8,128)S(1)}) custom-call(f32[32,16,128]{2,1,0:T(8,128)S(1)} %all_to_all.31.cols_ref, f32[32,16,128]{2,1,0:T(8,128)S(1)} %all_to_all.33.image_cols_ref, bf16[4096,1024]{1,0:T(8,128)(2,1)S(1)} %get-tuple-element.13.high_ref, bf16[4096,1024]{1,0:T(8,128)(2,1)S(1)} %get-tuple-element.14.low_ref), custom_call_target="tpu_custom_call" | custom-call | tf_op jit(solution)/shard_map/second_product/pallas_call | solution.py:217
  71.9 10.3 %all_to_all.34.part_ref = f32[8,72,128]{2,1,0:T(8,128)S(1)} all-to-all(f32[8,72,128]{2,1,0:T(8,128)S(1)} %get-tuple-element.15), channel_id=1, replica_groups=mesh['z'=8,'xl'=2,'y'=4,'xh'=2,'core'=2] {'xl','xh','core'}, dimensions={0} | all-to-all | bytes 589824 | tf_op jit(solution)/shard_map/all_to_all | solution.py:256
  82.1 0.3 second_image.1
  82.4 14.2 %all_to_all.35.sums_ref = f32[32,8,128]{2,1,0:T(8,128)S(1)} all-to-all(f32[32,8,128]{2,1,0:T(8,128)S(1)} %get-tuple-element.19), channel_id=1, replica_groups=mesh['z'=8,'xl'=2,'y'=4,'xh'=2,'core'=2] {'z','y'}, dimensions={0} | all-to-all | bytes 262144 | tf_op jit(solution)/shard_map/all_to_all | solution.py:264
  96.6 0.9 finish.1
  (2 shorter events, 0.0 us)

commit v3 on v2

v3 whole, which is shorter than its diff:
```python
import math

import jax
import jax.numpy as jnp
from jax import lax
from jax.experimental import pallas as pl
from jax.experimental.pallas import tpu as pltpu
from jax.sharding import Mesh
from jax.sharding import PartitionSpec as P

f32 = jnp.float32
bf16 = jnp.bfloat16
VMEM = pltpu.VMEM

AXES = ("z", "xl", "y", "xh", "core")
SIZES = (8, 2, 4, 2, 2)
ROWG = ("xl", "xh", "core")
COLG = ("z", "y")
NR, NC = 8, 32
OWN = 128
NI, NJ = NR * OWN, NC * OWN
noise_level = 0.5

POINT_SCALE = math.sqrt(5.0 / 3.0)
ROOT3 = math.sqrt(3.0)
EXP_SCALE = -math.sqrt(3.0) * math.log2(math.e)

TI, TJ = 256, 256


def pieces(x):
    first = x.astype(bf16).astype(f32)
    rest = x - first
    second = rest.astype(bf16).astype(f32)
    return first, second, rest - second


def features(x, left):
    x = x * POINT_SCALE
    square = jnp.sum(x * x, axis=0, keepdims=True)
    a, b, c = pieces(x)
    s1, s2, s3 = pieces(square)
    one, zero = jnp.ones_like(square), jnp.zeros_like(square)
    if left:
        tail = [s1, s2, s3, one, one, one, zero, zero]
        parts = [a, a, b, b, a, c]
    else:
        tail = [one, one, one, s1, s2, s3, zero, zero]
        parts = [-2.0 * a, -2.0 * b, -2.0 * a, -2.0 * b, -2.0 * c, -2.0 * a]
    return jnp.concatenate(parts + [jnp.concatenate(tail, 0), jnp.zeros_like(a)], 0)


def matern(tau):
    tau = jnp.maximum(tau, 1e-30)
    s = tau * lax.rsqrt(tau)
    return ((1.0 + tau) + ROOT3 * s) * jnp.exp2(EXP_SCALE * s)


def stacked(values):
    return jnp.concatenate(pieces(values), 0).astype(bf16)


def lanes(ref, first_row, count, start=0):
    return jnp.concatenate(
        [ref[start + k, first_row : first_row + 8, :] for k in range(count)], 1
    )


def total(x):
    return jnp.sum(x, axis=1, keepdims=True)


def pack(points_hbm, lengthscale_hbm, targets_hbm, own_ref, copies_ref, points_ref, lengthscale_ref, targets_ref, sems):
    arriving = [
        pltpu.make_async_copy(points_hbm, points_ref, sems.at[0]),
        pltpu.make_async_copy(lengthscale_hbm, lengthscale_ref, sems.at[1]),
        pltpu.make_async_copy(targets_hbm, targets_ref, sems.at[2]),
    ]
    for copy in arriving:
        copy.start()
    for copy in arriving:
        copy.wait()
    row = lax.broadcasted_iota(jnp.int32, (8, OWN), 0)
    scale = jnp.zeros((8, OWN), f32)
    for k in range(8):
        scale = jnp.where(row == k, lengthscale_ref[k], scale)
    scaled = points_ref[...] / scale
    targets = targets_ref[...]
    own_ref[0, 0:8, :] = scaled
    own_ref[0, 8:16, :] = targets
    for copy in range(NC):
        copies_ref[copy, 0:8, :] = scaled
        copies_ref[copy, 8:16, :] = targets


def my_row_block():
    return lax.axis_index("xl") * 4 + lax.axis_index("xh") * 2 + lax.axis_index("core")


def first_product(rows_ref, cols_ref, high_ref, low_ref, out_ref):
    left = features(lanes(rows_ref, 0, NR), True).astype(bf16)
    right = features(lanes(cols_ref, 0, NC), False).T.astype(bf16)
    values = stacked(lanes(cols_ref, 8, NC))
    form = jnp.zeros((8, OWN), f32)
    for i in range(0, NI, TI):
        acc = jnp.zeros((24, TI), f32)
        for j in range(0, NJ, TJ):
            tau = jnp.dot(right[j : j + TJ], left[:, i : i + TI], preferred_element_type=f32)
            tile = matern(tau)
            high = tile.astype(bf16)
            low = (tile - high.astype(f32)).astype(bf16)
            high_ref[j : j + TJ, i : i + TI] = high
            low_ref[j : j + TJ, i : i + TI] = low
            part = values[:, j : j + TJ]
            acc = acc + jnp.dot(part, high, preferred_element_type=f32)
            acc = acc + jnp.dot(part, low, preferred_element_type=f32)
        acc = acc[0:8] + acc[8:16] + acc[16:24]
        for k in range(TI // OWN):
            block = i // OWN + k
            part = acc[:, k * OWN : (k + 1) * OWN]
            out_ref[block % 2, block // 2, 0:8, :] = part
            form = form + part * rows_ref[block, 8:16, :]
    form = jnp.broadcast_to(total(form), (8, OWN))
    for block in range(NR):
        out_ref[block % 2, block // 2, 8:16, :] = form


def at_lanes(columns):
    lane = lax.broadcasted_iota(jnp.int32, (8, OWN), 1)
    out = jnp.zeros((8, OWN), f32)
    for k, column in enumerate(columns):
        out = jnp.where(lane == k, column, out)
    return out


def first_image(own_ref, xh_ref, xl_ref, both_ref, rows_ref, out_ref):
    sums = (own_ref[0] + xh_ref[0]) + (xl_ref[0] + both_ref[0])
    targets = rows_ref[0, 8:16, :]
    bb = jnp.zeros((8, OWN), f32)
    for k in range(NR):
        bb = bb + rows_ref[k, 8:16, :] * rows_ref[k, 8:16, :]
    bb = total(bb)
    image = sums[0:8] + noise_level * targets
    scalars = at_lanes([bb, sums[8:16, 0:1] + noise_level * bb])
    for copy in range(NC):
        out_ref[copy, 0:8, :] = image
        out_ref[copy, 8:16, :] = scalars


def second_product(cols_ref, image_cols_ref, high_ref, low_ref, out_ref, image_ref, scalar_ref):
    sums = image_cols_ref[0, 8:16, :]
    for k in range(1, NC):
        sums = sums + image_cols_ref[k, 8:16, :]
    norm = sums[:, 0:1]
    step = norm / sums[:, 1:2]
    residual = lanes(cols_ref, 8, NC) - step * lanes(image_cols_ref, 0, NC)
    norm_part = jnp.broadcast_to(total(residual * residual), (8, OWN))
    values = stacked(residual)
    mine = my_row_block()
    image = image_cols_ref[my_col_block(), 0:8, :]
    for i in range(0, NI, TI):
        acc = jnp.dot(values, high_ref[:, i : i + TI], preferred_element_type=f32)
        acc = acc + jnp.dot(values, low_ref[:, i : i + TI], preferred_element_type=f32)
        acc = acc[0:8] + acc[8:16] + acc[16:24]
        for k in range(TI // OWN):
            row = pl.multiple_of((mine ^ (i // OWN + k)) * 8, 8)
            out_ref[pl.ds(row, 8), :] = acc[:, k * OWN : (k + 1) * OWN]
    out_ref[NR * 8 : NR * 8 + 8, :] = norm_part
    image_ref[...] = image
    scalar_ref[...] = at_lanes([norm, step])


def core_sum(ours_ref, theirs_ref, ours_image_ref, theirs_image_ref, out_ref):
    core = lax.axis_index("core")
    out_ref[0 : NR * 8 + 8, :] = ours_ref[...] + theirs_ref[...]
    first = pl.multiple_of(NR * 8 + 8 + core * 8, 8)
    out_ref[pl.ds(first, 8), :] = ours_image_ref[...]
    second = pl.multiple_of(NR * 8 + 16 - core * 8, 8)
    out_ref[pl.ds(second, 8), :] = theirs_image_ref[...]


def second_image(own_part, xh_part, xl_part, both_part, rows_ref, scalar_ref, own_ref, out_ref, keep_ref, part_ref):
    mine = my_row_block()
    chip = mine // 2
    for k, ref in enumerate((own_part, xh_part, xl_part, both_part)):
        part_ref[chip ^ k] = ref[...]
    norm, step = scalar_ref[:, 0:1], scalar_ref[:, 1:2]

    def summed(row):
        out = part_ref[0, row : row + 8, :]
        for k in range(1, 4):
            out = out + part_ref[k, row : row + 8, :]
        return out

    norm_next = summed(NR * 8)
    ratio = norm_next / norm
    residuals, images = [], []
    di = jnp.zeros((8, OWN), f32)
    ri = jnp.zeros((8, OWN), f32)
    ii = jnp.zeros((8, OWN), f32)
    for k in range(NR):
        target = rows_ref[mine ^ k, 8:16, :]
        first = NR * 8 + 8 + (k % 2) * 8
        image0 = part_ref[k // 2, first : first + 8, :]
        residual = target - step * image0
        direction = residual + ratio * target
        image = (summed(8 * k) + noise_level * residual) + ratio * image0
        keep_ref[0, k] = residual
        keep_ref[1, k] = direction
        keep_ref[2, k] = image
        residuals.append(residual)
        images.append(image)
        di = di + direction * image
        ri = ri + residual * image
        ii = ii + image * image
    ii = total(ii)
    guess = total(ri) / jnp.where(ii > 0.0, ii, 1.0)
    ss = jnp.zeros((8, OWN), f32)
    si = jnp.zeros((8, OWN), f32)
    for k in range(NR):
        left = residuals[k] - guess * images[k]
        ss = ss + left * left
        si = si + left * images[k]
    scalars = in_one_row([total(di), guess, total(ss), total(si), ii])
    for copy in range(NC):
        out_ref[copy] = scalars
    own_ref[0] = keep_ref[0, mine]
    own_ref[1] = keep_ref[1, mine]
    own_ref[2] = keep_ref[2, mine]
    own_ref[3] = norm_next


def in_one_row(columns):
    lane = lax.broadcasted_iota(jnp.int32, (8, OWN), 1)
    row = lax.broadcasted_iota(jnp.int32, (8, OWN), 0)
    out = jnp.zeros((8, OWN), f32)
    for k, column in enumerate(columns):
        out = jnp.where(lane == 8 * k + row, column, out)
    return jnp.sum(out, axis=0, keepdims=True)


def column_of(row_vector, k):
    lane = lax.broadcasted_iota(jnp.int32, (8, OWN), 1)
    row = lax.broadcasted_iota(jnp.int32, (8, OWN), 0)
    return total(jnp.where(lane == 8 * k + row, row_vector, 0.0))


def finish(own_ref, sums_ref, residual_ref, direction_ref):
    norm = own_ref[3][:, 0:1]
    rows = [sums_ref[k] for k in range(NC)]
    step = norm / column_of(sum(rows[1:], rows[0]), 0)
    norm_next = jnp.zeros((8, 1), f32)
    for k in range(NC):
        guess, ss, si, ii = [column_of(rows[k], q) for q in range(1, 5)]
        off = step - guess
        norm_next = norm_next + (ss + off * (off * ii - 2.0 * si))
    residual = own_ref[0] - step * own_ref[2]
    residual_ref[...] = residual
    direction_ref[...] = residual + (norm_next / norm) * own_ref[1]


def my_col_block():
    return lax.axis_index("z") * 4 + lax.axis_index("y")


def call(kernel, outs, name, args, scratch=(), vmem=4 << 20):
    return pl.pallas_call(
        kernel,
        in_specs=[
            pl.BlockSpec(memory_space=VMEM) for _ in args
        ],
        out_specs=[pl.BlockSpec(memory_space=VMEM)] * len(outs),
        out_shape=outs,
        scratch_shapes=scratch,
        compiler_params=pltpu.CompilerParams(vmem_limit_bytes=vmem),
        name=name,
    )(*args)


def shape(*dims):
    return jax.ShapeDtypeStruct(dims, f32)


def swap(x, axes):
    size = 2 ** len(axes)
    return lax.ppermute(x, axes, [(i, size - 1 - i) for i in range(size)])


CHIPS = (("xh",), ("xl",), ("xl", "xh"))


def per_device(points, lengthscale, targets):
    own, copies = pl.pallas_call(
        pack,
        in_specs=[pl.BlockSpec(memory_space=pltpu.HBM)] * 3,
        out_specs=[pl.BlockSpec(memory_space=VMEM)] * 2,
        out_shape=[shape(1, 16, OWN), shape(NC, 16, OWN)],
        scratch_shapes=[
            pltpu.VMEM((8, OWN), f32),
            pltpu.SMEM((8,), f32),
            pltpu.VMEM((8, OWN), f32),
            pltpu.SemaphoreType.DMA((3,)),
        ],
        compiler_params=pltpu.CompilerParams(vmem_limit_bytes=4 << 20),
        name="pack",
    )(*[pltpu.with_memory_space_constraint(a, pltpu.HBM) for a in (points, lengthscale, targets)])
    cols = lax.all_to_all(copies, COLG, 0, 0)
    rows = jnp.concatenate([own, swap(own, ("core",))], 0)
    rows = jnp.concatenate([rows] + [swap(rows, axes) for axes in CHIPS], 0)
    tile = VMEM((NJ, NI), bf16)
    high, low, part = call(
        first_product, [tile, tile, shape(2, 4, 16, OWN)], "first_product", [rows, cols], vmem=24 << 20
    )
    part = part[0] + swap(part[1], ("core",))
    parts = [part[0:1]] + [swap(part[k : k + 1], axes) for k, axes in enumerate(CHIPS, 1)]
    message = call(first_image, [shape(NC, 16, OWN)], "first_image", parts + [rows])[0]
    image_cols = lax.all_to_all(message, COLG, 0, 0)
    high = pltpu.with_memory_space_constraint(high, VMEM)
    low = pltpu.with_memory_space_constraint(low, VMEM)
    part, image, scalars = call(
        second_product,
        [shape(NR * 8 + 8, OWN), shape(8, OWN), shape(8, OWN)],
        "second_product",
        [cols, image_cols, high, low],
        vmem=8 << 20,
    )
    part = call(
        core_sum,
        [shape(NR * 8 + 24, OWN)],
        "core_sum",
        [part, swap(part, ("core",)), image, swap(image, ("core",))],
    )[0]
    parts = [part] + [swap(part, axes) for axes in CHIPS]
    keep, message = call(
        second_image,
        [shape(4, 8, OWN), shape(NC, 1, OWN)],
        "second_image",
        parts + [rows, scalars],
        scratch=[pltpu.VMEM((3, NR, 8, OWN), f32), pltpu.VMEM((4, NR * 8 + 24, OWN), f32)],
    )
    sums = lax.all_to_all(message, COLG, 0, 0)
    residual, direction = call(
        finish, [shape(8, OWN), shape(8, OWN)], "finish", [keep, sums]
    )
    return residual, direction


def solution(mesh):
    fine = Mesh(mesh.devices.reshape(SIZES), AXES)
    placed = (P(None, AXES), P(), P(None, AXES))
    return jax.shard_map(
        per_device,
        mesh=fine,
        in_specs=placed,
        out_specs=(P(None, AXES), P(None, AXES)),
        check_vma=False,
    )
```

time: 98.6 us -> 88.5 us (0.90)
  blocking collectives: 82.7 us -> 30.7 us
  starting transfers between devices: 0 us -> 26.3 us
  waiting for transfers between devices: 0 us -> 15.6 us
  Pallas kernels: 12.7 us -> 14.4 us
  other arithmetic: 1.45 us -> 0.01 us
    all_to_all x4 -> x0, blocking collectives: 52.1 us -> none  [the longest x1 22.6 us: per_device(): cols = lax.all_to_all(jnp.broadcast_to(own, (NC, 16, OWN)), COLG, 0, 0)]
    ppermute x0 -> x13, starting transfers between devices: none -> 14.6 us  [swap(): return lax.ppermute(x, axes, [(i, size - 1 - i) for i in range(size)])]
    ppermute x0 -> x13, waiting for transfers between devices: none -> 13.6 us  [swap(): return lax.ppermute(x, axes, [(i, size - 1 - i) for i in range(size)])]
    all_to_all x0 -> x1, starting transfers between devices: none -> 11.7 us  [per_device(): cols = lax.all_to_all(copies, COLG, 0, 0)]
    all_to_all x0 -> x1, waiting for transfers between devices: none -> 1.97 us  [per_device(): cols = lax.all_to_all(copies, COLG, 0, 0)]
    pallas_call x0 -> x1, Pallas kernels: none -> 1.54 us  [per_device(): pl.pallas_call(pack, in_specs=[pl.BlockSpec(memory_space=pltpu.HBM)] * 3,...]
    pallas_call x5 -> x6, Pallas kernels: 12.7 us -> 12.8 us  [call(): pl.pallas_call(kernel, in_specs=[pl.BlockSpec(memory_space=VMEM) for _ in...]
  transfers between devices with their start and end apart: 0 -> 14, of which waited for: 0 -> 12; matrix products, arithmetic and copies ran while one was open for 0% -> 0% of each run, Pallas kernels for 0% -> 0%
where the time goes in v3:
time: 88.5 us; the launch traced here: 87.7 us
  blocking collectives  30.7 us (35%)
  starting transfers between devices  26.3 us (30%)
  waiting for transfers between devices  15.6 us (18%)
  Pallas kernels  14.4 us (16%)
    all_to_all x1, blocking collectives, per_device(): image_cols = lax.all_to_all(message, COLG, 0, 0)  16.8 us
    ppermute x13, starting transfers between devices, swap(): return lax.ppermute(x, axes, [(i, size - 1 - i) for i in range(size)])  14.6 us
    all_to_all x1, blocking collectives, per_device(): sums = lax.all_to_all(message, COLG, 0, 0)  13.9 us
    ppermute x13, waiting for transfers between devices, swap(): return lax.ppermute(x, axes, [(i, size - 1 - i) for i in range(size)])  13.6 us
    pallas_call x6, Pallas kernels, call(): pl.pallas_call(kernel, in_specs=[pl.BlockSpec(memory_space=VMEM) for _ in...  12.8 us
    all_to_all x1, starting transfers between devices, per_device(): cols = lax.all_to_all(copies, COLG, 0, 0)  11.7 us
    all_to_all x1, waiting for transfers between devices, per_device(): cols = lax.all_to_all(copies, COLG, 0, 0)  1.97 us
  transfers between devices with their start and end apart: 14, of which 12 were waited for; matrix products, arithmetic and copies ran while one was open for 0% of the time, Pallas kernels for 0%

profile of v3, /device:TPU:8, one launch (start us, length us, event | category | flops | bytes accessed | tf_op | source)
XLA Modules:
  0.0 87.7 jit_solution(5667967012788077379)
XLA Ops:
  0.6 1.5 %pack.1 = (f32[1,16,128]{2,1,0:T(8,128)S(1)}, f32[32,16,128]{2,1,0:T(8,128)}) custom-call(f32[8,128]{1,0:T(8,128)} %points_hbm.1, f32[8]{0:T(128)} %lengthscale_hbm.1, f32[8,128]{1,0:T(8,128)} %targets_hbm.1), custom_call_target="tpu_custom_call" | custom-call | tf_op jit(solution)/shard_map/pack/pallas_call | solution.py:293
  2.2 11.7 %all-to-all-start = ((f32[32,16,128]{2,1,0:T(8,128)}), f32[32,16,128]{2,1,0:T(8,128)S(1)}, u32[]{:S(2)}, u32[]{:S(2)}) async-start(f32[32,16,128]{2,1,0:T(8,128)} %get-tuple-element.12), calls=%async_computation | async-start | bytes 524288 | tf_op jit(solution)/shard_map/all_to_all | solution.py:307
  13.9 0.1 collective-permute-start
  14.0 1.1 %collective-permute-done = f32[1,16,128]{2,1,0:T(8,128)S(1)} collective-permute-done((f32[1,16,128]{2,1,0:T(8,128)S(1)}, f32[1,16,128]{2,1,0:T(8,128)S(1)}, u32[]{:S(2)}, u32[]{:S(2)}) %collective-permute-start) | collective-permute-done | bytes 8224 | tf_op jit(solution)/shard_map/ppermute | solution.py:286
  15.2 3.0 %collective-permute-start.1 = (f32[2,16,128]{2,1,0:T(8,128)S(1)}, f32[2,16,128]{2,1,0:T(8,128)S(1)}, u32[]{:S(2)}, u32[]{:S(2)}) collective-permute-start(f32[2,16,128]{2,1,0:T(8,128)S(1)} %get-tuple-element.26), channel_id=1, source_target_pairs={{0,2},{2,0},{1,3},{3,1},{4,6},{6,4},{5,7},{7,5},{8,10},{10,8},{9,1... | collective-permute-start | bytes 49160 | tf_op jit(solution)/shard_map/ppermute | solution.py:286
  18.2 1.1 %collective-permute-start.3 = (f32[2,16,128]{2,1,0:T(8,128)S(1)}, f32[2,16,128]{2,1,0:T(8,128)S(1)}, u32[]{:S(2)}, u32[]{:S(2)}) collective-permute-start(f32[2,16,128]{2,1,0:T(8,128)S(1)} %get-tuple-element.26), channel_id=1, source_target_pairs={{0,18},{2,16},{16,2},{18,0},{1,19},{3,17},{17,3},{19,1},{4,22},{6,... | collective-permute-start | bytes 49160 | tf_op jit(solution)/shard_map/ppermute | solution.py:286
  19.3 0.0 collective-permute-start.2
  19.3 1.1 %collective-permute-done.1 = f32[2,16,128]{2,1,0:T(8,128)S(1)} collective-permute-done((f32[2,16,128]{2,1,0:T(8,128)S(1)}, f32[2,16,128]{2,1,0:T(8,128)S(1)}, u32[]{:S(2)}, u32[]{:S(2)}) %collective-permute-start.1) | collective-permute-done | bytes 16416 | tf_op jit(solution)/shard_map/ppermute | solution.py:286
  20.4 2.7 %collective-permute-done.2 = f32[2,16,128]{2,1,0:T(8,128)S(1)} collective-permute-done((f32[2,16,128]{2,1,0:T(8,128)S(1)}, f32[2,16,128]{2,1,0:T(8,128)S(1)}, u32[]{:S(2)}, u32[]{:S(2)}) %collective-permute-start.2) | collective-permute-done | bytes 16416 | tf_op jit(solution)/shard_map/ppermute | solution.py:286
  23.1 0.1 collective-permute-done.3
  23.1 2.0 %all-to-all-done.cols_ref = f32[32,16,128]{2,1,0:T(8,128)S(1)} async-done(((f32[32,16,128]{2,1,0:T(8,128)}), f32[32,16,128]{2,1,0:T(8,128)S(1)}, u32[]{:S(2)}, u32[]{:S(2)}) %all-to-all-start) | async-done | bytes 262176 | tf_op jit(solution)/shard_map/all_to_all | solution.py:307
  25.1 8.3 %first_product.1 = (bf16[4096,1024]{1,0:T(8,128)(2,1)S(1)}, bf16[4096,1024]{1,0:T(8,128)(2,1)S(1)}, f32[2,4,16,128]{3,2,1,0:T(8,128)S(1)}) custom-call(f32[8,16,128]{2,1,0:T(8,128)S(1)} %constant_dynamic-update-slice_fusion.2.rows_ref, f32[32,16,128]{2,1,0:T(8,128)S(1)} %all-to-all-done.cols_ref), custom_call_target="tpu_custom_call" | custom-call | tf_op jit(solution)/shard_map/first_product/pallas_call | solution.py:267
  33.4 0.0 collective-permute-start.4
  33.5 1.2 %collective-permute-done.4 = f32[4,16,128]{2,1,0:T(8,128)S(1)} collective-permute-done((f32[4,16,128]{2,1,0:T(8,128)S(1)}, f32[4,16,128]{2,1,0:T(8,128)S(1)}, u32[]{:S(2)}, u32[]{:S(2)}) %collective-permute-start.4) | collective-permute-done | bytes 32800 | tf_op jit(solution)/shard_map/ppermute | solution.py:286
  34.7 3.0 %collective-permute-start.7 = (f32[1,16,128]{2,1,0:T(8,128)S(1)}, f32[1,16,128]{2,1,0:T(8,128)S(1)}, u32[]{:S(2)}, u32[]{:S(2)}) collective-permute-start(f32[1,16,128]{2,1,0:T(8,128)S(1)} %get-tuple-element.22), channel_id=1, source_target_pairs={{0,18},{2,16},{16,2},{18,0},{1,19},{3,17},{17,3},{19,1},{4,22},{6,... | collective-permute-start | bytes 24584 | tf_op jit(solution)/shard_map/ppermute | solution.py:286
  37.7 0.2 collective-permute-start.6
  37.9 1.7 %collective-permute-start.5 = (f32[1,16,128]{2,1,0:T(8,128)S(1)}, f32[1,16,128]{2,1,0:T(8,128)S(1)}, u32[]{:S(2)}, u32[]{:S(2)}) collective-permute-start(f32[1,16,128]{2,1,0:T(8,128)S(1)} %get-tuple-element.24), channel_id=1, source_target_pairs={{0,2},{2,0},{1,3},{3,1},{4,6},{6,4},{5,7},{7,5},{8,10},{10,8},{9,1... | collective-permute-start | bytes 24584 | tf_op jit(solution)/shard_map/ppermute | solution.py:286
  39.7 0.2 collective-permute-done.7.both_ref
  39.8 1.5 %collective-permute-done.6.xl_ref = f32[1,16,128]{2,1,0:T(8,128)S(1)} collective-permute-done((f32[1,16,128]{2,1,0:T(8,128)S(1)}, f32[1,16,128]{2,1,0:T(8,128)S(1)}, u32[]{:S(2)}, u32[]{:S(2)}) %collective-permute-start.6) | collective-permute-done | bytes 8224 | tf_op jit(solution)/shard_map/ppermute | solution.py:286
  41.4 1.7 %collective-permute-done.5.xh_ref = f32[1,16,128]{2,1,0:T(8,128)S(1)} collective-permute-done((f32[1,16,128]{2,1,0:T(8,128)S(1)}, f32[1,16,128]{2,1,0:T(8,128)S(1)}, u32[]{:S(2)}, u32[]{:S(2)}) %collective-permute-start.5) | collective-permute-done | bytes 8224 | tf_op jit(solution)/shard_map/ppermute | solution.py:286
  43.1 0.2 first_image.1
  43.3 16.8 %all_to_all.15.image_cols_ref = f32[32,16,128]{2,1,0:T(8,128)S(1)} all-to-all(f32[32,16,128]{2,1,0:T(8,128)S(1)} %first_image.1), channel_id=1, replica_groups=mesh['z'=8,'xl'=2,'y'=4,'xh'=2,'core'=2] {'z','y'}, dimensions={0} | all-to-all | bytes 524288 | tf_op jit(solution)/shard_map/all_to_all | solution.py:317
  60.0 3.2 %second_product.1 = (f32[72,128]{1,0:T(8,128)S(1)}, f32[8,128]{1,0:T(8,128)S(1)}, f32[8,128]{1,0:T(8,128)S(1)}) custom-call(f32[32,16,128]{2,1,0:T(8,128)S(1)} %all-to-all-done.cols_ref, f32[32,16,128]{2,1,0:T(8,128)S(1)} %all_to_all.15.image_cols_ref, bf16[4096,1024]{1,0:T(8,128)(2,1)S(1)} %get-tuple-element.15.high_ref, ...), custom_call_target="tpu_custom_call" | custom-call | tf_op jit(solution)/shard_map/second_product/pallas_call | solution.py:267
  63.2 0.1 collective-permute-start.8
  63.3 0.5 collective-permute-start.9
  63.8 0.8 collective-permute-done.9.theirs_image_ref
  64.6 0.0 collective-permute-done.8.theirs_ref
  64.6 1.3 %collective-permute-start.12 = (f32[88,128]{1,0:T(8,128)S(1)}, f32[88,128]{1,0:T(8,128)S(1)}, u32[]{:S(2)}, u32[]{:S(2)}) collective-permute-start(f32[88,128]{1,0:T(8,128)S(1)} %core_sum.1.own_part), channel_id=1, source_target_pairs={{0,18},{2,16},{16,2},{18,0},{1,19},{3,17},{17,3},{19,1},{4,22},{6,... | collective-permute-start | bytes 135176 | tf_op jit(solution)/shard_map/ppermute | solution.py:286
  66.0 1.1 %collective-permute-start.11 = (f32[88,128]{1,0:T(8,128)S(1)}, f32[88,128]{1,0:T(8,128)S(1)}, u32[]{:S(2)}, u32[]{:S(2)}) collective-permute-start(f32[88,128]{1,0:T(8,128)S(1)} %core_sum.1.own_part), channel_id=1, source_target_pairs={{0,16},{16,0},{1,17},{17,1},{2,18},{18,2},{3,19},{19,3},{4,20},{20... | collective-permute-start | bytes 135176 | tf_op jit(solution)/shard_map/ppermute | solution.py:286
  67.1 2.4 %collective-permute-start.10 = (f32[88,128]{1,0:T(8,128)S(1)}, f32[88,128]{1,0:T(8,128)S(1)}, u32[]{:S(2)}, u32[]{:S(2)}) collective-permute-start(f32[88,128]{1,0:T(8,128)S(1)} %core_sum.1.own_part), channel_id=1, source_target_pairs={{0,2},{2,0},{1,3},{3,1},{4,6},{6,4},{5,7},{7,5},{8,10},{10,8},{9,1... | collective-permute-start | bytes 135176 | tf_op jit(solution)/shard_map/ppermute | solution.py:286
  69.4 0.6 collective-permute-done.12.both_part
  70.0 0.0 collective-permute-done.11.xl_part
  70.0 2.6 %collective-permute-done.10.xh_part = f32[88,128]{1,0:T(8,128)S(1)} collective-permute-done((f32[88,128]{1,0:T(8,128)S(1)}, f32[88,128]{1,0:T(8,128)S(1)}, u32[]{:S(2)}, u32[]{:S(2)}) %collective-permute-start.10) | collective-permute-done | bytes 45088 | tf_op jit(solution)/shard_map/ppermute | solution.py:286
  72.6 0.3 second_image.1
  72.9 13.9 %all_to_all.16.sums_ref = f32[32,1,128]{2,1,0:T(1,128)S(1)} all-to-all(f32[32,1,128]{2,1,0:T(1,128)S(1)} %get-tuple-element.21), channel_id=1, replica_groups=mesh['z'=8,'xl'=2,'y'=4,'xh'=2,'core'=2] {'z','y'}, dimensions={0} | all-to-all | bytes 32768 | tf_op jit(solution)/shard_map/all_to_all | solution.py:341
  86.8 0.9 %finish.1 = (f32[8,128]{1,0:T(8,128)}, f32[8,128]{1,0:T(8,128)}) custom-call(f32[4,8,128]{2,1,0:T(8,128)S(1)} %get-tuple-element.20.own_ref, f32[32,1,128]{2,1,0:T(1,128)S(1)} %all_to_all.16.sums_ref), custom_call_target="tpu_custom_call" | custom-call | tf_op jit(solution)/shard_map/finish/pallas_call | solution.py:267
  (9 shorter events, 0.0 us)
Async XLA Ops:
  2.2 22.9 %all-to-all-start = ((f32[32,16,128]{2,1,0:T(8,128)}), f32[32,16,128]{2,1,0:T(8,128)S(1)}, u32[]{:S(2)}, u32[]{:S(2)}) async-start(f32[32,16,128]{2,1,0:T(8,128)} %get-tuple-element.12), calls=%async_computation | async-start | bytes 524288 | tf_op jit(solution)/shard_map/all_to_all | solution.py:307
  13.9 1.3 %collective-permute-start = (f32[1,16,128]{2,1,0:T(8,128)S(1)}, f32[1,16,128]{2,1,0:T(8,128)S(1)}, u32[]{:S(2)}, u32[]{:S(2)}) collective-permute-start(f32[1,16,128]{2,1,0:T(8,128)S(1)} %get-tuple-element.13), channel_id=1, source_target_pairs={{0,1},{1,0},{2,3},{3,2},{4,5},{5,4},{6,7},{7,6},{8,9},{9,8},{10,11... | collective-permute-start | bytes 24584 | tf_op jit(solution)/shard_map/ppermute | solution.py:286
  15.2 5.2 %collective-permute-start.1 = (f32[2,16,128]{2,1,0:T(8,128)S(1)}, f32[2,16,128]{2,1,0:T(8,128)S(1)}, u32[]{:S(2)}, u32[]{:S(2)}) collective-permute-start(f32[2,16,128]{2,1,0:T(8,128)S(1)} %get-tuple-element.26), channel_id=1, source_target_pairs={{0,2},{2,0},{1,3},{3,1},{4,6},{6,4},{5,7},{7,5},{8,10},{10,8},{9,1... | collective-permute-start | bytes 49160 | tf_op jit(solution)/shard_map/ppermute | solution.py:286
  18.2 4.9 %collective-permute-start.3 = (f32[2,16,128]{2,1,0:T(8,128)S(1)}, f32[2,16,128]{2,1,0:T(8,128)S(1)}, u32[]{:S(2)}, u32[]{:S(2)}) collective-permute-start(f32[2,16,128]{2,1,0:T(8,128)S(1)} %get-tuple-element.26), channel_id=1, source_target_pairs={{0,18},{2,16},{16,2},{18,0},{1,19},{3,17},{17,3},{19,1},{4,22},{6,... | collective-permute-start | bytes 49160 | tf_op jit(solution)/shard_map/ppermute | solution.py:286
  19.3 3.7 %collective-permute-start.2 = (f32[2,16,128]{2,1,0:T(8,128)S(1)}, f32[2,16,128]{2,1,0:T(8,128)S(1)}, u32[]{:S(2)}, u32[]{:S(2)}) collective-permute-start(f32[2,16,128]{2,1,0:T(8,128)S(1)} %get-tuple-element.26), channel_id=1, source_target_pairs={{0,16},{16,0},{1,17},{17,1},{2,18},{18,2},{3,19},{19,3},{4,20},{20... | collective-permute-start | bytes 49160 | tf_op jit(solution)/shard_map/ppermute | solution.py:286
  33.4 1.2 %collective-permute-start.4 = (f32[4,16,128]{2,1,0:T(8,128)S(1)}, f32[4,16,128]{2,1,0:T(8,128)S(1)}, u32[]{:S(2)}, u32[]{:S(2)}) collective-permute-start(f32[4,16,128]{2,1,0:T(8,128)S(1)} %slice_bitcast_fusion), channel_id=1, source_target_pairs={{0,1},{1,0},{2,3},{3,2},{4,5},{5,4},{6,7},{7,6},{8,9},{9,8},{10,11... | collective-permute-start | bytes 98312 | tf_op jit(solution)/shard_map/ppermute | solution.py:286
  34.7 5.1 %collective-permute-start.7 = (f32[1,16,128]{2,1,0:T(8,128)S(1)}, f32[1,16,128]{2,1,0:T(8,128)S(1)}, u32[]{:S(2)}, u32[]{:S(2)}) collective-permute-start(f32[1,16,128]{2,1,0:T(8,128)S(1)} %get-tuple-element.22), channel_id=1, source_target_pairs={{0,18},{2,16},{16,2},{18,0},{1,19},{3,17},{17,3},{19,1},{4,22},{6,... | collective-permute-start | bytes 24584 | tf_op jit(solution)/shard_map/ppermute | solution.py:286
  37.7 3.7 %collective-permute-start.6 = (f32[1,16,128]{2,1,0:T(8,128)S(1)}, f32[1,16,128]{2,1,0:T(8,128)S(1)}, u32[]{:S(2)}, u32[]{:S(2)}) collective-permute-start(f32[1,16,128]{2,1,0:T(8,128)S(1)} %get-tuple-element.23), channel_id=1, source_target_pairs={{0,16},{16,0},{1,17},{17,1},{2,18},{18,2},{3,19},{19,3},{4,20},{20... | collective-permute-start | bytes 24584 | tf_op jit(solution)/shard_map/ppermute | solution.py:286
  37.9 5.2 %collective-permute-start.5 = (f32[1,16,128]{2,1,0:T(8,128)S(1)}, f32[1,16,128]{2,1,0:T(8,128)S(1)}, u32[]{:S(2)}, u32[]{:S(2)}) collective-permute-start(f32[1,16,128]{2,1,0:T(8,128)S(1)} %get-tuple-element.24), channel_id=1, source_target_pairs={{0,2},{2,0},{1,3},{3,1},{4,6},{6,4},{5,7},{7,5},{8,10},{10,8},{9,1... | collective-permute-start | bytes 24584 | tf_op jit(solution)/shard_map/ppermute | solution.py:286
  63.2 1.4 %collective-permute-start.8 = (f32[72,128]{1,0:T(8,128)S(1)}, f32[72,128]{1,0:T(8,128)S(1)}, u32[]{:S(2)}, u32[]{:S(2)}) collective-permute-start(f32[72,128]{1,0:T(8,128)S(1)} %get-tuple-element.17.ours_ref), channel_id=1, source_target_pairs={{0,1},{1,0},{2,3},{3,2},{4,5},{5,4},{6,7},{7,6},{8,9},{9,8},{10,11... | collective-permute-start | bytes 110600 | tf_op jit(solution)/shard_map/ppermute | solution.py:286
  63.3 1.3 %collective-permute-start.9 = (f32[8,128]{1,0:T(8,128)S(1)}, f32[8,128]{1,0:T(8,128)S(1)}, u32[]{:S(2)}, u32[]{:S(2)}) collective-permute-start(f32[8,128]{1,0:T(8,128)S(1)} %get-tuple-element.18.ours_image_ref), channel_id=1, source_target_pairs={{0,1},{1,0},{2,3},{3,2},{4,5},{5,4},{6,7},{7,6},{8,9},{9,8},{10,11... | collective-permute-start | bytes 12296 | tf_op jit(solution)/shard_map/ppermute | solution.py:286
  64.6 5.3 %collective-permute-start.12 = (f32[88,128]{1,0:T(8,128)S(1)}, f32[88,128]{1,0:T(8,128)S(1)}, u32[]{:S(2)}, u32[]{:S(2)}) collective-permute-start(f32[88,128]{1,0:T(8,128)S(1)} %core_sum.1.own_part), channel_id=1, source_target_pairs={{0,18},{2,16},{16,2},{18,0},{1,19},{3,17},{17,3},{19,1},{4,22},{6,... | collective-permute-start | bytes 135176 | tf_op jit(solution)/shard_map/ppermute | solution.py:286
  66.0 4.0 %collective-permute-start.11 = (f32[88,128]{1,0:T(8,128)S(1)}, f32[88,128]{1,0:T(8,128)S(1)}, u32[]{:S(2)}, u32[]{:S(2)}) collective-permute-start(f32[88,128]{1,0:T(8,128)S(1)} %core_sum.1.own_part), channel_id=1, source_target_pairs={{0,16},{16,0},{1,17},{17,1},{2,18},{18,2},{3,19},{19,3},{4,20},{20... | collective-permute-start | bytes 135176 | tf_op jit(solution)/shard_map/ppermute | solution.py:286
  67.1 5.6 %collective-permute-start.10 = (f32[88,128]{1,0:T(8,128)S(1)}, f32[88,128]{1,0:T(8,128)S(1)}, u32[]{:S(2)}, u32[]{:S(2)}) collective-permute-start(f32[88,128]{1,0:T(8,128)S(1)} %core_sum.1.own_part), channel_id=1, source_target_pairs={{0,2},{2,0},{1,3},{3,1},{4,6},{6,4},{5,7},{7,5},{8,10},{10,8},{9,1... | collective-permute-start | bytes 135176 | tf_op jit(solution)/shard_map/ppermute | solution.py:286

commit v4 on v3

--- a/solution.py
+++ b/solution.py
@@ -21,9 +21,11 @@
 NI, NJ = NR * OWN, NC * OWN
 noise_level = 0.5
 
-POINT_SCALE = math.sqrt(5.0 / 3.0)
-ROOT3 = math.sqrt(3.0)
-EXP_SCALE = -math.sqrt(3.0) * math.log2(math.e)
+LOG2E = math.log2(math.e)
+POINT_SCALE = math.sqrt(5.0) * LOG2E
+SHIFT = 1.5 * LOG2E
+REST = SHIFT * SHIFT / 3.0
+FACTOR = 2.0**SHIFT * 0.75 / (SHIFT * SHIFT)
 
 TI, TJ = 256, 256
 
@@ -50,10 +52,17 @@
     return jnp.concatenate(parts + [jnp.concatenate(tail, 0), jnp.zeros_like(a)], 0)
 
 
-def matern(tau):
-    tau = jnp.maximum(tau, 1e-30)
-    s = tau * lax.rsqrt(tau)
-    return ((1.0 + tau) + ROOT3 * s) * jnp.exp2(EXP_SCALE * s)
+def matern(square):
+    square = jnp.maximum(square, 1e-30)
+    u = -SHIFT - square * lax.rsqrt(square)
+    return (u * u + REST) * jnp.exp2(u)
+
+
+def product(values, tile):
+    high = tile.astype(bf16)
+    low = (tile - high.astype(f32)).astype(bf16)
+    out = jnp.dot(values, high, preferred_element_type=f32)
+    return out + jnp.dot(values, low, preferred_element_type=f32)
 
 
 def stacked(values):
@@ -97,7 +106,7 @@
     return lax.axis_index("xl") * 4 + lax.axis_index("xh") * 2 + lax.axis_index("core")
 
 
-def first_product(rows_ref, cols_ref, high_ref, low_ref, out_ref):
+def first_product(rows_ref, cols_ref, kernel_ref, out_ref):
     left = features(lanes(rows_ref, 0, NR), True).astype(bf16)
     right = features(lanes(cols_ref, 0, NC), False).T.astype(bf16)
     values = stacked(lanes(cols_ref, 8, NC))
@@ -105,16 +114,11 @@
     for i in range(0, NI, TI):
         acc = jnp.zeros((24, TI), f32)
         for j in range(0, NJ, TJ):
-            tau = jnp.dot(right[j : j + TJ], left[:, i : i + TI], preferred_element_type=f32)
-            tile = matern(tau)
-            high = tile.astype(bf16)
-            low = (tile - high.astype(f32)).astype(bf16)
-            high_ref[j : j + TJ, i : i + TI] = high
-            low_ref[j : j + TJ, i : i + TI] = low
-            part = values[:, j : j + TJ]
-            acc = acc + jnp.dot(part, high, preferred_element_type=f32)
-            acc = acc + jnp.dot(part, low, preferred_element_type=f32)
-        acc = acc[0:8] + acc[8:16] + acc[16:24]
+            square = jnp.dot(right[j : j + TJ], left[:, i : i + TI], preferred_element_type=f32)
+            tile = matern(square)
+            kernel_ref[j : j + TJ, i : i + TI] = tile
+            acc = acc + product(values[:, j : j + TJ], tile)
+        acc = (acc[0:8] + acc[8:16] + acc[16:24]) * FACTOR
         for k in range(TI // OWN):
             block = i // OWN + k
             part = acc[:, k * OWN : (k + 1) * OWN]
@@ -133,7 +137,7 @@
     return out
 
 
-def first_image(own_ref, xh_ref, xl_ref, both_ref, rows_ref, out_ref):
+def first_image(own_ref, xh_ref, xl_ref, both_ref, rows_ref, out_ref, image_ref):
     sums = (own_ref[0] + xh_ref[0]) + (xl_ref[0] + both_ref[0])
     targets = rows_ref[0, 8:16, :]
     bb = jnp.zeros((8, OWN), f32)
@@ -141,42 +145,44 @@
         bb = bb + rows_ref[k, 8:16, :] * rows_ref[k, 8:16, :]
     bb = total(bb)
     image = sums[0:8] + noise_level * targets
-    scalars = at_lanes([bb, sums[8:16, 0:1] + noise_level * bb])
+    scalars = in_one_row([bb, sums[8:16, 0:1] + noise_level * bb])
     for copy in range(NC):
-        out_ref[copy, 0:8, :] = image
-        out_ref[copy, 8:16, :] = scalars
-
-
-def second_product(cols_ref, image_cols_ref, high_ref, low_ref, out_ref, image_ref, scalar_ref):
-    sums = image_cols_ref[0, 8:16, :]
+        for row in range(8):
+            out_ref[9 * copy + row] = image[row : row + 1]
+        out_ref[9 * copy + 8] = scalars
+    image_ref[...] = image
+
+
+def second_product(cols_ref, image_cols_ref, image_ref, kernel_ref, out_ref, scalar_ref):
+    sums = image_cols_ref[8]
     for k in range(1, NC):
-        sums = sums + image_cols_ref[k, 8:16, :]
-    norm = sums[:, 0:1]
-    step = norm / sums[:, 1:2]
-    residual = lanes(cols_ref, 8, NC) - step * lanes(image_cols_ref, 0, NC)
+        sums = sums + image_cols_ref[9 * k + 8]
+    norm = column_of(sums, 0)
+    step = norm / column_of(sums, 1)
+    images = [image_cols_ref[9 * k : 9 * k + 8].reshape(8, OWN) for k in range(NC)]
+    residual = lanes(cols_ref, 8, NC) - step * jnp.concatenate(images, 1)
     norm_part = jnp.broadcast_to(total(residual * residual), (8, OWN))
     values = stacked(residual)
     mine = my_row_block()
-    image = image_cols_ref[my_col_block(), 0:8, :]
     for i in range(0, NI, TI):
-        acc = jnp.dot(values, high_ref[:, i : i + TI], preferred_element_type=f32)
-        acc = acc + jnp.dot(values, low_ref[:, i : i + TI], preferred_element_type=f32)
-        acc = acc[0:8] + acc[8:16] + acc[16:24]
+        acc = jnp.zeros((24, TI), f32)
+        for j in range(0, NJ, TJ):
+            acc = acc + product(values[:, j : j + TJ], kernel_ref[j : j + TJ, i : i + TI])
+        acc = (acc[0:8] + acc[8:16] + acc[16:24]) * FACTOR
         for k in range(TI // OWN):
             row = pl.multiple_of((mine ^ (i // OWN + k)) * 8, 8)
             out_ref[pl.ds(row, 8), :] = acc[:, k * OWN : (k + 1) * OWN]
     out_ref[NR * 8 : NR * 8 + 8, :] = norm_part
-    image_ref[...] = image
+    out_ref[NR * 8 + 8 :, :] = image_ref[...]
     scalar_ref[...] = at_lanes([norm, step])
 
 
-def core_sum(ours_ref, theirs_ref, ours_image_ref, theirs_image_ref, out_ref):
+def core_sum(ours_ref, theirs_ref, out_ref):
     core = lax.axis_index("core")
-    out_ref[0 : NR * 8 + 8, :] = ours_ref[...] + theirs_ref[...]
-    first = pl.multiple_of(NR * 8 + 8 + core * 8, 8)
-    out_ref[pl.ds(first, 8), :] = ours_image_ref[...]
-    second = pl.multiple_of(NR * 8 + 16 - core * 8, 8)
-    out_ref[pl.ds(second, 8), :] = theirs_image_ref[...]
+    sums = NR * 8 + 8
+    out_ref[0:sums, :] = ours_ref[0:sums, :] + theirs_ref[0:sums, :]
+    out_ref[pl.ds(pl.multiple_of(sums + core * 8, 8), 8), :] = ours_ref[sums:, :]
+    out_ref[pl.ds(pl.multiple_of(sums + 8 - core * 8, 8), 8), :] = theirs_ref[sums:, :]
 
 
 def second_image(own_part, xh_part, xl_part, both_part, rows_ref, scalar_ref, own_ref, out_ref, keep_ref, part_ref):
@@ -259,10 +265,6 @@
     direction_ref[...] = residual + (norm_next / norm) * own_ref[1]
 
 
-def my_col_block():
-    return lax.axis_index("z") * 4 + lax.axis_index("y")
-
-
 def call(kernel, outs, name, args, scratch=(), vmem=4 << 20):
     return pl.pallas_call(
         kernel,
@@ -307,28 +309,29 @@
     cols = lax.all_to_all(copies, COLG, 0, 0)
     rows = jnp.concatenate([own, swap(own, ("core",))], 0)
     rows = jnp.concatenate([rows] + [swap(rows, axes) for axes in CHIPS], 0)
-    tile = VMEM((NJ, NI), bf16)
-    high, low, part = call(
-        first_product, [tile, tile, shape(2, 4, 16, OWN)], "first_product", [rows, cols], vmem=24 << 20
+    kernel, part = call(
+        first_product,
+        [VMEM((NJ, NI), f32), shape(2, 4, 16, OWN)],
+        "first_product",
+        [rows, cols],
+        vmem=24 << 20,
     )
     part = part[0] + swap(part[1], ("core",))
     parts = [part[0:1]] + [swap(part[k : k + 1], axes) for k, axes in enumerate(CHIPS, 1)]
-    message = call(first_image, [shape(NC, 16, OWN)], "first_image", parts + [rows])[0]
-    image_cols = lax.all_to_all(message, COLG, 0, 0)
-    high = pltpu.with_memory_space_constraint(high, VMEM)
-    low = pltpu.with_memory_space_constraint(low, VMEM)
-    part, image, scalars = call(
+    message, image = call(
+        first_image, [shape(NC * 9, 1, OWN), shape(8, OWN)], "first_image", parts + [rows]
+    )
+    image_cols = lax.all_to_all(message, COLG, 0, 0, tiled=True)
+    kernel = pltpu.with_memory_space_constraint(kernel, VMEM)
+    part, scalars = call(
         second_product,
-        [shape(NR * 8 + 8, OWN), shape(8, OWN), shape(8, OWN)],
+        [shape(NR * 8 + 16, OWN), shape(8, OWN)],
         "second_product",
-        [cols, image_cols, high, low],
+        [cols, image_cols, image, kernel],
         vmem=8 << 20,
     )
     part = call(
-        core_sum,
-        [shape(NR * 8 + 24, OWN)],
-        "core_sum",
-        [part, swap(part, ("core",)), image, swap(image, ("core",))],
+        core_sum, [shape(NR * 8 + 24, OWN)], "core_sum", [part, swap(part, ("core",))]
     )[0]
     parts = [part] + [swap(part, axes) for axes in CHIPS]
     keep, message = call(

time: 88.5 us -> 86.2 us (0.974)
  blocking collectives: 30.7 us -> 29.1 us
    all_to_all x1, blocking collectives: 16.8 us -> 15.6 us  [per_device(): image_cols = lax.all_to_all(message, COLG, 0, 0, tiled=True)]
    ppermute x13 -> x12, starting transfers between devices: 14.6 us -> 14 us  [swap(): return lax.ppermute(x, axes, [(i, size - 1 - i) for i in range(size)])]
    ppermute x13 -> x12, waiting for transfers between devices: 13.6 us -> 14.3 us  [swap(): return lax.ppermute(x, axes, [(i, size - 1 - i) for i in range(size)])]
  transfers between devices with their start and end apart: 14 -> 13, of which waited for: 12 -> 12; matrix products, arithmetic and copies ran while one was open for 0% -> 0% of each run, Pallas kernels for 0% -> 0%
where the time goes in v4:
time: 86.2 us; the launch traced here: 85.6 us
  blocking collectives  29.1 us (34%)
  starting transfers between devices  25.7 us (30%)
  waiting for transfers between devices  16.2 us (19%)
  Pallas kernels  13.8 us (16%)
    all_to_all x1, blocking collectives, per_device(): image_cols = lax.all_to_all(message, COLG, 0, 0, tiled=True)  15.6 us
    ppermute x12, waiting for transfers between devices, swap(): return lax.ppermute(x, axes, [(i, size - 1 - i) for i in range(size)])  14.3 us
    ppermute x12, starting transfers between devices, swap(): return lax.ppermute(x, axes, [(i, size - 1 - i) for i in range(size)])  14 us
    all_to_all x1, blocking collectives, per_device(): sums = lax.all_to_all(message, COLG, 0, 0)  13.6 us
    pallas_call x6, Pallas kernels, call(): pl.pallas_call(kernel, in_specs=[pl.BlockSpec(memory_space=VMEM) for _ in...  12.3 us
    all_to_all x1, starting transfers between devices, per_device(): cols = lax.all_to_all(copies, COLG, 0, 0)  11.7 us
    all_to_all x1, waiting for transfers between devices, per_device(): cols = lax.all_to_all(copies, COLG, 0, 0)  1.97 us
  transfers between devices with their start and end apart: 13, of which 12 were waited for; matrix products, arithmetic and copies ran while one was open for 0% of the time, Pallas kernels for 0%

profile of v4, /device:TPU:8, one launch (start us, length us, event | category | flops | bytes accessed | tf_op | source)
XLA Modules:
  0.0 85.6 jit_solution(2577199399021349039)
XLA Ops:
  0.6 1.5 %pack.1 = (f32[1,16,128]{2,1,0:T(8,128)S(1)}, f32[32,16,128]{2,1,0:T(8,128)}) custom-call(f32[8,128]{1,0:T(8,128)} %points_hbm.1, f32[8]{0:T(128)} %lengthscale_hbm.1, f32[8,128]{1,0:T(8,128)} %targets_hbm.1), custom_call_target="tpu_custom_call" | custom-call | tf_op jit(solution)/shard_map/pack/pallas_call | solution.py:295
  2.2 11.7 %all-to-all-start = ((f32[32,16,128]{2,1,0:T(8,128)}), f32[32,16,128]{2,1,0:T(8,128)S(1)}, u32[]{:S(2)}, u32[]{:S(2)}) async-start(f32[32,16,128]{2,1,0:T(8,128)} %get-tuple-element.12), calls=%async_computation | async-start | bytes 524288 | tf_op jit(solution)/shard_map/all_to_all | solution.py:309
  13.9 0.1 collective-permute-start
  14.0 1.1 %collective-permute-done = f32[1,16,128]{2,1,0:T(8,128)S(1)} collective-permute-done((f32[1,16,128]{2,1,0:T(8,128)S(1)}, f32[1,16,128]{2,1,0:T(8,128)S(1)}, u32[]{:S(2)}, u32[]{:S(2)}) %collective-permute-start) | collective-permute-done | bytes 8224 | tf_op jit(solution)/shard_map/ppermute | solution.py:288
  15.2 3.0 %collective-permute-start.1 = (f32[2,16,128]{2,1,0:T(8,128)S(1)}, f32[2,16,128]{2,1,0:T(8,128)S(1)}, u32[]{:S(2)}, u32[]{:S(2)}) collective-permute-start(f32[2,16,128]{2,1,0:T(8,128)S(1)} %get-tuple-element.26), channel_id=1, source_target_pairs={{0,2},{2,0},{1,3},{3,1},{4,6},{6,4},{5,7},{7,5},{8,10},{10,8},{9,1... | collective-permute-start | bytes 49160 | tf_op jit(solution)/shard_map/ppermute | solution.py:288
  18.2 1.1 %collective-permute-start.3 = (f32[2,16,128]{2,1,0:T(8,128)S(1)}, f32[2,16,128]{2,1,0:T(8,128)S(1)}, u32[]{:S(2)}, u32[]{:S(2)}) collective-permute-start(f32[2,16,128]{2,1,0:T(8,128)S(1)} %get-tuple-element.26), channel_id=1, source_target_pairs={{0,18},{2,16},{16,2},{18,0},{1,19},{3,17},{17,3},{19,1},{4,22},{6,... | collective-permute-start | bytes 49160 | tf_op jit(solution)/shard_map/ppermute | solution.py:288
  19.3 0.0 collective-permute-start.2
  19.3 1.1 %collective-permute-done.1 = f32[2,16,128]{2,1,0:T(8,128)S(1)} collective-permute-done((f32[2,16,128]{2,1,0:T(8,128)S(1)}, f32[2,16,128]{2,1,0:T(8,128)S(1)}, u32[]{:S(2)}, u32[]{:S(2)}) %collective-permute-start.1) | collective-permute-done | bytes 16416 | tf_op jit(solution)/shard_map/ppermute | solution.py:288
  20.4 2.7 %collective-permute-done.2 = f32[2,16,128]{2,1,0:T(8,128)S(1)} collective-permute-done((f32[2,16,128]{2,1,0:T(8,128)S(1)}, f32[2,16,128]{2,1,0:T(8,128)S(1)}, u32[]{:S(2)}, u32[]{:S(2)}) %collective-permute-start.2) | collective-permute-done | bytes 16416 | tf_op jit(solution)/shard_map/ppermute | solution.py:288
  23.1 0.1 collective-permute-done.3
  23.1 2.0 %all-to-all-done.cols_ref = f32[32,16,128]{2,1,0:T(8,128)S(1)} async-done(((f32[32,16,128]{2,1,0:T(8,128)}), f32[32,16,128]{2,1,0:T(8,128)S(1)}, u32[]{:S(2)}, u32[]{:S(2)}) %all-to-all-start) | async-done | bytes 262176 | tf_op jit(solution)/shard_map/all_to_all | solution.py:309
  25.1 7.7 %first_product.1 = (f32[4096,1024]{1,0:T(8,128)S(1)}, f32[2,4,16,128]{3,2,1,0:T(8,128)S(1)}) custom-call(f32[8,16,128]{2,1,0:T(8,128)S(1)} %constant_dynamic-update-slice_fusion.2.rows_ref, f32[32,16,128]{2,1,0:T(8,128)S(1)} %all-to-all-done.cols_ref), custom_call_target="tpu_custom_call" | custom-call | tf_op jit(solution)/shard_map/first_product/pallas_call | solution.py:269
  32.8 0.0 collective-permute-start.4
  32.9 1.2 %collective-permute-done.4 = f32[4,16,128]{2,1,0:T(8,128)S(1)} collective-permute-done((f32[4,16,128]{2,1,0:T(8,128)S(1)}, f32[4,16,128]{2,1,0:T(8,128)S(1)}, u32[]{:S(2)}, u32[]{:S(2)}) %collective-permute-start.4) | collective-permute-done | bytes 32800 | tf_op jit(solution)/shard_map/ppermute | solution.py:288
  34.1 2.8 %collective-permute-start.7 = (f32[1,16,128]{2,1,0:T(8,128)S(1)}, f32[1,16,128]{2,1,0:T(8,128)S(1)}, u32[]{:S(2)}, u32[]{:S(2)}) collective-permute-start(f32[1,16,128]{2,1,0:T(8,128)S(1)} %get-tuple-element.22), channel_id=1, source_target_pairs={{0,18},{2,16},{16,2},{18,0},{1,19},{3,17},{17,3},{19,1},{4,22},{6,... | collective-permute-start | bytes 24584 | tf_op jit(solution)/shard_map/ppermute | solution.py:288
  36.9 0.2 collective-permute-start.6
  37.1 1.7 %collective-permute-start.5 = (f32[1,16,128]{2,1,0:T(8,128)S(1)}, f32[1,16,128]{2,1,0:T(8,128)S(1)}, u32[]{:S(2)}, u32[]{:S(2)}) collective-permute-start(f32[1,16,128]{2,1,0:T(8,128)S(1)} %get-tuple-element.24), channel_id=1, source_target_pairs={{0,2},{2,0},{1,3},{3,1},{4,6},{6,4},{5,7},{7,5},{8,10},{10,8},{9,1... | collective-permute-start | bytes 24584 | tf_op jit(solution)/shard_map/ppermute | solution.py:288
  38.9 0.2 collective-permute-done.7.both_ref
  39.0 1.5 %collective-permute-done.6.xl_ref = f32[1,16,128]{2,1,0:T(8,128)S(1)} collective-permute-done((f32[1,16,128]{2,1,0:T(8,128)S(1)}, f32[1,16,128]{2,1,0:T(8,128)S(1)}, u32[]{:S(2)}, u32[]{:S(2)}) %collective-permute-start.6) | collective-permute-done | bytes 8224 | tf_op jit(solution)/shard_map/ppermute | solution.py:288
  40.6 1.7 %collective-permute-done.5.xh_ref = f32[1,16,128]{2,1,0:T(8,128)S(1)} collective-permute-done((f32[1,16,128]{2,1,0:T(8,128)S(1)}, f32[1,16,128]{2,1,0:T(8,128)S(1)}, u32[]{:S(2)}, u32[]{:S(2)}) %collective-permute-start.5) | collective-permute-done | bytes 8224 | tf_op jit(solution)/shard_map/ppermute | solution.py:288
  42.3 0.2 first_image.1
  42.5 15.6 %all_to_all.15.image_cols_ref = f32[288,1,128]{2,1,0:T(1,128)S(1)} all-to-all(f32[288,1,128]{2,1,0:T(1,128)S(1)} %get-tuple-element.15), channel_id=1, replica_groups=mesh['z'=8,'xl'=2,'y'=4,'xh'=2,'core'=2] {'z','y'}, dimensions={0} | all-to-all | bytes 294912 | tf_op jit(solution)/shard_map/all_to_all | solution.py:324
  58.0 3.2 %second_product.1 = (f32[80,128]{1,0:T(8,128)S(1)}, f32[8,128]{1,0:T(8,128)S(1)}) custom-call(f32[32,16,128]{2,1,0:T(8,128)S(1)} %all-to-all-done.cols_ref, f32[288,1,128]{2,1,0:T(1,128)S(1)} %all_to_all.15.image_cols_ref, f32[8,128]{1,0:T(8,128)S(1)} %get-tuple-element.16.image_ref, f32[4096,1024]{1,0:T(8,128)S(1)} %get-tuple-element.17.kernel_ref), custom_call_target="tpu_custom_call" | custom-call | tf_op jit(solution)/shard_map/second_product/pallas_call | solution.py:269
  61.3 0.1 collective-permute-start.8
  61.4 1.2 %collective-permute-done.8.theirs_ref = f32[80,128]{1,0:T(8,128)S(1)} collective-permute-done((f32[80,128]{1,0:T(8,128)S(1)}, f32[80,128]{1,0:T(8,128)S(1)}, u32[]{:S(2)}, u32[]{:S(2)}) %collective-permute-start.8) | collective-permute-done | bytes 40992 | tf_op jit(solution)/shard_map/ppermute | solution.py:288
  62.6 1.3 %collective-permute-start.11 = (f32[88,128]{1,0:T(8,128)S(1)}, f32[88,128]{1,0:T(8,128)S(1)}, u32[]{:S(2)}, u32[]{:S(2)}) collective-permute-start(f32[88,128]{1,0:T(8,128)S(1)} %core_sum.1.own_part), channel_id=1, source_target_pairs={{0,18},{2,16},{16,2},{18,0},{1,19},{3,17},{17,3},{19,1},{4,22},{6,... | collective-permute-start | bytes 135176 | tf_op jit(solution)/shard_map/ppermute | solution.py:288
  63.9 1.4 %collective-permute-start.10 = (f32[88,128]{1,0:T(8,128)S(1)}, f32[88,128]{1,0:T(8,128)S(1)}, u32[]{:S(2)}, u32[]{:S(2)}) collective-permute-start(f32[88,128]{1,0:T(8,128)S(1)} %core_sum.1.own_part), channel_id=1, source_target_pairs={{0,16},{16,0},{1,17},{17,1},{2,18},{18,2},{3,19},{19,3},{4,20},{20... | collective-permute-start | bytes 135176 | tf_op jit(solution)/shard_map/ppermute | solution.py:288
  65.3 2.1 %collective-permute-start.9 = (f32[88,128]{1,0:T(8,128)S(1)}, f32[88,128]{1,0:T(8,128)S(1)}, u32[]{:S(2)}, u32[]{:S(2)}) collective-permute-start(f32[88,128]{1,0:T(8,128)S(1)} %core_sum.1.own_part), channel_id=1, source_target_pairs={{0,2},{2,0},{1,3},{3,1},{4,6},{6,4},{5,7},{7,5},{8,10},{10,8},{9,1... | collective-permute-start | bytes 135176 | tf_op jit(solution)/shard_map/ppermute | solution.py:288
  67.3 0.6 collective-permute-done.11.both_part
  67.9 0.0 collective-permute-done.10.xl_part
  67.9 2.9 %collective-permute-done.9.xh_part = f32[88,128]{1,0:T(8,128)S(1)} collective-permute-done((f32[88,128]{1,0:T(8,128)S(1)}, f32[88,128]{1,0:T(8,128)S(1)}, u32[]{:S(2)}, u32[]{:S(2)}) %collective-permute-start.9) | collective-permute-done | bytes 45088 | tf_op jit(solution)/shard_map/ppermute | solution.py:288
  70.8 0.3 second_image.1
  71.1 13.6 %all_to_all.16.sums_ref = f32[32,1,128]{2,1,0:T(1,128)S(1)} all-to-all(f32[32,1,128]{2,1,0:T(1,128)S(1)} %get-tuple-element.21), channel_id=1, replica_groups=mesh['z'=8,'xl'=2,'y'=4,'xh'=2,'core'=2] {'z','y'}, dimensions={0} | all-to-all | bytes 32768 | tf_op jit(solution)/shard_map/all_to_all | solution.py:344
  84.7 0.9 %finish.1 = (f32[8,128]{1,0:T(8,128)}, f32[8,128]{1,0:T(8,128)}) custom-call(f32[4,8,128]{2,1,0:T(8,128)S(1)} %get-tuple-element.20.own_ref, f32[32,1,128]{2,1,0:T(1,128)S(1)} %all_to_all.16.sums_ref), custom_call_target="tpu_custom_call" | custom-call | tf_op jit(solution)/shard_map/finish/pallas_call | solution.py:269
  (9 shorter events, 0.0 us)
Async XLA Ops:
  2.2 22.9 %all-to-all-start = ((f32[32,16,128]{2,1,0:T(8,128)}), f32[32,16,128]{2,1,0:T(8,128)S(1)}, u32[]{:S(2)}, u32[]{:S(2)}) async-start(f32[32,16,128]{2,1,0:T(8,128)} %get-tuple-element.12), calls=%async_computation | async-start | bytes 524288 | tf_op jit(solution)/shard_map/all_to_all | solution.py:309
  13.9 1.3 %collective-permute-start = (f32[1,16,128]{2,1,0:T(8,128)S(1)}, f32[1,16,128]{2,1,0:T(8,128)S(1)}, u32[]{:S(2)}, u32[]{:S(2)}) collective-permute-start(f32[1,16,128]{2,1,0:T(8,128)S(1)} %get-tuple-element.13), channel_id=1, source_target_pairs={{0,1},{1,0},{2,3},{3,2},{4,5},{5,4},{6,7},{7,6},{8,9},{9,8},{10,11... | collective-permute-start | bytes 24584 | tf_op jit(solution)/shard_map/ppermute | solution.py:288
  15.2 5.2 %collective-permute-start.1 = (f32[2,16,128]{2,1,0:T(8,128)S(1)}, f32[2,16,128]{2,1,0:T(8,128)S(1)}, u32[]{:S(2)}, u32[]{:S(2)}) collective-permute-start(f32[2,16,128]{2,1,0:T(8,128)S(1)} %get-tuple-element.26), channel_id=1, source_target_pairs={{0,2},{2,0},{1,3},{3,1},{4,6},{6,4},{5,7},{7,5},{8,10},{10,8},{9,1... | collective-permute-start | bytes 49160 | tf_op jit(solution)/shard_map/ppermute | solution.py:288
  18.2 4.9 %collective-permute-start.3 = (f32[2,16,128]{2,1,0:T(8,128)S(1)}, f32[2,16,128]{2,1,0:T(8,128)S(1)}, u32[]{:S(2)}, u32[]{:S(2)}) collective-permute-start(f32[2,16,128]{2,1,0:T(8,128)S(1)} %get-tuple-element.26), channel_id=1, source_target_pairs={{0,18},{2,16},{16,2},{18,0},{1,19},{3,17},{17,3},{19,1},{4,22},{6,... | collective-permute-start | bytes 49160 | tf_op jit(solution)/shard_map/ppermute | solution.py:288
  19.3 3.7 %collective-permute-start.2 = (f32[2,16,128]{2,1,0:T(8,128)S(1)}, f32[2,16,128]{2,1,0:T(8,128)S(1)}, u32[]{:S(2)}, u32[]{:S(2)}) collective-permute-start(f32[2,16,128]{2,1,0:T(8,128)S(1)} %get-tuple-element.26), channel_id=1, source_target_pairs={{0,16},{16,0},{1,17},{17,1},{2,18},{18,2},{3,19},{19,3},{4,20},{20... | collective-permute-start | bytes 49160 | tf_op jit(solution)/shard_map/ppermute | solution.py:288
  32.8 1.2 %collective-permute-start.4 = (f32[4,16,128]{2,1,0:T(8,128)S(1)}, f32[4,16,128]{2,1,0:T(8,128)S(1)}, u32[]{:S(2)}, u32[]{:S(2)}) collective-permute-start(f32[4,16,128]{2,1,0:T(8,128)S(1)} %slice_bitcast_fusion), channel_id=1, source_target_pairs={{0,1},{1,0},{2,3},{3,2},{4,5},{5,4},{6,7},{7,6},{8,9},{9,8},{10,11... | collective-permute-start | bytes 98312 | tf_op jit(solution)/shard_map/ppermute | solution.py:288
  34.1 4.9 %collective-permute-start.7 = (f32[1,16,128]{2,1,0:T(8,128)S(1)}, f32[1,16,128]{2,1,0:T(8,128)S(1)}, u32[]{:S(2)}, u32[]{:S(2)}) collective-permute-start(f32[1,16,128]{2,1,0:T(8,128)S(1)} %get-tuple-element.22), channel_id=1, source_target_pairs={{0,18},{2,16},{16,2},{18,0},{1,19},{3,17},{17,3},{19,1},{4,22},{6,... | collective-permute-start | bytes 24584 | tf_op jit(solution)/shard_map/ppermute | solution.py:288
  36.9 3.7 %collective-permute-start.6 = (f32[1,16,128]{2,1,0:T(8,128)S(1)}, f32[1,16,128]{2,1,0:T(8,128)S(1)}, u32[]{:S(2)}, u32[]{:S(2)}) collective-permute-start(f32[1,16,128]{2,1,0:T(8,128)S(1)} %get-tuple-element.23), channel_id=1, source_target_pairs={{0,16},{16,0},{1,17},{17,1},{2,18},{18,2},{3,19},{19,3},{4,20},{20... | collective-permute-start | bytes 24584 | tf_op jit(solution)/shard_map/ppermute | solution.py:288
  37.1 5.2 %collective-permute-start.5 = (f32[1,16,128]{2,1,0:T(8,128)S(1)}, f32[1,16,128]{2,1,0:T(8,128)S(1)}, u32[]{:S(2)}, u32[]{:S(2)}) collective-permute-start(f32[1,16,128]{2,1,0:T(8,128)S(1)} %get-tuple-element.24), channel_id=1, source_target_pairs={{0,2},{2,0},{1,3},{3,1},{4,6},{6,4},{5,7},{7,5},{8,10},{10,8},{9,1... | collective-permute-start | bytes 24584 | tf_op jit(solution)/shard_map/ppermute | solution.py:288
  61.3 1.3 %collective-permute-start.8 = (f32[80,128]{1,0:T(8,128)S(1)}, f32[80,128]{1,0:T(8,128)S(1)}, u32[]{:S(2)}, u32[]{:S(2)}) collective-permute-start(f32[80,128]{1,0:T(8,128)S(1)} %get-tuple-element.18.ours_ref), channel_id=1, source_target_pairs={{0,1},{1,0},{2,3},{3,2},{4,5},{5,4},{6,7},{7,6},{8,9},{9,8},{10,11... | collective-permute-start | bytes 122888 | tf_op jit(solution)/shard_map/ppermute | solution.py:288
  62.6 5.3 %collective-permute-start.11 = (f32[88,128]{1,0:T(8,128)S(1)}, f32[88,128]{1,0:T(8,128)S(1)}, u32[]{:S(2)}, u32[]{:S(2)}) collective-permute-start(f32[88,128]{1,0:T(8,128)S(1)} %core_sum.1.own_part), channel_id=1, source_target_pairs={{0,18},{2,16},{16,2},{18,0},{1,19},{3,17},{17,3},{19,1},{4,22},{6,... | collective-permute-start | bytes 135176 | tf_op jit(solution)/shard_map/ppermute | solution.py:288
  63.9 4.0 %collective-permute-start.10 = (f32[88,128]{1,0:T(8,128)S(1)}, f32[88,128]{1,0:T(8,128)S(1)}, u32[]{:S(2)}, u32[]{:S(2)}) collective-permute-start(f32[88,128]{1,0:T(8,128)S(1)} %core_sum.1.own_part), channel_id=1, source_target_pairs={{0,16},{16,0},{1,17},{17,1},{2,18},{18,2},{3,19},{19,3},{4,20},{20... | collective-permute-start | bytes 135176 | tf_op jit(solution)/shard_map/ppermute | solution.py:288
  65.3 5.6 %collective-permute-start.9 = (f32[88,128]{1,0:T(8,128)S(1)}, f32[88,128]{1,0:T(8,128)S(1)}, u32[]{:S(2)}, u32[]{:S(2)}) collective-permute-start(f32[88,128]{1,0:T(8,128)S(1)} %core_sum.1.own_part), channel_id=1, source_target_pairs={{0,2},{2,0},{1,3},{3,1},{4,6},{6,4},{5,7},{7,5},{8,10},{10,8},{9,1... | collective-permute-start | bytes 135176 | tf_op jit(solution)/shard_map/ppermute | solution.py:288

commit v5 on v4

--- a/solution.py
+++ b/solution.py
@@ -14,8 +14,6 @@
 
 AXES = ("z", "xl", "y", "xh", "core")
 SIZES = (8, 2, 4, 2, 2)
-ROWG = ("xl", "xh", "core")
-COLG = ("z", "y")
 NR, NC = 8, 32
 OWN = 128
 NI, NJ = NR * OWN, NC * OWN
@@ -113,11 +111,14 @@
     form = jnp.zeros((8, OWN), f32)
     for i in range(0, NI, TI):
         acc = jnp.zeros((24, TI), f32)
+        lag = TJ
         for j in range(0, NJ, TJ):
             square = jnp.dot(right[j : j + TJ], left[:, i : i + TI], preferred_element_type=f32)
             tile = matern(square)
             kernel_ref[j : j + TJ, i : i + TI] = tile
-            acc = acc + product(values[:, j : j + TJ], tile)
+            if j >= lag:
+                acc = acc + product(values[:, j - lag : j - lag + TJ], kernel_ref[j - lag : j - lag + TJ, i : i + TI])
+        acc = acc + product(values[:, NJ - lag :], kernel_ref[NJ - lag :, i : i + TI])
         acc = (acc[0:8] + acc[8:16] + acc[16:24]) * FACTOR
         for k in range(TI // OWN):
             block = i // OWN + k
@@ -283,6 +284,20 @@
     return jax.ShapeDtypeStruct(dims, f32)
 
 
+def column_groups():
+    order = [
+        ((z + 4) % 8, ((y if z % 2 == 0 else 3 - y) + 2) % 4) for z in range(8) for y in range(4)
+    ]
+    return [
+        [(((z * 2 + r // 4) * 4 + y) * 2 + r // 2 % 2) * 2 + r % 2 for z, y in order]
+        for r in range(NR)
+    ]
+
+
+def column_exchange(x):
+    return lax.all_to_all(x, AXES, 0, 0, axis_index_groups=column_groups(), tiled=True)
+
+
 def swap(x, axes):
     size = 2 ** len(axes)
     return lax.ppermute(x, axes, [(i, size - 1 - i) for i in range(size)])
@@ -306,7 +321,7 @@
         compiler_params=pltpu.CompilerParams(vmem_limit_bytes=4 << 20),
         name="pack",
     )(*[pltpu.with_memory_space_constraint(a, pltpu.HBM) for a in (points, lengthscale, targets)])
-    cols = lax.all_to_all(copies, COLG, 0, 0)
+    cols = column_exchange(copies)
     rows = jnp.concatenate([own, swap(own, ("core",))], 0)
     rows = jnp.concatenate([rows] + [swap(rows, axes) for axes in CHIPS], 0)
     kernel, part = call(
@@ -321,7 +336,7 @@
     message, image = call(
         first_image, [shape(NC * 9, 1, OWN), shape(8, OWN)], "first_image", parts + [rows]
     )
-    image_cols = lax.all_to_all(message, COLG, 0, 0, tiled=True)
+    image_cols = column_exchange(message)
     kernel = pltpu.with_memory_space_constraint(kernel, VMEM)
     part, scalars = call(
         second_product,
@@ -341,7 +356,7 @@
         parts + [rows, scalars],
         scratch=[pltpu.VMEM((3, NR, 8, OWN), f32), pltpu.VMEM((4, NR * 8 + 24, OWN), f32)],
     )
-    sums = lax.all_to_all(message, COLG, 0, 0)
+    sums = column_exchange(message)
     residual, direction = call(
         finish, [shape(8, OWN), shape(8, OWN)], "finish", [keep, sums]
     )

time: 86.2 us -> 81.1 us (0.941)
  waiting for transfers between devices: 16.2 us -> 13.3 us
  blocking collectives: 29.1 us -> 26.9 us
    all_to_all x2, blocking collectives: 29.1 us -> 26.9 us  [column_exchange(): lax.all_to_all(x, AXES, 0, 0, axis_index_groups=column_groups(), tiled=True)]
    all_to_all x1, waiting for transfers between devices: 1.97 us -> 0.01 us  [column_exchange(): lax.all_to_all(x, AXES, 0, 0, axis_index_groups=column_groups(), tiled=True)]
    ppermute x12, waiting for transfers between devices: 14.3 us -> 13.3 us  [swap(): return lax.ppermute(x, axes, [(i, size - 1 - i) for i in range(size)])]
  transfers between devices with their start and end apart: 13 -> 13, of which waited for: 12 -> 11; matrix products, arithmetic and copies ran while one was open for 0% -> 0% of each run, Pallas kernels for 0% -> 0%
where the time goes in v5:
time: 81.1 us; the launch traced here: 80.8 us
  blocking collectives  26.9 us (33%)
  starting transfers between devices  26.3 us (32%)
  Pallas kernels  13.5 us (17%)
  waiting for transfers between devices  13.3 us (16%)
    all_to_all x2, blocking collectives, column_exchange(): lax.all_to_all(x, AXES, 0, 0, axis_index_groups=column_groups(), tiled=True)  26.9 us
    ppermute x12, starting transfers between devices, swap(): return lax.ppermute(x, axes, [(i, size - 1 - i) for i in range(size)])  14 us
    ppermute x12, waiting for transfers between devices, swap(): return lax.ppermute(x, axes, [(i, size - 1 - i) for i in range(size)])  13.3 us
    all_to_all x1, starting transfers between devices, column_exchange(): lax.all_to_all(x, AXES, 0, 0, axis_index_groups=column_groups(), tiled=True)  12.3 us
    pallas_call x6, Pallas kernels, call(): pl.pallas_call(kernel, in_specs=[pl.BlockSpec(memory_space=VMEM) for _ in...  12 us
  transfers between devices with their start and end apart: 13, of which 11 were waited for; matrix products, arithmetic and copies ran while one was open for 0% of the time, Pallas kernels for 0%

profile of v5, /device:TPU:8, one launch (start us, length us, event | category | flops | bytes accessed | tf_op | source)
XLA Modules:
  0.0 80.8 jit_solution(3892023512510344610)
XLA Ops:
  0.6 1.5 %pack.1 = (f32[1,16,128]{2,1,0:T(8,128)S(1)}, f32[32,16,128]{2,1,0:T(8,128)}) custom-call(f32[8,128]{1,0:T(8,128)} %points_hbm.1, f32[8]{0:T(128)} %lengthscale_hbm.1, f32[8,128]{1,0:T(8,128)} %targets_hbm.1), custom_call_target="tpu_custom_call" | custom-call | tf_op jit(solution)/shard_map/pack/pallas_call | solution.py:310
  2.2 12.3 %all-to-all-start = ((f32[32,16,128]{2,1,0:T(8,128)}), f32[32,16,128]{2,1,0:T(8,128)S(1)}, u32[]{:S(2)}, u32[]{:S(2)}) async-start(f32[32,16,128]{2,1,0:T(8,128)} %get-tuple-element.12), calls=%async_computation | async-start | bytes 524288 | tf_op jit(solution)/shard_map/all_to_all | solution.py:298
  14.5 0.1 collective-permute-start
  14.6 1.1 %collective-permute-done = f32[1,16,128]{2,1,0:T(8,128)S(1)} collective-permute-done((f32[1,16,128]{2,1,0:T(8,128)S(1)}, f32[1,16,128]{2,1,0:T(8,128)S(1)}, u32[]{:S(2)}, u32[]{:S(2)}) %collective-permute-start) | collective-permute-done | bytes 8224 | tf_op jit(solution)/shard_map/ppermute | solution.py:303
  15.7 3.0 %collective-permute-start.1 = (f32[2,16,128]{2,1,0:T(8,128)S(1)}, f32[2,16,128]{2,1,0:T(8,128)S(1)}, u32[]{:S(2)}, u32[]{:S(2)}) collective-permute-start(f32[2,16,128]{2,1,0:T(8,128)S(1)} %get-tuple-element.26), channel_id=1, source_target_pairs={{0,2},{2,0},{1,3},{3,1},{4,6},{6,4},{5,7},{7,5},{8,10},{10,8},{9,1... | collective-permute-start | bytes 49160 | tf_op jit(solution)/shard_map/ppermute | solution.py:303
  18.8 1.1 %collective-permute-start.3 = (f32[2,16,128]{2,1,0:T(8,128)S(1)}, f32[2,16,128]{2,1,0:T(8,128)S(1)}, u32[]{:S(2)}, u32[]{:S(2)}) collective-permute-start(f32[2,16,128]{2,1,0:T(8,128)S(1)} %get-tuple-element.26), channel_id=1, source_target_pairs={{0,18},{2,16},{16,2},{18,0},{1,19},{3,17},{17,3},{19,1},{4,22},{6,... | collective-permute-start | bytes 49160 | tf_op jit(solution)/shard_map/ppermute | solution.py:303
  19.9 0.0 collective-permute-start.2
  19.9 1.1 %collective-permute-done.1 = f32[2,16,128]{2,1,0:T(8,128)S(1)} collective-permute-done((f32[2,16,128]{2,1,0:T(8,128)S(1)}, f32[2,16,128]{2,1,0:T(8,128)S(1)}, u32[]{:S(2)}, u32[]{:S(2)}) %collective-permute-start.1) | collective-permute-done | bytes 16416 | tf_op jit(solution)/shard_map/ppermute | solution.py:303
  21.0 2.7 %collective-permute-done.2 = f32[2,16,128]{2,1,0:T(8,128)S(1)} collective-permute-done((f32[2,16,128]{2,1,0:T(8,128)S(1)}, f32[2,16,128]{2,1,0:T(8,128)S(1)}, u32[]{:S(2)}, u32[]{:S(2)}) %collective-permute-start.2) | collective-permute-done | bytes 16416 | tf_op jit(solution)/shard_map/ppermute | solution.py:303
  23.7 0.1 collective-permute-done.3
  23.7 0.0 all-to-all-done.cols_ref
  23.7 7.4 %first_product.1 = (f32[4096,1024]{1,0:T(8,128)S(1)}, f32[2,4,16,128]{3,2,1,0:T(8,128)S(1)}) custom-call(f32[8,16,128]{2,1,0:T(8,128)S(1)} %constant_dynamic-update-slice_fusion.2.rows_ref, f32[32,16,128]{2,1,0:T(8,128)S(1)} %all-to-all-done.cols_ref), custom_call_target="tpu_custom_call" | custom-call | tf_op jit(solution)/shard_map/first_product/pallas_call | solution.py:270
  31.1 0.0 collective-permute-start.4
  31.2 1.2 %collective-permute-done.4 = f32[4,16,128]{2,1,0:T(8,128)S(1)} collective-permute-done((f32[4,16,128]{2,1,0:T(8,128)S(1)}, f32[4,16,128]{2,1,0:T(8,128)S(1)}, u32[]{:S(2)}, u32[]{:S(2)}) %collective-permute-start.4) | collective-permute-done | bytes 32800 | tf_op jit(solution)/shard_map/ppermute | solution.py:303
  32.4 2.1 %collective-permute-start.7 = (f32[1,16,128]{2,1,0:T(8,128)S(1)}, f32[1,16,128]{2,1,0:T(8,128)S(1)}, u32[]{:S(2)}, u32[]{:S(2)}) collective-permute-start(f32[1,16,128]{2,1,0:T(8,128)S(1)} %get-tuple-element.22), channel_id=1, source_target_pairs={{0,18},{2,16},{16,2},{18,0},{1,19},{3,17},{17,3},{19,1},{4,22},{6,... | collective-permute-start | bytes 24584 | tf_op jit(solution)/shard_map/ppermute | solution.py:303
  34.5 0.0 collective-permute-start.6
  34.5 2.7 %collective-permute-start.5 = (f32[1,16,128]{2,1,0:T(8,128)S(1)}, f32[1,16,128]{2,1,0:T(8,128)S(1)}, u32[]{:S(2)}, u32[]{:S(2)}) collective-permute-start(f32[1,16,128]{2,1,0:T(8,128)S(1)} %get-tuple-element.24), channel_id=1, source_target_pairs={{0,2},{2,0},{1,3},{3,1},{4,6},{6,4},{5,7},{7,5},{8,10},{10,8},{9,1... | collective-permute-start | bytes 24584 | tf_op jit(solution)/shard_map/ppermute | solution.py:303
  37.2 0.2 collective-permute-done.7.both_ref
  37.3 0.8 %collective-permute-done.6.xl_ref = f32[1,16,128]{2,1,0:T(8,128)S(1)} collective-permute-done((f32[1,16,128]{2,1,0:T(8,128)S(1)}, f32[1,16,128]{2,1,0:T(8,128)S(1)}, u32[]{:S(2)}, u32[]{:S(2)}) %collective-permute-start.6) | collective-permute-done | bytes 8224 | tf_op jit(solution)/shard_map/ppermute | solution.py:303
  38.2 1.5 %collective-permute-done.5.xh_ref = f32[1,16,128]{2,1,0:T(8,128)S(1)} collective-permute-done((f32[1,16,128]{2,1,0:T(8,128)S(1)}, f32[1,16,128]{2,1,0:T(8,128)S(1)}, u32[]{:S(2)}, u32[]{:S(2)}) %collective-permute-start.5) | collective-permute-done | bytes 8224 | tf_op jit(solution)/shard_map/ppermute | solution.py:303
  39.7 0.2 first_image.1
  39.9 14.2 %all_to_all.15.image_cols_ref = f32[288,1,128]{2,1,0:T(1,128)S(1)} all-to-all(f32[288,1,128]{2,1,0:T(1,128)S(1)} %get-tuple-element.15), channel_id=1, replica_groups={{136,140,128,132,164,160,172,168,200,204,192,196,228,224,236,232,8,12,0..., dimensions={0} | all-to-all | bytes 294912 | tf_op jit(solution)/shard_map/all_to_all | solution.py:298
  54.1 3.2 %second_product.1 = (f32[80,128]{1,0:T(8,128)S(1)}, f32[8,128]{1,0:T(8,128)S(1)}) custom-call(f32[32,16,128]{2,1,0:T(8,128)S(1)} %all-to-all-done.cols_ref, f32[288,1,128]{2,1,0:T(1,128)S(1)} %all_to_all.15.image_cols_ref, f32[8,128]{1,0:T(8,128)S(1)} %get-tuple-element.16.image_ref, f32[4096,1024]{1,0:T(8,128)S(1)} %get-tuple-element.17.kernel_ref), custom_call_target="tpu_custom_call" | custom-call | tf_op jit(solution)/shard_map/second_product/pallas_call | solution.py:270
  57.3 0.1 collective-permute-start.8
  57.4 1.2 %collective-permute-done.8.theirs_ref = f32[80,128]{1,0:T(8,128)S(1)} collective-permute-done((f32[80,128]{1,0:T(8,128)S(1)}, f32[80,128]{1,0:T(8,128)S(1)}, u32[]{:S(2)}, u32[]{:S(2)}) %collective-permute-start.8) | collective-permute-done | bytes 40992 | tf_op jit(solution)/shard_map/ppermute | solution.py:303
  58.6 1.3 %collective-permute-start.11 = (f32[88,128]{1,0:T(8,128)S(1)}, f32[88,128]{1,0:T(8,128)S(1)}, u32[]{:S(2)}, u32[]{:S(2)}) collective-permute-start(f32[88,128]{1,0:T(8,128)S(1)} %core_sum.1.own_part), channel_id=1, source_target_pairs={{0,18},{2,16},{16,2},{18,0},{1,19},{3,17},{17,3},{19,1},{4,22},{6,... | collective-permute-start | bytes 135176 | tf_op jit(solution)/shard_map/ppermute | solution.py:303
  59.9 1.4 %collective-permute-start.10 = (f32[88,128]{1,0:T(8,128)S(1)}, f32[88,128]{1,0:T(8,128)S(1)}, u32[]{:S(2)}, u32[]{:S(2)}) collective-permute-start(f32[88,128]{1,0:T(8,128)S(1)} %core_sum.1.own_part), channel_id=1, source_target_pairs={{0,16},{16,0},{1,17},{17,1},{2,18},{18,2},{3,19},{19,3},{4,20},{20... | collective-permute-start | bytes 135176 | tf_op jit(solution)/shard_map/ppermute | solution.py:303
  61.3 2.1 %collective-permute-start.9 = (f32[88,128]{1,0:T(8,128)S(1)}, f32[88,128]{1,0:T(8,128)S(1)}, u32[]{:S(2)}, u32[]{:S(2)}) collective-permute-start(f32[88,128]{1,0:T(8,128)S(1)} %core_sum.1.own_part), channel_id=1, source_target_pairs={{0,2},{2,0},{1,3},{3,1},{4,6},{6,4},{5,7},{7,5},{8,10},{10,8},{9,1... | collective-permute-start | bytes 135176 | tf_op jit(solution)/shard_map/ppermute | solution.py:303
  63.4 0.6 collective-permute-done.11.both_part
  63.9 0.0 collective-permute-done.10.xl_part
  64.0 2.9 %collective-permute-done.9.xh_part = f32[88,128]{1,0:T(8,128)S(1)} collective-permute-done((f32[88,128]{1,0:T(8,128)S(1)}, f32[88,128]{1,0:T(8,128)S(1)}, u32[]{:S(2)}, u32[]{:S(2)}) %collective-permute-start.9) | collective-permute-done | bytes 45088 | tf_op jit(solution)/shard_map/ppermute | solution.py:303
  66.8 0.3 second_image.1
  67.1 12.7 %all_to_all.16.sums_ref = f32[32,1,128]{2,1,0:T(1,128)S(1)} all-to-all(f32[32,1,128]{2,1,0:T(1,128)S(1)} %get-tuple-element.21), channel_id=1, replica_groups={{136,140,128,132,164,160,172,168,200,204,192,196,228,224,236,232,8,12,0..., dimensions={0} | all-to-all | bytes 32768 | tf_op jit(solution)/shard_map/all_to_all | solution.py:298
  79.8 0.9 %finish.1 = (f32[8,128]{1,0:T(8,128)}, f32[8,128]{1,0:T(8,128)}) custom-call(f32[4,8,128]{2,1,0:T(8,128)S(1)} %get-tuple-element.20.own_ref, f32[32,1,128]{2,1,0:T(1,128)S(1)} %all_to_all.16.sums_ref), custom_call_target="tpu_custom_call" | custom-call | tf_op jit(solution)/shard_map/finish/pallas_call | solution.py:270
  (9 shorter events, 0.0 us)
Async XLA Ops:
  2.2 21.5 %all-to-all-start = ((f32[32,16,128]{2,1,0:T(8,128)}), f32[32,16,128]{2,1,0:T(8,128)S(1)}, u32[]{:S(2)}, u32[]{:S(2)}) async-start(f32[32,16,128]{2,1,0:T(8,128)} %get-tuple-element.12), calls=%async_computation | async-start | bytes 524288 | tf_op jit(solution)/shard_map/all_to_all | solution.py:298
  14.5 1.3 %collective-permute-start = (f32[1,16,128]{2,1,0:T(8,128)S(1)}, f32[1,16,128]{2,1,0:T(8,128)S(1)}, u32[]{:S(2)}, u32[]{:S(2)}) collective-permute-start(f32[1,16,128]{2,1,0:T(8,128)S(1)} %get-tuple-element.13), channel_id=1, source_target_pairs={{0,1},{1,0},{2,3},{3,2},{4,5},{5,4},{6,7},{7,6},{8,9},{9,8},{10,11... | collective-permute-start | bytes 24584 | tf_op jit(solution)/shard_map/ppermute | solution.py:303
  15.7 5.2 %collective-permute-start.1 = (f32[2,16,128]{2,1,0:T(8,128)S(1)}, f32[2,16,128]{2,1,0:T(8,128)S(1)}, u32[]{:S(2)}, u32[]{:S(2)}) collective-permute-start(f32[2,16,128]{2,1,0:T(8,128)S(1)} %get-tuple-element.26), channel_id=1, source_target_pairs={{0,2},{2,0},{1,3},{3,1},{4,6},{6,4},{5,7},{7,5},{8,10},{10,8},{9,1... | collective-permute-start | bytes 49160 | tf_op jit(solution)/shard_map/ppermute | solution.py:303
  18.8 4.9 %collective-permute-start.3 = (f32[2,16,128]{2,1,0:T(8,128)S(1)}, f32[2,16,128]{2,1,0:T(8,128)S(1)}, u32[]{:S(2)}, u32[]{:S(2)}) collective-permute-start(f32[2,16,128]{2,1,0:T(8,128)S(1)} %get-tuple-element.26), channel_id=1, source_target_pairs={{0,18},{2,16},{16,2},{18,0},{1,19},{3,17},{17,3},{19,1},{4,22},{6,... | collective-permute-start | bytes 49160 | tf_op jit(solution)/shard_map/ppermute | solution.py:303
  19.9 3.7 %collective-permute-start.2 = (f32[2,16,128]{2,1,0:T(8,128)S(1)}, f32[2,16,128]{2,1,0:T(8,128)S(1)}, u32[]{:S(2)}, u32[]{:S(2)}) collective-permute-start(f32[2,16,128]{2,1,0:T(8,128)S(1)} %get-tuple-element.26), channel_id=1, source_target_pairs={{0,16},{16,0},{1,17},{17,1},{2,18},{18,2},{3,19},{19,3},{4,20},{20... | collective-permute-start | bytes 49160 | tf_op jit(solution)/shard_map/ppermute | solution.py:303
  31.1 1.2 %collective-permute-start.4 = (f32[4,16,128]{2,1,0:T(8,128)S(1)}, f32[4,16,128]{2,1,0:T(8,128)S(1)}, u32[]{:S(2)}, u32[]{:S(2)}) collective-permute-start(f32[4,16,128]{2,1,0:T(8,128)S(1)} %slice_bitcast_fusion), channel_id=1, source_target_pairs={{0,1},{1,0},{2,3},{3,2},{4,5},{5,4},{6,7},{7,6},{8,9},{9,8},{10,11... | collective-permute-start | bytes 98312 | tf_op jit(solution)/shard_map/ppermute | solution.py:303
  32.4 4.9 %collective-permute-start.7 = (f32[1,16,128]{2,1,0:T(8,128)S(1)}, f32[1,16,128]{2,1,0:T(8,128)S(1)}, u32[]{:S(2)}, u32[]{:S(2)}) collective-permute-start(f32[1,16,128]{2,1,0:T(8,128)S(1)} %get-tuple-element.22), channel_id=1, source_target_pairs={{0,18},{2,16},{16,2},{18,0},{1,19},{3,17},{17,3},{19,1},{4,22},{6,... | collective-permute-start | bytes 24584 | tf_op jit(solution)/shard_map/ppermute | solution.py:303
  34.5 3.7 %collective-permute-start.6 = (f32[1,16,128]{2,1,0:T(8,128)S(1)}, f32[1,16,128]{2,1,0:T(8,128)S(1)}, u32[]{:S(2)}, u32[]{:S(2)}) collective-permute-start(f32[1,16,128]{2,1,0:T(8,128)S(1)} %get-tuple-element.23), channel_id=1, source_target_pairs={{0,16},{16,0},{1,17},{17,1},{2,18},{18,2},{3,19},{19,3},{4,20},{20... | collective-permute-start | bytes 24584 | tf_op jit(solution)/shard_map/ppermute | solution.py:303
  34.5 5.2 %collective-permute-start.5 = (f32[1,16,128]{2,1,0:T(8,128)S(1)}, f32[1,16,128]{2,1,0:T(8,128)S(1)}, u32[]{:S(2)}, u32[]{:S(2)}) collective-permute-start(f32[1,16,128]{2,1,0:T(8,128)S(1)} %get-tuple-element.24), channel_id=1, source_target_pairs={{0,2},{2,0},{1,3},{3,1},{4,6},{6,4},{5,7},{7,5},{8,10},{10,8},{9,1... | collective-permute-start | bytes 24584 | tf_op jit(solution)/shard_map/ppermute | solution.py:303
  57.3 1.3 %collective-permute-start.8 = (f32[80,128]{1,0:T(8,128)S(1)}, f32[80,128]{1,0:T(8,128)S(1)}, u32[]{:S(2)}, u32[]{:S(2)}) collective-permute-start(f32[80,128]{1,0:T(8,128)S(1)} %get-tuple-element.18.ours_ref), channel_id=1, source_target_pairs={{0,1},{1,0},{2,3},{3,2},{4,5},{5,4},{6,7},{7,6},{8,9},{9,8},{10,11... | collective-permute-start | bytes 122888 | tf_op jit(solution)/shard_map/ppermute | solution.py:303
  58.6 5.3 %collective-permute-start.11 = (f32[88,128]{1,0:T(8,128)S(1)}, f32[88,128]{1,0:T(8,128)S(1)}, u32[]{:S(2)}, u32[]{:S(2)}) collective-permute-start(f32[88,128]{1,0:T(8,128)S(1)} %core_sum.1.own_part), channel_id=1, source_target_pairs={{0,18},{2,16},{16,2},{18,0},{1,19},{3,17},{17,3},{19,1},{4,22},{6,... | collective-permute-start | bytes 135176 | tf_op jit(solution)/shard_map/ppermute | solution.py:303
  59.9 4.0 %collective-permute-start.10 = (f32[88,128]{1,0:T(8,128)S(1)}, f32[88,128]{1,0:T(8,128)S(1)}, u32[]{:S(2)}, u32[]{:S(2)}) collective-permute-start(f32[88,128]{1,0:T(8,128)S(1)} %core_sum.1.own_part), channel_id=1, source_target_pairs={{0,16},{16,0},{1,17},{17,1},{2,18},{18,2},{3,19},{19,3},{4,20},{20... | collective-permute-start | bytes 135176 | tf_op jit(solution)/shard_map/ppermute | solution.py:303
  61.3 5.6 %collective-permute-start.9 = (f32[88,128]{1,0:T(8,128)S(1)}, f32[88,128]{1,0:T(8,128)S(1)}, u32[]{:S(2)}, u32[]{:S(2)}) collective-permute-start(f32[88,128]{1,0:T(8,128)S(1)} %core_sum.1.own_part), channel_id=1, source_target_pairs={{0,2},{2,0},{1,3},{3,1},{4,6},{6,4},{5,7},{7,5},{8,10},{10,8},{9,1... | collective-permute-start | bytes 135176 | tf_op jit(solution)/shard_map/ppermute | solution.py:303

commit v6 on v5

--- a/solution.py
+++ b/solution.py
@@ -17,6 +17,7 @@
 NR, NC = 8, 32
 OWN = 128
 NI, NJ = NR * OWN, NC * OWN
+NEAR = 2 * OWN
 noise_level = 0.5
 
 LOG2E = math.log2(math.e)
@@ -104,30 +105,49 @@
     return lax.axis_index("xl") * 4 + lax.axis_index("xh") * 2 + lax.axis_index("core")
 
 
-def first_product(rows_ref, cols_ref, kernel_ref, out_ref):
-    left = features(lanes(rows_ref, 0, NR), True).astype(bf16)
-    right = features(lanes(cols_ref, 0, NC), False).T.astype(bf16)
-    values = stacked(lanes(cols_ref, 8, NC))
-    form = jnp.zeros((8, OWN), f32)
-    for i in range(0, NI, TI):
+def first_rows(points, right, values, kernel_ref):
+    left = features(points, True).astype(bf16)
+    out = []
+    for i in range(0, points.shape[1], TI):
         acc = jnp.zeros((24, TI), f32)
-        lag = TJ
         for j in range(0, NJ, TJ):
             square = jnp.dot(right[j : j + TJ], left[:, i : i + TI], preferred_element_type=f32)
-            tile = matern(square)
-            kernel_ref[j : j + TJ, i : i + TI] = tile
-            if j >= lag:
-                acc = acc + product(values[:, j - lag : j - lag + TJ], kernel_ref[j - lag : j - lag + TJ, i : i + TI])
-        acc = acc + product(values[:, NJ - lag :], kernel_ref[NJ - lag :, i : i + TI])
-        acc = (acc[0:8] + acc[8:16] + acc[16:24]) * FACTOR
-        for k in range(TI // OWN):
-            block = i // OWN + k
-            part = acc[:, k * OWN : (k + 1) * OWN]
-            out_ref[block % 2, block // 2, 0:8, :] = part
-            form = form + part * rows_ref[block, 8:16, :]
+            kernel_ref[j : j + TJ, i : i + TI] = matern(square)
+            if j > 0:
+                last = kernel_ref[j - TJ : j, i : i + TI]
+                acc = acc + product(values[:, j - TJ : j], last)
+        acc = acc + product(values[:, NJ - TJ :], kernel_ref[NJ - TJ :, i : i + TI])
+        out.append((acc[0:8] + acc[8:16] + acc[16:24]) * FACTOR)
+    return jnp.concatenate(out, 1)
+
+
+def near_product(near_ref, cols_ref, kernel_ref, right_ref, part_ref, form_ref):
+    right = features(lanes(cols_ref, 0, NC), False).T.astype(bf16)
+    right_ref[...] = right
+    values = stacked(lanes(cols_ref, 8, NC))
+    part = first_rows(lanes(near_ref, 0, 2), right, values, kernel_ref)
+    part_ref[0] = part[:, :OWN]
+    part_ref[1] = part[:, OWN:]
+    form_ref[...] = part[:, :OWN] * near_ref[0, 8:16, :] + part[:, OWN:] * near_ref[1, 8:16, :]
+
+
+def far_product(xh_ref, xl_ref, both_ref, cols_ref, right_ref, near_part_ref, form_ref, kernel_ref, out_ref):
+    refs = (xh_ref, xl_ref, both_ref)
+    values = stacked(lanes(cols_ref, 8, NC))
+    points = jnp.concatenate([lanes(ref, 0, 2) for ref in refs], 1)
+    part = first_rows(points, right_ref, values, kernel_ref)
+    form = form_ref[...]
+    for core in range(2):
+        out_ref[core, 0, 0:8, :] = near_part_ref[core]
+        for chip, ref in enumerate(refs):
+            first = (chip * 2 + core) * OWN
+            block = part[:, first : first + OWN]
+            out_ref[core, chip + 1, 0:8, :] = block
+            form = form + block * ref[core, 8:16, :]
     form = jnp.broadcast_to(total(form), (8, OWN))
-    for block in range(NR):
-        out_ref[block % 2, block // 2, 8:16, :] = form
+    for core in range(2):
+        for chip in range(4):
+            out_ref[core, chip, 8:16, :] = form
 
 
 def at_lanes(columns):
@@ -154,7 +174,7 @@
     image_ref[...] = image
 
 
-def second_product(cols_ref, image_cols_ref, image_ref, kernel_ref, out_ref, scalar_ref):
+def second_product(cols_ref, image_cols_ref, image_ref, near_ref, far_ref, out_ref, scalar_ref):
     sums = image_cols_ref[8]
     for k in range(1, NC):
         sums = sums + image_cols_ref[9 * k + 8]
@@ -167,8 +187,9 @@
     mine = my_row_block()
     for i in range(0, NI, TI):
         acc = jnp.zeros((24, TI), f32)
+        kernel_ref, first = (near_ref, i) if i < NEAR else (far_ref, i - NEAR)
         for j in range(0, NJ, TJ):
-            acc = acc + product(values[:, j : j + TJ], kernel_ref[j : j + TJ, i : i + TI])
+            acc = acc + product(values[:, j : j + TJ], kernel_ref[j : j + TJ, first : first + TI])
         acc = (acc[0:8] + acc[8:16] + acc[16:24]) * FACTOR
         for k in range(TI // OWN):
             row = pl.multiple_of((mine ^ (i // OWN + k)) * 8, 8)
@@ -266,7 +287,7 @@
     direction_ref[...] = residual + (norm_next / norm) * own_ref[1]
 
 
-def call(kernel, outs, name, args, scratch=(), vmem=4 << 20):
+def call(kernel, outs, name, args, scratch=(), vmem=4 << 20, cost=None):
     return pl.pallas_call(
         kernel,
         in_specs=[
@@ -276,6 +297,7 @@
         out_shape=outs,
         scratch_shapes=scratch,
         compiler_params=pltpu.CompilerParams(vmem_limit_bytes=vmem),
+        cost_estimate=cost,
         name=name,
     )(*args)
 
@@ -322,27 +344,37 @@
         name="pack",
     )(*[pltpu.with_memory_space_constraint(a, pltpu.HBM) for a in (points, lengthscale, targets)])
     cols = column_exchange(copies)
-    rows = jnp.concatenate([own, swap(own, ("core",))], 0)
-    rows = jnp.concatenate([rows] + [swap(rows, axes) for axes in CHIPS], 0)
-    kernel, part = call(
-        first_product,
-        [VMEM((NJ, NI), f32), shape(2, 4, 16, OWN)],
-        "first_product",
-        [rows, cols],
-        vmem=24 << 20,
-    )
+    near = jnp.concatenate([own, swap(own, ("core",))], 0)
+    far = [swap(near, axes) for axes in CHIPS]
+    near_kernel, right, near_part, form = call(
+        near_product,
+        [VMEM((NJ, NEAR), f32), jax.ShapeDtypeStruct((NJ, 64), bf16), shape(2, 8, OWN), shape(8, OWN)],
+        "near_product",
+        [near, cols],
+        vmem=16 << 20,
+        cost=pl.CostEstimate(flops=2 * NJ * NEAR * 128, bytes_accessed=4 * NJ * NEAR, transcendentals=2 * NJ * NEAR),
+    )
+    far_kernel, part = call(
+        far_product,
+        [VMEM((NJ, NI - NEAR), f32), shape(2, 4, 16, OWN)],
+        "far_product",
+        far + [cols, right, near_part, form],
+        vmem=20 << 20,
+    )
+    rows = jnp.concatenate([near] + far, 0)
     part = part[0] + swap(part[1], ("core",))
     parts = [part[0:1]] + [swap(part[k : k + 1], axes) for k, axes in enumerate(CHIPS, 1)]
     message, image = call(
         first_image, [shape(NC * 9, 1, OWN), shape(8, OWN)], "first_image", parts + [rows]
     )
     image_cols = column_exchange(message)
-    kernel = pltpu.with_memory_space_constraint(kernel, VMEM)
+    near_kernel = pltpu.with_memory_space_constraint(near_kernel, VMEM)
+    far_kernel = pltpu.with_memory_space_constraint(far_kernel, VMEM)
     part, scalars = call(
         second_product,
         [shape(NR * 8 + 16, OWN), shape(8, OWN)],
         "second_product",
-        [cols, image_cols, image, kernel],
+        [cols, image_cols, image, near_kernel, far_kernel],
         vmem=8 << 20,
     )
     part = call(

time: 81.1 us -> 79.5 us (0.980)
  waiting for transfers between devices: 13.3 us -> 11.6 us
    ppermute x12, waiting for transfers between devices: 13.3 us -> 10.9 us  [swap(): return lax.ppermute(x, axes, [(i, size - 1 - i) for i in range(size)])]
    pallas_call x6 -> x7, Pallas kernels: 12 us -> 12.6 us  [call(): pl.pallas_call(kernel, in_specs=[pl.BlockSpec(memory_space=VMEM) for _ in...]
  transfers between devices with their start and end apart: 13 -> 13, of which waited for: 11 -> 10; matrix products, arithmetic and copies ran while one was open for 0% -> 0% of each run, Pallas kernels for 0% -> 3%
where the time goes in v6:
time: 79.5 us; the launch traced here: 79.2 us
  blocking collectives  26.4 us (33%)
  starting transfers between devices  26.3 us (33%)
  Pallas kernels  14.2 us (18%)
  waiting for transfers between devices  11.6 us (15%)
    all_to_all x2, blocking collectives, column_exchange(): lax.all_to_all(x, AXES, 0, 0, axis_index_groups=column_groups(), tiled=True)  26.4 us
    ppermute x12, starting transfers between devices, swap(): return lax.ppermute(x, axes, [(i, size - 1 - i) for i in range(size)])  14 us
    pallas_call x7, Pallas kernels, call(): pl.pallas_call(kernel, in_specs=[pl.BlockSpec(memory_space=VMEM) for _ in...  12.6 us
    all_to_all x1, starting transfers between devices, column_exchange(): lax.all_to_all(x, AXES, 0, 0, axis_index_groups=column_groups(), tiled=True)  12.3 us
    ppermute x12, waiting for transfers between devices, swap(): return lax.ppermute(x, axes, [(i, size - 1 - i) for i in range(size)])  10.9 us
  transfers between devices with their start and end apart: 13, of which 10 were waited for; matrix products, arithmetic and copies ran while one was open for 0% of the time, Pallas kernels for 3%

profile of v6, /device:TPU:8, one launch (start us, length us, event | category | flops | bytes accessed | tf_op | source)
XLA Modules:
  0.0 79.2 jit_solution(14869129638570974399)
XLA Ops:
  0.6 1.5 %pack.1 = (f32[1,16,128]{2,1,0:T(8,128)S(1)}, f32[32,16,128]{2,1,0:T(8,128)}) custom-call(f32[8,128]{1,0:T(8,128)} %points_hbm.1, f32[8]{0:T(128)} %lengthscale_hbm.1, f32[8,128]{1,0:T(8,128)} %targets_hbm.1), custom_call_target="tpu_custom_call" | custom-call | tf_op jit(solution)/shard_map/pack/pallas_call | solution.py:332
  2.2 12.3 %all-to-all-start = ((f32[32,16,128]{2,1,0:T(8,128)}), f32[32,16,128]{2,1,0:T(8,128)S(1)}, u32[]{:S(2)}, u32[]{:S(2)}) async-start(f32[32,16,128]{2,1,0:T(8,128)} %get-tuple-element.16), calls=%async_computation | async-start | bytes 524288 | tf_op jit(solution)/shard_map/all_to_all | solution.py:320
  14.5 0.1 collective-permute-start
  14.6 1.1 %collective-permute-done = f32[1,16,128]{2,1,0:T(8,128)S(1)} collective-permute-done((f32[1,16,128]{2,1,0:T(8,128)S(1)}, f32[1,16,128]{2,1,0:T(8,128)S(1)}, u32[]{:S(2)}, u32[]{:S(2)}) %collective-permute-start) | collective-permute-done | bytes 8224 | tf_op jit(solution)/shard_map/ppermute | solution.py:325
  15.8 3.0 %collective-permute-start.1 = (f32[2,16,128]{2,1,0:T(8,128)S(1)}, f32[2,16,128]{2,1,0:T(8,128)S(1)}, u32[]{:S(2)}, u32[]{:S(2)}) collective-permute-start(f32[2,16,128]{2,1,0:T(8,128)S(1)} %get-tuple-element.35.near_ref), channel_id=1, source_target_pairs={{0,2},{2,0},{1,3},{3,1},{4,6},{6,4},{5,7},{7,5},{8,10},{10,8},{9,1... | collective-permute-start | bytes 49160 | tf_op jit(solution)/shard_map/ppermute | solution.py:325
  18.8 1.1 %collective-permute-start.3 = (f32[2,16,128]{2,1,0:T(8,128)S(1)}, f32[2,16,128]{2,1,0:T(8,128)S(1)}, u32[]{:S(2)}, u32[]{:S(2)}) collective-permute-start(f32[2,16,128]{2,1,0:T(8,128)S(1)} %get-tuple-element.35.near_ref), channel_id=1, source_target_pairs={{0,18},{2,16},{16,2},{18,0},{1,19},{3,17},{17,3},{19,1},{4,22},{6,... | collective-permute-start | bytes 49160 | tf_op jit(solution)/shard_map/ppermute | solution.py:325
  19.9 0.0 collective-permute-start.2
  19.9 1.1 %collective-permute-done.1.xh_ref = f32[2,16,128]{2,1,0:T(8,128)S(1)} collective-permute-done((f32[2,16,128]{2,1,0:T(8,128)S(1)}, f32[2,16,128]{2,1,0:T(8,128)S(1)}, u32[]{:S(2)}, u32[]{:S(2)}) %collective-permute-start.1) | collective-permute-done | bytes 16416 | tf_op jit(solution)/shard_map/ppermute | solution.py:325
  21.0 0.7 all-to-all-done.cols_ref
  21.7 2.2 %near_product.1 = (f32[4096,256]{1,0:T(8,128)S(1)}, bf16[4096,64]{1,0:T(8,128)(2,1)S(1)}, f32[2,8,128]{2,1,0:T(8,128)S(1)}, f32[8,128]{1,0:T(8,128)S(1)}) custom-call(f32[2,16,128]{2,1,0:T(8,128)S(1)} %get-tuple-element.35.near_ref, f32[32,16,128]{2,1,0:T(8,128)S(1)} %all-to-all-done.cols_ref), custom_call_target="tpu_custom_call" | custom-call | flops 268435456 | bytes 4194304 | tf_op jit(solution)/shard_map/near_product/pallas_call | solution.py:291
  23.9 0.0 collective-permute-done.3.both_ref
  23.9 0.0 collective-permute-done.2.xl_ref
  23.9 5.6 %far_product.1 = (f32[4096,768]{1,0:T(8,128)S(1)}, f32[2,4,16,128]{3,2,1,0:T(8,128)S(1)}) custom-call(f32[2,16,128]{2,1,0:T(8,128)S(1)} %collective-permute-done.1.xh_ref, f32[2,16,128]{2,1,0:T(8,128)S(1)} %collective-permute-done.2.xl_ref, f32[2,16,128]{2,1,0:T(8,128)S(1)} %collective-permute-done.3.both_ref, f32[32,16,128]{2,1,0:T(8,128)S(1)} %all-to-all-done.cols_ref, ...), custom_call_target="tpu_custom_call" | custom-call | tf_op jit(solution)/shard_map/far_product/pallas_call | solution.py:291
  29.5 0.0 collective-permute-start.4
  29.6 1.2 %collective-permute-done.4 = f32[4,16,128]{2,1,0:T(8,128)S(1)} collective-permute-done((f32[4,16,128]{2,1,0:T(8,128)S(1)}, f32[4,16,128]{2,1,0:T(8,128)S(1)}, u32[]{:S(2)}, u32[]{:S(2)}) %collective-permute-start.4) | collective-permute-done | bytes 32800 | tf_op jit(solution)/shard_map/ppermute | solution.py:325
  30.8 2.8 %collective-permute-start.7 = (f32[1,16,128]{2,1,0:T(8,128)S(1)}, f32[1,16,128]{2,1,0:T(8,128)S(1)}, u32[]{:S(2)}, u32[]{:S(2)}) collective-permute-start(f32[1,16,128]{2,1,0:T(8,128)S(1)} %get-tuple-element.30), channel_id=1, source_target_pairs={{0,18},{2,16},{16,2},{18,0},{1,19},{3,17},{17,3},{19,1},{4,22},{6,... | collective-permute-start | bytes 24584 | tf_op jit(solution)/shard_map/ppermute | solution.py:325
  33.6 0.2 collective-permute-start.6
  33.9 1.7 %collective-permute-start.5 = (f32[1,16,128]{2,1,0:T(8,128)S(1)}, f32[1,16,128]{2,1,0:T(8,128)S(1)}, u32[]{:S(2)}, u32[]{:S(2)}) collective-permute-start(f32[1,16,128]{2,1,0:T(8,128)S(1)} %get-tuple-element.32), channel_id=1, source_target_pairs={{0,2},{2,0},{1,3},{3,1},{4,6},{6,4},{5,7},{7,5},{8,10},{10,8},{9,1... | collective-permute-start | bytes 24584 | tf_op jit(solution)/shard_map/ppermute | solution.py:325
  35.6 0.2 collective-permute-done.7.both_ref
  35.7 1.5 %collective-permute-done.6.xl_ref = f32[1,16,128]{2,1,0:T(8,128)S(1)} collective-permute-done((f32[1,16,128]{2,1,0:T(8,128)S(1)}, f32[1,16,128]{2,1,0:T(8,128)S(1)}, u32[]{:S(2)}, u32[]{:S(2)}) %collective-permute-start.6) | collective-permute-done | bytes 8224 | tf_op jit(solution)/shard_map/ppermute | solution.py:325
  37.3 1.7 %collective-permute-done.5.xh_ref = f32[1,16,128]{2,1,0:T(8,128)S(1)} collective-permute-done((f32[1,16,128]{2,1,0:T(8,128)S(1)}, f32[1,16,128]{2,1,0:T(8,128)S(1)}, u32[]{:S(2)}, u32[]{:S(2)}) %collective-permute-start.5) | collective-permute-done | bytes 8224 | tf_op jit(solution)/shard_map/ppermute | solution.py:325
  39.0 0.2 first_image.1
  39.2 13.7 %all_to_all.15.image_cols_ref = f32[288,1,128]{2,1,0:T(1,128)S(1)} all-to-all(f32[288,1,128]{2,1,0:T(1,128)S(1)} %get-tuple-element.22), channel_id=1, replica_groups={{136,140,128,132,164,160,172,168,200,204,192,196,228,224,236,232,8,12,0..., dimensions={0} | all-to-all | bytes 294912 | tf_op jit(solution)/shard_map/all_to_all | solution.py:320
  52.9 3.4 %second_product.1 = (f32[80,128]{1,0:T(8,128)S(1)}, f32[8,128]{1,0:T(8,128)S(1)}) custom-call(f32[32,16,128]{2,1,0:T(8,128)S(1)} %all-to-all-done.cols_ref, f32[288,1,128]{2,1,0:T(1,128)S(1)} %all_to_all.15.image_cols_ref, f32[8,128]{1,0:T(8,128)S(1)} %get-tuple-element.23.image_ref, f32[4096,256]{1,0:T(8,128)S(1)} %get-tuple-element.24.near_ref, ...), custom_call_target="tpu_custom_call" | custom-call | tf_op jit(solution)/shard_map/second_product/pallas_call | solution.py:291
  56.3 0.1 collective-permute-start.8
  56.4 1.2 %collective-permute-done.8.theirs_ref = f32[80,128]{1,0:T(8,128)S(1)} collective-permute-done((f32[80,128]{1,0:T(8,128)S(1)}, f32[80,128]{1,0:T(8,128)S(1)}, u32[]{:S(2)}, u32[]{:S(2)}) %collective-permute-start.8) | collective-permute-done | bytes 40992 | tf_op jit(solution)/shard_map/ppermute | solution.py:325
  57.6 1.1 %collective-permute-start.11 = (f32[88,128]{1,0:T(8,128)S(1)}, f32[88,128]{1,0:T(8,128)S(1)}, u32[]{:S(2)}, u32[]{:S(2)}) collective-permute-start(f32[88,128]{1,0:T(8,128)S(1)} %core_sum.1.own_part), channel_id=1, source_target_pairs={{0,18},{2,16},{16,2},{18,0},{1,19},{3,17},{17,3},{19,1},{4,22},{6,... | collective-permute-start | bytes 135176 | tf_op jit(solution)/shard_map/ppermute | solution.py:325
  58.7 1.0 %collective-permute-start.10 = (f32[88,128]{1,0:T(8,128)S(1)}, f32[88,128]{1,0:T(8,128)S(1)}, u32[]{:S(2)}, u32[]{:S(2)}) collective-permute-start(f32[88,128]{1,0:T(8,128)S(1)} %core_sum.1.own_part), channel_id=1, source_target_pairs={{0,16},{16,0},{1,17},{17,1},{2,18},{18,2},{3,19},{19,3},{4,20},{20... | collective-permute-start | bytes 135176 | tf_op jit(solution)/shard_map/ppermute | solution.py:325
  59.7 2.7 %collective-permute-start.9 = (f32[88,128]{1,0:T(8,128)S(1)}, f32[88,128]{1,0:T(8,128)S(1)}, u32[]{:S(2)}, u32[]{:S(2)}) collective-permute-start(f32[88,128]{1,0:T(8,128)S(1)} %core_sum.1.own_part), channel_id=1, source_target_pairs={{0,2},{2,0},{1,3},{3,1},{4,6},{6,4},{5,7},{7,5},{8,10},{10,8},{9,1... | collective-permute-start | bytes 135176 | tf_op jit(solution)/shard_map/ppermute | solution.py:325
  62.4 0.6 collective-permute-done.11.both_part
  63.0 0.0 collective-permute-done.10.xl_part
  63.0 2.3 %collective-permute-done.9.xh_part = f32[88,128]{1,0:T(8,128)S(1)} collective-permute-done((f32[88,128]{1,0:T(8,128)S(1)}, f32[88,128]{1,0:T(8,128)S(1)}, u32[]{:S(2)}, u32[]{:S(2)}) %collective-permute-start.9) | collective-permute-done | bytes 45088 | tf_op jit(solution)/shard_map/ppermute | solution.py:325
  65.3 0.3 second_image.1
  65.5 12.7 %all_to_all.16.sums_ref = f32[32,1,128]{2,1,0:T(1,128)S(1)} all-to-all(f32[32,1,128]{2,1,0:T(1,128)S(1)} %get-tuple-element.29), channel_id=1, replica_groups={{136,140,128,132,164,160,172,168,200,204,192,196,228,224,236,232,8,12,0..., dimensions={0} | all-to-all | bytes 32768 | tf_op jit(solution)/shard_map/all_to_all | solution.py:320
  78.3 0.9 %finish.1 = (f32[8,128]{1,0:T(8,128)}, f32[8,128]{1,0:T(8,128)}) custom-call(f32[4,8,128]{2,1,0:T(8,128)S(1)} %get-tuple-element.28.own_ref, f32[32,1,128]{2,1,0:T(1,128)S(1)} %all_to_all.16.sums_ref), custom_call_target="tpu_custom_call" | custom-call | tf_op jit(solution)/shard_map/finish/pallas_call | solution.py:291
  (9 shorter events, 0.0 us)
Async XLA Ops:
  2.2 19.5 %all-to-all-start = ((f32[32,16,128]{2,1,0:T(8,128)}), f32[32,16,128]{2,1,0:T(8,128)S(1)}, u32[]{:S(2)}, u32[]{:S(2)}) async-start(f32[32,16,128]{2,1,0:T(8,128)} %get-tuple-element.16), calls=%async_computation | async-start | bytes 524288 | tf_op jit(solution)/shard_map/all_to_all | solution.py:320
  14.5 1.3 %collective-permute-start = (f32[1,16,128]{2,1,0:T(8,128)S(1)}, f32[1,16,128]{2,1,0:T(8,128)S(1)}, u32[]{:S(2)}, u32[]{:S(2)}) collective-permute-start(f32[1,16,128]{2,1,0:T(8,128)S(1)} %get-tuple-element.17), channel_id=1, source_target_pairs={{0,1},{1,0},{2,3},{3,2},{4,5},{5,4},{6,7},{7,6},{8,9},{9,8},{10,11... | collective-permute-start | bytes 24584 | tf_op jit(solution)/shard_map/ppermute | solution.py:325
  15.8 5.2 %collective-permute-start.1 = (f32[2,16,128]{2,1,0:T(8,128)S(1)}, f32[2,16,128]{2,1,0:T(8,128)S(1)}, u32[]{:S(2)}, u32[]{:S(2)}) collective-permute-start(f32[2,16,128]{2,1,0:T(8,128)S(1)} %get-tuple-element.35.near_ref), channel_id=1, source_target_pairs={{0,2},{2,0},{1,3},{3,1},{4,6},{6,4},{5,7},{7,5},{8,10},{10,8},{9,1... | collective-permute-start | bytes 49160 | tf_op jit(solution)/shard_map/ppermute | solution.py:325
  18.8 5.1 %collective-permute-start.3 = (f32[2,16,128]{2,1,0:T(8,128)S(1)}, f32[2,16,128]{2,1,0:T(8,128)S(1)}, u32[]{:S(2)}, u32[]{:S(2)}) collective-permute-start(f32[2,16,128]{2,1,0:T(8,128)S(1)} %get-tuple-element.35.near_ref), channel_id=1, source_target_pairs={{0,18},{2,16},{16,2},{18,0},{1,19},{3,17},{17,3},{19,1},{4,22},{6,... | collective-permute-start | bytes 49160 | tf_op jit(solution)/shard_map/ppermute | solution.py:325
  19.9 4.0 %collective-permute-start.2 = (f32[2,16,128]{2,1,0:T(8,128)S(1)}, f32[2,16,128]{2,1,0:T(8,128)S(1)}, u32[]{:S(2)}, u32[]{:S(2)}) collective-permute-start(f32[2,16,128]{2,1,0:T(8,128)S(1)} %get-tuple-element.35.near_ref), channel_id=1, source_target_pairs={{0,16},{16,0},{1,17},{17,1},{2,18},{18,2},{3,19},{19,3},{4,20},{20... | collective-permute-start | bytes 49160 | tf_op jit(solution)/shard_map/ppermute | solution.py:325
  29.5 1.2 %collective-permute-start.4 = (f32[4,16,128]{2,1,0:T(8,128)S(1)}, f32[4,16,128]{2,1,0:T(8,128)S(1)}, u32[]{:S(2)}, u32[]{:S(2)}) collective-permute-start(f32[4,16,128]{2,1,0:T(8,128)S(1)} %slice_bitcast_fusion), channel_id=1, source_target_pairs={{0,1},{1,0},{2,3},{3,2},{4,5},{5,4},{6,7},{7,6},{8,9},{9,8},{10,11... | collective-permute-start | bytes 98312 | tf_op jit(solution)/shard_map/ppermute | solution.py:325
  30.8 4.9 %collective-permute-start.7 = (f32[1,16,128]{2,1,0:T(8,128)S(1)}, f32[1,16,128]{2,1,0:T(8,128)S(1)}, u32[]{:S(2)}, u32[]{:S(2)}) collective-permute-start(f32[1,16,128]{2,1,0:T(8,128)S(1)} %get-tuple-element.30), channel_id=1, source_target_pairs={{0,18},{2,16},{16,2},{18,0},{1,19},{3,17},{17,3},{19,1},{4,22},{6,... | collective-permute-start | bytes 24584 | tf_op jit(solution)/shard_map/ppermute | solution.py:325
  33.6 3.7 %collective-permute-start.6 = (f32[1,16,128]{2,1,0:T(8,128)S(1)}, f32[1,16,128]{2,1,0:T(8,128)S(1)}, u32[]{:S(2)}, u32[]{:S(2)}) collective-permute-start(f32[1,16,128]{2,1,0:T(8,128)S(1)} %get-tuple-element.31), channel_id=1, source_target_pairs={{0,16},{16,0},{1,17},{17,1},{2,18},{18,2},{3,19},{19,3},{4,20},{20... | collective-permute-start | bytes 24584 | tf_op jit(solution)/shard_map/ppermute | solution.py:325
  33.9 5.2 %collective-permute-start.5 = (f32[1,16,128]{2,1,0:T(8,128)S(1)}, f32[1,16,128]{2,1,0:T(8,128)S(1)}, u32[]{:S(2)}, u32[]{:S(2)}) collective-permute-start(f32[1,16,128]{2,1,0:T(8,128)S(1)} %get-tuple-element.32), channel_id=1, source_target_pairs={{0,2},{2,0},{1,3},{3,1},{4,6},{6,4},{5,7},{7,5},{8,10},{10,8},{9,1... | collective-permute-start | bytes 24584 | tf_op jit(solution)/shard_map/ppermute | solution.py:325
  56.3 1.3 %collective-permute-start.8 = (f32[80,128]{1,0:T(8,128)S(1)}, f32[80,128]{1,0:T(8,128)S(1)}, u32[]{:S(2)}, u32[]{:S(2)}) collective-permute-start(f32[80,128]{1,0:T(8,128)S(1)} %get-tuple-element.26.ours_ref), channel_id=1, source_target_pairs={{0,1},{1,0},{2,3},{3,2},{4,5},{5,4},{6,7},{7,6},{8,9},{9,8},{10,11... | collective-permute-start | bytes 122888 | tf_op jit(solution)/shard_map/ppermute | solution.py:325
  57.6 5.3 %collective-permute-start.11 = (f32[88,128]{1,0:T(8,128)S(1)}, f32[88,128]{1,0:T(8,128)S(1)}, u32[]{:S(2)}, u32[]{:S(2)}) collective-permute-start(f32[88,128]{1,0:T(8,128)S(1)} %core_sum.1.own_part), channel_id=1, source_target_pairs={{0,18},{2,16},{16,2},{18,0},{1,19},{3,17},{17,3},{19,1},{4,22},{6,... | collective-permute-start | bytes 135176 | tf_op jit(solution)/shard_map/ppermute | solution.py:325
  58.7 4.2 %collective-permute-start.10 = (f32[88,128]{1,0:T(8,128)S(1)}, f32[88,128]{1,0:T(8,128)S(1)}, u32[]{:S(2)}, u32[]{:S(2)}) collective-permute-start(f32[88,128]{1,0:T(8,128)S(1)} %core_sum.1.own_part), channel_id=1, source_target_pairs={{0,16},{16,0},{1,17},{17,1},{2,18},{18,2},{3,19},{19,3},{4,20},{20... | collective-permute-start | bytes 135176 | tf_op jit(solution)/shard_map/ppermute | solution.py:325
  59.7 5.6 %collective-permute-start.9 = (f32[88,128]{1,0:T(8,128)S(1)}, f32[88,128]{1,0:T(8,128)S(1)}, u32[]{:S(2)}, u32[]{:S(2)}) collective-permute-start(f32[88,128]{1,0:T(8,128)S(1)} %core_sum.1.own_part), channel_id=1, source_target_pairs={{0,2},{2,0},{1,3},{3,1},{4,6},{6,4},{5,7},{7,5},{8,10},{10,8},{9,1... | collective-permute-start | bytes 135176 | tf_op jit(solution)/shard_map/ppermute | solution.py:325

commit v7 on v6

--- a/solution.py
+++ b/solution.py
@@ -78,27 +78,29 @@
     return jnp.sum(x, axis=1, keepdims=True)
 
 
-def pack(points_hbm, lengthscale_hbm, targets_hbm, own_ref, copies_ref, points_ref, lengthscale_ref, targets_ref, sems):
-    arriving = [
-        pltpu.make_async_copy(points_hbm, points_ref, sems.at[0]),
-        pltpu.make_async_copy(lengthscale_hbm, lengthscale_ref, sems.at[1]),
-        pltpu.make_async_copy(targets_hbm, targets_ref, sems.at[2]),
-    ]
-    for copy in arriving:
-        copy.start()
-    for copy in arriving:
-        copy.wait()
+def pack(points_hbm, targets_hbm, own_ref, copies_ref, sems):
+    points = pltpu.make_async_copy(points_hbm, own_ref.at[0, 0:8, :], sems.at[0])
+    targets = pltpu.make_async_copy(targets_hbm, own_ref.at[0, 8:16, :], sems.at[1])
+    points.start()
+    targets.start()
+    points.wait()
+    targets.wait()
+    for copy in range(NC):
+        copies_ref[copy] = own_ref[0]
+
+
+def near_points(near_ref, lengthscale_hbm, near_out_ref, scale_ref, lengthscale_ref, sem):
+    copy = pltpu.make_async_copy(lengthscale_hbm, lengthscale_ref, sem)
+    copy.start()
+    copy.wait()
     row = lax.broadcasted_iota(jnp.int32, (8, OWN), 0)
     scale = jnp.zeros((8, OWN), f32)
     for k in range(8):
         scale = jnp.where(row == k, lengthscale_ref[k], scale)
-    scaled = points_ref[...] / scale
-    targets = targets_ref[...]
-    own_ref[0, 0:8, :] = scaled
-    own_ref[0, 8:16, :] = targets
-    for copy in range(NC):
-        copies_ref[copy, 0:8, :] = scaled
-        copies_ref[copy, 8:16, :] = targets
+    scale_ref[...] = scale
+    for block in range(2):
+        near_out_ref[block, 0:8, :] = near_ref[block, 0:8, :] / scale
+        near_out_ref[block, 8:16, :] = near_ref[block, 8:16, :]
 
 
 def my_row_block():
@@ -121,8 +123,8 @@
     return jnp.concatenate(out, 1)
 
 
-def near_product(near_ref, cols_ref, kernel_ref, right_ref, part_ref, form_ref):
-    right = features(lanes(cols_ref, 0, NC), False).T.astype(bf16)
+def near_product(near_ref, cols_ref, scale_ref, kernel_ref, right_ref, part_ref, form_ref):
+    right = features(lanes(cols_ref, 0, NC) / scale_ref[:, 0:1], False).T.astype(bf16)
     right_ref[...] = right
     values = stacked(lanes(cols_ref, 8, NC))
     part = first_rows(lanes(near_ref, 0, 2), right, values, kernel_ref)
@@ -131,11 +133,11 @@
     form_ref[...] = part[:, :OWN] * near_ref[0, 8:16, :] + part[:, OWN:] * near_ref[1, 8:16, :]
 
 
-def far_product(xh_ref, xl_ref, both_ref, cols_ref, right_ref, near_part_ref, form_ref, kernel_ref, out_ref):
+def far_product(xh_ref, xl_ref, both_ref, cols_ref, scale_ref, right_ref, near_part_ref, form_ref, kernel_ref, out_ref):
     refs = (xh_ref, xl_ref, both_ref)
     values = stacked(lanes(cols_ref, 8, NC))
     points = jnp.concatenate([lanes(ref, 0, 2) for ref in refs], 1)
-    part = first_rows(points, right_ref, values, kernel_ref)
+    part = first_rows(points / scale_ref[:, 0:1], right_ref, values, kernel_ref)
     form = form_ref[...]
     for core in range(2):
         out_ref[core, 0, 0:8, :] = near_part_ref[core]
@@ -158,7 +160,7 @@
     return out
 
 
-def first_image(own_ref, xh_ref, xl_ref, both_ref, rows_ref, out_ref, image_ref):
+def first_image(own_ref, both_ref, xl_ref, xh_ref, rows_ref, out_ref, image_ref):
     sums = (own_ref[0] + xh_ref[0]) + (xl_ref[0] + both_ref[0])
     targets = rows_ref[0, 8:16, :]
     bb = jnp.zeros((8, OWN), f32)
@@ -207,7 +209,7 @@
     out_ref[pl.ds(pl.multiple_of(sums + 8 - core * 8, 8), 8), :] = theirs_ref[sums:, :]
 
 
-def second_image(own_part, xh_part, xl_part, both_part, rows_ref, scalar_ref, own_ref, out_ref, keep_ref, part_ref):
+def second_image(own_part, both_part, xl_part, xh_part, rows_ref, scalar_ref, own_ref, out_ref, keep_ref, part_ref):
     mine = my_row_block()
     chip = mine // 2
     for k, ref in enumerate((own_part, xh_part, xl_part, both_part)):
@@ -331,26 +333,30 @@
 def per_device(points, lengthscale, targets):
     own, copies = pl.pallas_call(
         pack,
-        in_specs=[pl.BlockSpec(memory_space=pltpu.HBM)] * 3,
+        in_specs=[pl.BlockSpec(memory_space=pltpu.HBM)] * 2,
         out_specs=[pl.BlockSpec(memory_space=VMEM)] * 2,
-        out_shape=[shape(1, 16, OWN), shape(NC, 16, OWN)],
-        scratch_shapes=[
-            pltpu.VMEM((8, OWN), f32),
-            pltpu.SMEM((8,), f32),
-            pltpu.VMEM((8, OWN), f32),
-            pltpu.SemaphoreType.DMA((3,)),
-        ],
+        out_shape=[shape(1, 16, OWN), VMEM((NC, 16, OWN), f32)],
+        scratch_shapes=[pltpu.SemaphoreType.DMA((2,))],
         compiler_params=pltpu.CompilerParams(vmem_limit_bytes=4 << 20),
         name="pack",
-    )(*[pltpu.with_memory_space_constraint(a, pltpu.HBM) for a in (points, lengthscale, targets)])
+    )(*[pltpu.with_memory_space_constraint(a, pltpu.HBM) for a in (points, targets)])
     cols = column_exchange(copies)
     near = jnp.concatenate([own, swap(own, ("core",))], 0)
     far = [swap(near, axes) for axes in CHIPS]
+    scaled_near, scale = pl.pallas_call(
+        near_points,
+        in_specs=[pl.BlockSpec(memory_space=VMEM), pl.BlockSpec(memory_space=pltpu.HBM)],
+        out_specs=[pl.BlockSpec(memory_space=VMEM)] * 2,
+        out_shape=[shape(2, 16, OWN), shape(8, OWN)],
+        scratch_shapes=[pltpu.SMEM((8,), f32), pltpu.SemaphoreType.DMA],
+        compiler_params=pltpu.CompilerParams(vmem_limit_bytes=4 << 20),
+        name="near_points",
+    )(near, pltpu.with_memory_space_constraint(lengthscale, pltpu.HBM))
     near_kernel, right, near_part, form = call(
         near_product,
         [VMEM((NJ, NEAR), f32), jax.ShapeDtypeStruct((NJ, 64), bf16), shape(2, 8, OWN), shape(8, OWN)],
         "near_product",
-        [near, cols],
+        [scaled_near, cols, scale],
         vmem=16 << 20,
         cost=pl.CostEstimate(flops=2 * NJ * NEAR * 128, bytes_accessed=4 * NJ * NEAR, transcendentals=2 * NJ * NEAR),
     )
@@ -358,14 +364,14 @@
         far_product,
         [VMEM((NJ, NI - NEAR), f32), shape(2, 4, 16, OWN)],
         "far_product",
-        far + [cols, right, near_part, form],
+        far + [cols, scale, right, near_part, form],
         vmem=20 << 20,
     )
     rows = jnp.concatenate([near] + far, 0)
     part = part[0] + swap(part[1], ("core",))
     parts = [part[0:1]] + [swap(part[k : k + 1], axes) for k, axes in enumerate(CHIPS, 1)]
     message, image = call(
-        first_image, [shape(NC * 9, 1, OWN), shape(8, OWN)], "first_image", parts + [rows]
+        first_image, [shape(NC * 9, 1, OWN), shape(8, OWN)], "first_image", parts[:1] + parts[:0:-1] + [rows]
     )
     image_cols = column_exchange(message)
     near_kernel = pltpu.with_memory_space_constraint(near_kernel, VMEM)
@@ -385,7 +391,7 @@
         second_image,
         [shape(4, 8, OWN), shape(NC, 1, OWN)],
         "second_image",
-        parts + [rows, scalars],
+        parts[:1] + parts[:0:-1] + [rows, scalars],
         scratch=[pltpu.VMEM((3, NR, 8, OWN), f32), pltpu.VMEM((4, NR * 8 + 24, OWN), f32)],
     )
     sums = column_exchange(message)

time: 79.5 us -> 78.9 us (level)
  starting transfers between devices: 26.3 us -> 25.1 us
    ppermute x12, starting transfers between devices: 14 us -> 12.8 us  [swap(): return lax.ppermute(x, axes, [(i, size - 1 - i) for i in range(size)])]
    pallas_call x1 -> x2, Pallas kernels: 1.54 us -> 2.12 us  [the longest x1 1.43 us: per_device(): pl.pallas_call(pack, in_specs=[pl.BlockSpec(memory_space=pltpu.HBM)] * 2,...]
  transfers between devices with their start and end apart: 13 -> 13, of which waited for: 10 -> 10; matrix products, arithmetic and copies ran while one was open for 0% -> 0% of each run, Pallas kernels for 3% -> 4%
where the time goes in v7:
time: 78.9 us; the launch traced here: 78.6 us
  blocking collectives  26.3 us (33%)
  starting transfers between devices  25.1 us (32%)
  Pallas kernels  14.6 us (19%)
  waiting for transfers between devices  11.8 us (15%)
    all_to_all x2, blocking collectives, column_exchange(): lax.all_to_all(x, AXES, 0, 0, axis_index_groups=column_groups(), tiled=True)  26.3 us
    ppermute x12, starting transfers between devices, swap(): return lax.ppermute(x, axes, [(i, size - 1 - i) for i in range(size)])  12.8 us
    pallas_call x7, Pallas kernels, call(): pl.pallas_call(kernel, in_specs=[pl.BlockSpec(memory_space=VMEM) for _ in...  12.4 us
    all_to_all x1, starting transfers between devices, column_exchange(): lax.all_to_all(x, AXES, 0, 0, axis_index_groups=column_groups(), tiled=True)  12.3 us
    ppermute x12, waiting for transfers between devices, swap(): return lax.ppermute(x, axes, [(i, size - 1 - i) for i in range(size)])  11.1 us
  transfers between devices with their start and end apart: 13, of which 10 were waited for; matrix products, arithmetic and copies ran while one was open for 0% of the time, Pallas kernels for 4%

profile of v7, /device:TPU:8, one launch (start us, length us, event | category | flops | bytes accessed | tf_op | source)
XLA Modules:
  0.0 78.6 jit_solution(2655435174515344032)
XLA Ops:
  0.6 1.4 %pack.1 = (f32[1,16,128]{2,1,0:T(8,128)S(1)}, f32[32,16,128]{2,1,0:T(8,128)}) custom-call(f32[8,128]{1,0:T(8,128)} %points_hbm.1, f32[8,128]{1,0:T(8,128)} %targets_hbm.1), custom_call_target="tpu_custom_call" | custom-call | tf_op jit(solution)/shard_map/pack/pallas_call | solution.py:334
  2.1 12.3 %all-to-all-start = ((f32[32,16,128]{2,1,0:T(8,128)}), f32[32,16,128]{2,1,0:T(8,128)S(1)}, u32[]{:S(2)}, u32[]{:S(2)}) async-start(f32[32,16,128]{2,1,0:T(8,128)} %get-tuple-element.18), calls=%async_computation | async-start | bytes 524288 | tf_op jit(solution)/shard_map/all_to_all | solution.py:322
  14.4 0.1 collective-permute-start
  14.5 1.1 %collective-permute-done = f32[1,16,128]{2,1,0:T(8,128)S(1)} collective-permute-done((f32[1,16,128]{2,1,0:T(8,128)S(1)}, f32[1,16,128]{2,1,0:T(8,128)S(1)}, u32[]{:S(2)}, u32[]{:S(2)}) %collective-permute-start) | collective-permute-done | bytes 8224 | tf_op jit(solution)/shard_map/ppermute | solution.py:327
  15.6 3.0 %collective-permute-start.1 = (f32[2,16,128]{2,1,0:T(8,128)S(1)}, f32[2,16,128]{2,1,0:T(8,128)S(1)}, u32[]{:S(2)}, u32[]{:S(2)}) collective-permute-start(f32[2,16,128]{2,1,0:T(8,128)S(1)} %get-tuple-element.39.near_ref), channel_id=1, source_target_pairs={{0,2},{2,0},{1,3},{3,1},{4,6},{6,4},{5,7},{7,5},{8,10},{10,8},{9,1... | collective-permute-start | bytes 49160 | tf_op jit(solution)/shard_map/ppermute | solution.py:327
  18.7 1.1 %collective-permute-start.3 = (f32[2,16,128]{2,1,0:T(8,128)S(1)}, f32[2,16,128]{2,1,0:T(8,128)S(1)}, u32[]{:S(2)}, u32[]{:S(2)}) collective-permute-start(f32[2,16,128]{2,1,0:T(8,128)S(1)} %get-tuple-element.39.near_ref), channel_id=1, source_target_pairs={{0,18},{2,16},{16,2},{18,0},{1,19},{3,17},{17,3},{19,1},{4,22},{6,... | collective-permute-start | bytes 49160 | tf_op jit(solution)/shard_map/ppermute | solution.py:327
  19.8 0.0 collective-permute-start.2
  19.8 0.7 near_points.1
  20.5 0.4 collective-permute-done.1.xh_ref
  20.9 0.7 all-to-all-done.cols_ref
  21.5 2.2 %near_product.1 = (f32[4096,256]{1,0:T(8,128)S(1)}, bf16[4096,64]{1,0:T(8,128)(2,1)S(1)}, f32[2,8,128]{2,1,0:T(8,128)S(1)}, f32[8,128]{1,0:T(8,128)S(1)}) custom-call(f32[2,16,128]{2,1,0:T(8,128)S(1)} %get-tuple-element.21.near_ref, f32[32,16,128]{2,1,0:T(8,128)S(1)} %all-to-all-done.cols_ref, f32[8,128]{1,0:T(8,128)S(1)} %get-tuple-element.20.scale_ref), custom_call_target="tpu_custom_call" | custom-call | flops 268435456 | bytes 4194304 | tf_op jit(solution)/shard_map/near_product/pallas_call | solution.py:293
  23.8 0.0 collective-permute-done.3.both_ref
  23.8 0.0 collective-permute-done.2.xl_ref
  23.8 5.6 %far_product.1 = (f32[4096,768]{1,0:T(8,128)S(1)}, f32[2,4,16,128]{3,2,1,0:T(8,128)S(1)}) custom-call(f32[2,16,128]{2,1,0:T(8,128)S(1)} %collective-permute-done.1.xh_ref, f32[2,16,128]{2,1,0:T(8,128)S(1)} %collective-permute-done.2.xl_ref, f32[2,16,128]{2,1,0:T(8,128)S(1)} %collective-permute-done.3.both_ref, f32[32,16,128]{2,1,0:T(8,128)S(1)} %all-to-all-done.cols_ref, ...), custom_call_target="tpu_custom_call" | custom-call | tf_op jit(solution)/shard_map/far_product/pallas_call | solution.py:293
  29.5 0.0 collective-permute-start.4
  29.5 1.2 %collective-permute-done.4 = f32[4,16,128]{2,1,0:T(8,128)S(1)} collective-permute-done((f32[4,16,128]{2,1,0:T(8,128)S(1)}, f32[4,16,128]{2,1,0:T(8,128)S(1)}, u32[]{:S(2)}, u32[]{:S(2)}) %collective-permute-start.4) | collective-permute-done | bytes 32800 | tf_op jit(solution)/shard_map/ppermute | solution.py:327
  30.7 3.1 %collective-permute-start.7 = (f32[1,16,128]{2,1,0:T(8,128)S(1)}, f32[1,16,128]{2,1,0:T(8,128)S(1)}, u32[]{:S(2)}, u32[]{:S(2)}) collective-permute-start(f32[1,16,128]{2,1,0:T(8,128)S(1)} %get-tuple-element.34), channel_id=1, source_target_pairs={{0,2},{2,0},{1,3},{3,1},{4,6},{6,4},{5,7},{7,5},{8,10},{10,8},{9,1... | collective-permute-start | bytes 24584 | tf_op jit(solution)/shard_map/ppermute | solution.py:327
  33.8 0.6 collective-permute-start.6
  34.4 0.6 collective-permute-start.5
  35.0 1.0 %collective-permute-done.7.xh_ref = f32[1,16,128]{2,1,0:T(8,128)S(1)} collective-permute-done((f32[1,16,128]{2,1,0:T(8,128)S(1)}, f32[1,16,128]{2,1,0:T(8,128)S(1)}, u32[]{:S(2)}, u32[]{:S(2)}) %collective-permute-start.7) | collective-permute-done | bytes 8224 | tf_op jit(solution)/shard_map/ppermute | solution.py:327
  36.0 1.5 %collective-permute-done.6.xl_ref = f32[1,16,128]{2,1,0:T(8,128)S(1)} collective-permute-done((f32[1,16,128]{2,1,0:T(8,128)S(1)}, f32[1,16,128]{2,1,0:T(8,128)S(1)}, u32[]{:S(2)}, u32[]{:S(2)}) %collective-permute-start.6) | collective-permute-done | bytes 8224 | tf_op jit(solution)/shard_map/ppermute | solution.py:327
  37.5 1.8 %collective-permute-done.5.both_ref = f32[1,16,128]{2,1,0:T(8,128)S(1)} collective-permute-done((f32[1,16,128]{2,1,0:T(8,128)S(1)}, f32[1,16,128]{2,1,0:T(8,128)S(1)}, u32[]{:S(2)}, u32[]{:S(2)}) %collective-permute-start.5) | collective-permute-done | bytes 8224 | tf_op jit(solution)/shard_map/ppermute | solution.py:327
  39.3 0.2 first_image.1
  39.5 13.6 %all_to_all.15.image_cols_ref = f32[288,1,128]{2,1,0:T(1,128)S(1)} all-to-all(f32[288,1,128]{2,1,0:T(1,128)S(1)} %get-tuple-element.26), channel_id=1, replica_groups={{136,140,128,132,164,160,172,168,200,204,192,196,228,224,236,232,8,12,0..., dimensions={0} | all-to-all | bytes 294912 | tf_op jit(solution)/shard_map/all_to_all | solution.py:322
  53.0 3.2 %second_product.1 = (f32[80,128]{1,0:T(8,128)S(1)}, f32[8,128]{1,0:T(8,128)S(1)}) custom-call(f32[32,16,128]{2,1,0:T(8,128)S(1)} %all-to-all-done.cols_ref, f32[288,1,128]{2,1,0:T(1,128)S(1)} %all_to_all.15.image_cols_ref, f32[8,128]{1,0:T(8,128)S(1)} %get-tuple-element.27.image_ref, f32[4096,256]{1,0:T(8,128)S(1)} %get-tuple-element.28.near_ref, ...), custom_call_target="tpu_custom_call" | custom-call | tf_op jit(solution)/shard_map/second_product/pallas_call | solution.py:293
  56.2 0.1 collective-permute-start.8
  56.3 1.2 %collective-permute-done.8.theirs_ref = f32[80,128]{1,0:T(8,128)S(1)} collective-permute-done((f32[80,128]{1,0:T(8,128)S(1)}, f32[80,128]{1,0:T(8,128)S(1)}, u32[]{:S(2)}, u32[]{:S(2)}) %collective-permute-start.8) | collective-permute-done | bytes 40992 | tf_op jit(solution)/shard_map/ppermute | solution.py:327
  57.6 1.0 %collective-permute-start.11 = (f32[88,128]{1,0:T(8,128)S(1)}, f32[88,128]{1,0:T(8,128)S(1)}, u32[]{:S(2)}, u32[]{:S(2)}) collective-permute-start(f32[88,128]{1,0:T(8,128)S(1)} %core_sum.1.own_part), channel_id=1, source_target_pairs={{0,2},{2,0},{1,3},{3,1},{4,6},{6,4},{5,7},{7,5},{8,10},{10,8},{9,1... | collective-permute-start | bytes 135176 | tf_op jit(solution)/shard_map/ppermute | solution.py:327
  58.6 0.8 %collective-permute-start.10 = (f32[88,128]{1,0:T(8,128)S(1)}, f32[88,128]{1,0:T(8,128)S(1)}, u32[]{:S(2)}, u32[]{:S(2)}) collective-permute-start(f32[88,128]{1,0:T(8,128)S(1)} %core_sum.1.own_part), channel_id=1, source_target_pairs={{0,16},{16,0},{1,17},{17,1},{2,18},{18,2},{3,19},{19,3},{4,20},{20... | collective-permute-start | bytes 135176 | tf_op jit(solution)/shard_map/ppermute | solution.py:327
  59.4 2.3 %collective-permute-start.9 = (f32[88,128]{1,0:T(8,128)S(1)}, f32[88,128]{1,0:T(8,128)S(1)}, u32[]{:S(2)}, u32[]{:S(2)}) collective-permute-start(f32[88,128]{1,0:T(8,128)S(1)} %core_sum.1.own_part), channel_id=1, source_target_pairs={{0,18},{2,16},{16,2},{18,0},{1,19},{3,17},{17,3},{19,1},{4,22},{6,... | collective-permute-start | bytes 135176 | tf_op jit(solution)/shard_map/ppermute | solution.py:327
  61.7 1.9 %collective-permute-done.11.xh_part = f32[88,128]{1,0:T(8,128)S(1)} collective-permute-done((f32[88,128]{1,0:T(8,128)S(1)}, f32[88,128]{1,0:T(8,128)S(1)}, u32[]{:S(2)}, u32[]{:S(2)}) %collective-permute-start.11) | collective-permute-done | bytes 45088 | tf_op jit(solution)/shard_map/ppermute | solution.py:327
  63.6 0.0 collective-permute-done.10.xl_part
  63.6 1.0 %collective-permute-done.9.both_part = f32[88,128]{1,0:T(8,128)S(1)} collective-permute-done((f32[88,128]{1,0:T(8,128)S(1)}, f32[88,128]{1,0:T(8,128)S(1)}, u32[]{:S(2)}, u32[]{:S(2)}) %collective-permute-start.9) | collective-permute-done | bytes 45088 | tf_op jit(solution)/shard_map/ppermute | solution.py:327
  64.6 0.3 second_image.1
  64.9 12.7 %all_to_all.16.sums_ref = f32[32,1,128]{2,1,0:T(1,128)S(1)} all-to-all(f32[32,1,128]{2,1,0:T(1,128)S(1)} %get-tuple-element.33), channel_id=1, replica_groups={{136,140,128,132,164,160,172,168,200,204,192,196,228,224,236,232,8,12,0..., dimensions={0} | all-to-all | bytes 32768 | tf_op jit(solution)/shard_map/all_to_all | solution.py:322
  77.7 0.9 %finish.1 = (f32[8,128]{1,0:T(8,128)}, f32[8,128]{1,0:T(8,128)}) custom-call(f32[4,8,128]{2,1,0:T(8,128)S(1)} %get-tuple-element.32.own_ref, f32[32,1,128]{2,1,0:T(1,128)S(1)} %all_to_all.16.sums_ref), custom_call_target="tpu_custom_call" | custom-call | tf_op jit(solution)/shard_map/finish/pallas_call | solution.py:293
  (9 shorter events, 0.0 us)
Async XLA Ops:
  2.1 19.5 %all-to-all-start = ((f32[32,16,128]{2,1,0:T(8,128)}), f32[32,16,128]{2,1,0:T(8,128)S(1)}, u32[]{:S(2)}, u32[]{:S(2)}) async-start(f32[32,16,128]{2,1,0:T(8,128)} %get-tuple-element.18), calls=%async_computation | async-start | bytes 524288 | tf_op jit(solution)/shard_map/all_to_all | solution.py:322
  14.4 1.3 %collective-permute-start = (f32[1,16,128]{2,1,0:T(8,128)S(1)}, f32[1,16,128]{2,1,0:T(8,128)S(1)}, u32[]{:S(2)}, u32[]{:S(2)}) collective-permute-start(f32[1,16,128]{2,1,0:T(8,128)S(1)} %get-tuple-element.19), channel_id=1, source_target_pairs={{0,1},{1,0},{2,3},{3,2},{4,5},{5,4},{6,7},{7,6},{8,9},{9,8},{10,11... | collective-permute-start | bytes 24584 | tf_op jit(solution)/shard_map/ppermute | solution.py:327
  15.6 5.2 %collective-permute-start.1 = (f32[2,16,128]{2,1,0:T(8,128)S(1)}, f32[2,16,128]{2,1,0:T(8,128)S(1)}, u32[]{:S(2)}, u32[]{:S(2)}) collective-permute-start(f32[2,16,128]{2,1,0:T(8,128)S(1)} %get-tuple-element.39.near_ref), channel_id=1, source_target_pairs={{0,2},{2,0},{1,3},{3,1},{4,6},{6,4},{5,7},{7,5},{8,10},{10,8},{9,1... | collective-permute-start | bytes 49160 | tf_op jit(solution)/shard_map/ppermute | solution.py:327
  18.7 5.2 %collective-permute-start.3 = (f32[2,16,128]{2,1,0:T(8,128)S(1)}, f32[2,16,128]{2,1,0:T(8,128)S(1)}, u32[]{:S(2)}, u32[]{:S(2)}) collective-permute-start(f32[2,16,128]{2,1,0:T(8,128)S(1)} %get-tuple-element.39.near_ref), channel_id=1, source_target_pairs={{0,18},{2,16},{16,2},{18,0},{1,19},{3,17},{17,3},{19,1},{4,22},{6,... | collective-permute-start | bytes 49160 | tf_op jit(solution)/shard_map/ppermute | solution.py:327
  19.8 4.0 %collective-permute-start.2 = (f32[2,16,128]{2,1,0:T(8,128)S(1)}, f32[2,16,128]{2,1,0:T(8,128)S(1)}, u32[]{:S(2)}, u32[]{:S(2)}) collective-permute-start(f32[2,16,128]{2,1,0:T(8,128)S(1)} %get-tuple-element.39.near_ref), channel_id=1, source_target_pairs={{0,16},{16,0},{1,17},{17,1},{2,18},{18,2},{3,19},{19,3},{4,20},{20... | collective-permute-start | bytes 49160 | tf_op jit(solution)/shard_map/ppermute | solution.py:327
  29.5 1.2 %collective-permute-start.4 = (f32[4,16,128]{2,1,0:T(8,128)S(1)}, f32[4,16,128]{2,1,0:T(8,128)S(1)}, u32[]{:S(2)}, u32[]{:S(2)}) collective-permute-start(f32[4,16,128]{2,1,0:T(8,128)S(1)} %slice_bitcast_fusion), channel_id=1, source_target_pairs={{0,1},{1,0},{2,3},{3,2},{4,5},{5,4},{6,7},{7,6},{8,9},{9,8},{10,11... | collective-permute-start | bytes 98312 | tf_op jit(solution)/shard_map/ppermute | solution.py:327
  30.7 5.2 %collective-permute-start.7 = (f32[1,16,128]{2,1,0:T(8,128)S(1)}, f32[1,16,128]{2,1,0:T(8,128)S(1)}, u32[]{:S(2)}, u32[]{:S(2)}) collective-permute-start(f32[1,16,128]{2,1,0:T(8,128)S(1)} %get-tuple-element.34), channel_id=1, source_target_pairs={{0,2},{2,0},{1,3},{3,1},{4,6},{6,4},{5,7},{7,5},{8,10},{10,8},{9,1... | collective-permute-start | bytes 24584 | tf_op jit(solution)/shard_map/ppermute | solution.py:327
  33.8 3.7 %collective-permute-start.6 = (f32[1,16,128]{2,1,0:T(8,128)S(1)}, f32[1,16,128]{2,1,0:T(8,128)S(1)}, u32[]{:S(2)}, u32[]{:S(2)}) collective-permute-start(f32[1,16,128]{2,1,0:T(8,128)S(1)} %get-tuple-element.35), channel_id=1, source_target_pairs={{0,16},{16,0},{1,17},{17,1},{2,18},{18,2},{3,19},{19,3},{4,20},{20... | collective-permute-start | bytes 24584 | tf_op jit(solution)/shard_map/ppermute | solution.py:327
  34.4 4.9 %collective-permute-start.5 = (f32[1,16,128]{2,1,0:T(8,128)S(1)}, f32[1,16,128]{2,1,0:T(8,128)S(1)}, u32[]{:S(2)}, u32[]{:S(2)}) collective-permute-start(f32[1,16,128]{2,1,0:T(8,128)S(1)} %get-tuple-element.36), channel_id=1, source_target_pairs={{0,18},{2,16},{16,2},{18,0},{1,19},{3,17},{17,3},{19,1},{4,22},{6,... | collective-permute-start | bytes 24584 | tf_op jit(solution)/shard_map/ppermute | solution.py:327
  56.2 1.3 %collective-permute-start.8 = (f32[80,128]{1,0:T(8,128)S(1)}, f32[80,128]{1,0:T(8,128)S(1)}, u32[]{:S(2)}, u32[]{:S(2)}) collective-permute-start(f32[80,128]{1,0:T(8,128)S(1)} %get-tuple-element.30.ours_ref), channel_id=1, source_target_pairs={{0,1},{1,0},{2,3},{3,2},{4,5},{5,4},{6,7},{7,6},{8,9},{9,8},{10,11... | collective-permute-start | bytes 122888 | tf_op jit(solution)/shard_map/ppermute | solution.py:327
  57.6 6.0 %collective-permute-start.11 = (f32[88,128]{1,0:T(8,128)S(1)}, f32[88,128]{1,0:T(8,128)S(1)}, u32[]{:S(2)}, u32[]{:S(2)}) collective-permute-start(f32[88,128]{1,0:T(8,128)S(1)} %core_sum.1.own_part), channel_id=1, source_target_pairs={{0,2},{2,0},{1,3},{3,1},{4,6},{6,4},{5,7},{7,5},{8,10},{10,8},{9,1... | collective-permute-start | bytes 135176 | tf_op jit(solution)/shard_map/ppermute | solution.py:327
  58.6 5.0 %collective-permute-start.10 = (f32[88,128]{1,0:T(8,128)S(1)}, f32[88,128]{1,0:T(8,128)S(1)}, u32[]{:S(2)}, u32[]{:S(2)}) collective-permute-start(f32[88,128]{1,0:T(8,128)S(1)} %core_sum.1.own_part), channel_id=1, source_target_pairs={{0,16},{16,0},{1,17},{17,1},{2,18},{18,2},{3,19},{19,3},{4,20},{20... | collective-permute-start | bytes 135176 | tf_op jit(solution)/shard_map/ppermute | solution.py:327
  59.4 5.3 %collective-permute-start.9 = (f32[88,128]{1,0:T(8,128)S(1)}, f32[88,128]{1,0:T(8,128)S(1)}, u32[]{:S(2)}, u32[]{:S(2)}) collective-permute-start(f32[88,128]{1,0:T(8,128)S(1)} %core_sum.1.own_part), channel_id=1, source_target_pairs={{0,18},{2,16},{16,2},{18,0},{1,19},{3,17},{17,3},{19,1},{4,22},{6,... | collective-permute-start | bytes 135176 | tf_op jit(solution)/shard_map/ppermute | solution.py:327

commit v8 on v7

--- a/solution.py
+++ b/solution.py
@@ -190,8 +190,9 @@
     for i in range(0, NI, TI):
         acc = jnp.zeros((24, TI), f32)
         kernel_ref, first = (near_ref, i) if i < NEAR else (far_ref, i - NEAR)
-        for j in range(0, NJ, TJ):
-            acc = acc + product(values[:, j : j + TJ], kernel_ref[j : j + TJ, first : first + TI])
+        for j in range(0, NJ, 2 * TJ):
+            tile = kernel_ref[j : j + 2 * TJ, first : first + TI]
+            acc = acc + product(values[:, j : j + 2 * TJ], tile)
         acc = (acc[0:8] + acc[8:16] + acc[16:24]) * FACTOR
         for k in range(TI // OWN):
             row = pl.multiple_of((mine ^ (i // OWN + k)) * 8, 8)

time: 78.9 us -> 79 us (level)
  no operation moved by 1% of the time
where the time goes in v8:
time: 79 us; the launch traced here: 78.7 us
  blocking collectives  26.3 us (33%)
  starting transfers between devices  25.1 us (32%)
  Pallas kernels  14.7 us (19%)
  waiting for transfers between devices  11.8 us (15%)
    all_to_all x2, blocking collectives, column_exchange(): lax.all_to_all(x, AXES, 0, 0, axis_index_groups=column_groups(), tiled=True)  26.3 us
    ppermute x12, starting transfers between devices, swap(): return lax.ppermute(x, axes, [(i, size - 1 - i) for i in range(size)])  12.8 us
    pallas_call x7, Pallas kernels, call(): pl.pallas_call(kernel, in_specs=[pl.BlockSpec(memory_space=VMEM) for _ in...  12.6 us
    all_to_all x1, starting transfers between devices, column_exchange(): lax.all_to_all(x, AXES, 0, 0, axis_index_groups=column_groups(), tiled=True)  12.3 us
    ppermute x12, waiting for transfers between devices, swap(): return lax.ppermute(x, axes, [(i, size - 1 - i) for i in range(size)])  11.1 us
  transfers between devices with their start and end apart: 13, of which 10 were waited for; matrix products, arithmetic and copies ran while one was open for 0% of the time, Pallas kernels for 4%

profile of v8, /device:TPU:8, one launch (start us, length us, event | category | flops | bytes accessed | tf_op | source)
XLA Modules:
  0.0 78.7 jit_solution(7621326043092116207)
XLA Ops:
  0.6 1.4 %pack.1 = (f32[1,16,128]{2,1,0:T(8,128)S(1)}, f32[32,16,128]{2,1,0:T(8,128)}) custom-call(f32[8,128]{1,0:T(8,128)} %points_hbm.1, f32[8,128]{1,0:T(8,128)} %targets_hbm.1), custom_call_target="tpu_custom_call" | custom-call | tf_op jit(solution)/shard_map/pack/pallas_call | solution.py:335
  2.1 12.3 %all-to-all-start = ((f32[32,16,128]{2,1,0:T(8,128)}), f32[32,16,128]{2,1,0:T(8,128)S(1)}, u32[]{:S(2)}, u32[]{:S(2)}) async-start(f32[32,16,128]{2,1,0:T(8,128)} %get-tuple-element.18), calls=%async_computation | async-start | bytes 524288 | tf_op jit(solution)/shard_map/all_to_all | solution.py:323
  14.4 0.1 collective-permute-start
  14.5 1.1 %collective-permute-done = f32[1,16,128]{2,1,0:T(8,128)S(1)} collective-permute-done((f32[1,16,128]{2,1,0:T(8,128)S(1)}, f32[1,16,128]{2,1,0:T(8,128)S(1)}, u32[]{:S(2)}, u32[]{:S(2)}) %collective-permute-start) | collective-permute-done | bytes 8224 | tf_op jit(solution)/shard_map/ppermute | solution.py:328
  15.6 3.0 %collective-permute-start.1 = (f32[2,16,128]{2,1,0:T(8,128)S(1)}, f32[2,16,128]{2,1,0:T(8,128)S(1)}, u32[]{:S(2)}, u32[]{:S(2)}) collective-permute-start(f32[2,16,128]{2,1,0:T(8,128)S(1)} %get-tuple-element.39.near_ref), channel_id=1, source_target_pairs={{0,2},{2,0},{1,3},{3,1},{4,6},{6,4},{5,7},{7,5},{8,10},{10,8},{9,1... | collective-permute-start | bytes 49160 | tf_op jit(solution)/shard_map/ppermute | solution.py:328
  18.7 1.1 %collective-permute-start.3 = (f32[2,16,128]{2,1,0:T(8,128)S(1)}, f32[2,16,128]{2,1,0:T(8,128)S(1)}, u32[]{:S(2)}, u32[]{:S(2)}) collective-permute-start(f32[2,16,128]{2,1,0:T(8,128)S(1)} %get-tuple-element.39.near_ref), channel_id=1, source_target_pairs={{0,18},{2,16},{16,2},{18,0},{1,19},{3,17},{17,3},{19,1},{4,22},{6,... | collective-permute-start | bytes 49160 | tf_op jit(solution)/shard_map/ppermute | solution.py:328
  19.8 0.0 collective-permute-start.2
  19.8 0.7 near_points.1
  20.5 0.4 collective-permute-done.1.xh_ref
  20.9 0.7 all-to-all-done.cols_ref
  21.5 2.2 %near_product.1 = (f32[4096,256]{1,0:T(8,128)S(1)}, bf16[4096,64]{1,0:T(8,128)(2,1)S(1)}, f32[2,8,128]{2,1,0:T(8,128)S(1)}, f32[8,128]{1,0:T(8,128)S(1)}) custom-call(f32[2,16,128]{2,1,0:T(8,128)S(1)} %get-tuple-element.21.near_ref, f32[32,16,128]{2,1,0:T(8,128)S(1)} %all-to-all-done.cols_ref, f32[8,128]{1,0:T(8,128)S(1)} %get-tuple-element.20.scale_ref), custom_call_target="tpu_custom_call" | custom-call | flops 268435456 | bytes 4194304 | tf_op jit(solution)/shard_map/near_product/pallas_call | solution.py:294
  23.8 0.0 collective-permute-done.3.both_ref
  23.8 0.0 collective-permute-done.2.xl_ref
  23.8 5.6 %far_product.1 = (f32[4096,768]{1,0:T(8,128)S(1)}, f32[2,4,16,128]{3,2,1,0:T(8,128)S(1)}) custom-call(f32[2,16,128]{2,1,0:T(8,128)S(1)} %collective-permute-done.1.xh_ref, f32[2,16,128]{2,1,0:T(8,128)S(1)} %collective-permute-done.2.xl_ref, f32[2,16,128]{2,1,0:T(8,128)S(1)} %collective-permute-done.3.both_ref, f32[32,16,128]{2,1,0:T(8,128)S(1)} %all-to-all-done.cols_ref, ...), custom_call_target="tpu_custom_call" | custom-call | tf_op jit(solution)/shard_map/far_product/pallas_call | solution.py:294
  29.5 0.0 collective-permute-start.4
  29.5 1.2 %collective-permute-done.4 = f32[4,16,128]{2,1,0:T(8,128)S(1)} collective-permute-done((f32[4,16,128]{2,1,0:T(8,128)S(1)}, f32[4,16,128]{2,1,0:T(8,128)S(1)}, u32[]{:S(2)}, u32[]{:S(2)}) %collective-permute-start.4) | collective-permute-done | bytes 32800 | tf_op jit(solution)/shard_map/ppermute | solution.py:328
  30.7 3.1 %collective-permute-start.7 = (f32[1,16,128]{2,1,0:T(8,128)S(1)}, f32[1,16,128]{2,1,0:T(8,128)S(1)}, u32[]{:S(2)}, u32[]{:S(2)}) collective-permute-start(f32[1,16,128]{2,1,0:T(8,128)S(1)} %get-tuple-element.34), channel_id=1, source_target_pairs={{0,2},{2,0},{1,3},{3,1},{4,6},{6,4},{5,7},{7,5},{8,10},{10,8},{9,1... | collective-permute-start | bytes 24584 | tf_op jit(solution)/shard_map/ppermute | solution.py:328
  33.8 0.6 collective-permute-start.6
  34.4 0.6 collective-permute-start.5
  35.0 1.0 %collective-permute-done.7.xh_ref = f32[1,16,128]{2,1,0:T(8,128)S(1)} collective-permute-done((f32[1,16,128]{2,1,0:T(8,128)S(1)}, f32[1,16,128]{2,1,0:T(8,128)S(1)}, u32[]{:S(2)}, u32[]{:S(2)}) %collective-permute-start.7) | collective-permute-done | bytes 8224 | tf_op jit(solution)/shard_map/ppermute | solution.py:328
  36.0 1.5 %collective-permute-done.6.xl_ref = f32[1,16,128]{2,1,0:T(8,128)S(1)} collective-permute-done((f32[1,16,128]{2,1,0:T(8,128)S(1)}, f32[1,16,128]{2,1,0:T(8,128)S(1)}, u32[]{:S(2)}, u32[]{:S(2)}) %collective-permute-start.6) | collective-permute-done | bytes 8224 | tf_op jit(solution)/shard_map/ppermute | solution.py:328
  37.5 1.8 %collective-permute-done.5.both_ref = f32[1,16,128]{2,1,0:T(8,128)S(1)} collective-permute-done((f32[1,16,128]{2,1,0:T(8,128)S(1)}, f32[1,16,128]{2,1,0:T(8,128)S(1)}, u32[]{:S(2)}, u32[]{:S(2)}) %collective-permute-start.5) | collective-permute-done | bytes 8224 | tf_op jit(solution)/shard_map/ppermute | solution.py:328
  39.3 0.2 first_image.1
  39.5 13.6 %all_to_all.15.image_cols_ref = f32[288,1,128]{2,1,0:T(1,128)S(1)} all-to-all(f32[288,1,128]{2,1,0:T(1,128)S(1)} %get-tuple-element.26), channel_id=1, replica_groups={{136,140,128,132,164,160,172,168,200,204,192,196,228,224,236,232,8,12,0..., dimensions={0} | all-to-all | bytes 294912 | tf_op jit(solution)/shard_map/all_to_all | solution.py:323
  53.0 3.3 %second_product.1 = (f32[80,128]{1,0:T(8,128)S(1)}, f32[8,128]{1,0:T(8,128)S(1)}) custom-call(f32[32,16,128]{2,1,0:T(8,128)S(1)} %all-to-all-done.cols_ref, f32[288,1,128]{2,1,0:T(1,128)S(1)} %all_to_all.15.image_cols_ref, f32[8,128]{1,0:T(8,128)S(1)} %get-tuple-element.27.image_ref, f32[4096,256]{1,0:T(8,128)S(1)} %get-tuple-element.28.near_ref, ...), custom_call_target="tpu_custom_call" | custom-call | tf_op jit(solution)/shard_map/second_product/pallas_call | solution.py:294
  56.4 0.1 collective-permute-start.8
  56.5 1.2 %collective-permute-done.8.theirs_ref = f32[80,128]{1,0:T(8,128)S(1)} collective-permute-done((f32[80,128]{1,0:T(8,128)S(1)}, f32[80,128]{1,0:T(8,128)S(1)}, u32[]{:S(2)}, u32[]{:S(2)}) %collective-permute-start.8) | collective-permute-done | bytes 40992 | tf_op jit(solution)/shard_map/ppermute | solution.py:328
  57.7 1.0 %collective-permute-start.11 = (f32[88,128]{1,0:T(8,128)S(1)}, f32[88,128]{1,0:T(8,128)S(1)}, u32[]{:S(2)}, u32[]{:S(2)}) collective-permute-start(f32[88,128]{1,0:T(8,128)S(1)} %core_sum.1.own_part), channel_id=1, source_target_pairs={{0,2},{2,0},{1,3},{3,1},{4,6},{6,4},{5,7},{7,5},{8,10},{10,8},{9,1... | collective-permute-start | bytes 135176 | tf_op jit(solution)/shard_map/ppermute | solution.py:328
  58.7 0.8 %collective-permute-start.10 = (f32[88,128]{1,0:T(8,128)S(1)}, f32[88,128]{1,0:T(8,128)S(1)}, u32[]{:S(2)}, u32[]{:S(2)}) collective-permute-start(f32[88,128]{1,0:T(8,128)S(1)} %core_sum.1.own_part), channel_id=1, source_target_pairs={{0,16},{16,0},{1,17},{17,1},{2,18},{18,2},{3,19},{19,3},{4,20},{20... | collective-permute-start | bytes 135176 | tf_op jit(solution)/shard_map/ppermute | solution.py:328
  59.5 2.3 %collective-permute-start.9 = (f32[88,128]{1,0:T(8,128)S(1)}, f32[88,128]{1,0:T(8,128)S(1)}, u32[]{:S(2)}, u32[]{:S(2)}) collective-permute-start(f32[88,128]{1,0:T(8,128)S(1)} %core_sum.1.own_part), channel_id=1, source_target_pairs={{0,18},{2,16},{16,2},{18,0},{1,19},{3,17},{17,3},{19,1},{4,22},{6,... | collective-permute-start | bytes 135176 | tf_op jit(solution)/shard_map/ppermute | solution.py:328
  61.9 1.9 %collective-permute-done.11.xh_part = f32[88,128]{1,0:T(8,128)S(1)} collective-permute-done((f32[88,128]{1,0:T(8,128)S(1)}, f32[88,128]{1,0:T(8,128)S(1)}, u32[]{:S(2)}, u32[]{:S(2)}) %collective-permute-start.11) | collective-permute-done | bytes 45088 | tf_op jit(solution)/shard_map/ppermute | solution.py:328
  63.7 0.0 collective-permute-done.10.xl_part
  63.7 1.0 %collective-permute-done.9.both_part = f32[88,128]{1,0:T(8,128)S(1)} collective-permute-done((f32[88,128]{1,0:T(8,128)S(1)}, f32[88,128]{1,0:T(8,128)S(1)}, u32[]{:S(2)}, u32[]{:S(2)}) %collective-permute-start.9) | collective-permute-done | bytes 45088 | tf_op jit(solution)/shard_map/ppermute | solution.py:328
  64.8 0.3 second_image.1
  65.1 12.7 %all_to_all.16.sums_ref = f32[32,1,128]{2,1,0:T(1,128)S(1)} all-to-all(f32[32,1,128]{2,1,0:T(1,128)S(1)} %get-tuple-element.33), channel_id=1, replica_groups={{136,140,128,132,164,160,172,168,200,204,192,196,228,224,236,232,8,12,0..., dimensions={0} | all-to-all | bytes 32768 | tf_op jit(solution)/shard_map/all_to_all | solution.py:323
  77.8 0.9 %finish.1 = (f32[8,128]{1,0:T(8,128)}, f32[8,128]{1,0:T(8,128)}) custom-call(f32[4,8,128]{2,1,0:T(8,128)S(1)} %get-tuple-element.32.own_ref, f32[32,1,128]{2,1,0:T(1,128)S(1)} %all_to_all.16.sums_ref), custom_call_target="tpu_custom_call" | custom-call | tf_op jit(solution)/shard_map/finish/pallas_call | solution.py:294
  (9 shorter events, 0.0 us)
Async XLA Ops:
  2.1 19.5 %all-to-all-start = ((f32[32,16,128]{2,1,0:T(8,128)}), f32[32,16,128]{2,1,0:T(8,128)S(1)}, u32[]{:S(2)}, u32[]{:S(2)}) async-start(f32[32,16,128]{2,1,0:T(8,128)} %get-tuple-element.18), calls=%async_computation | async-start | bytes 524288 | tf_op jit(solution)/shard_map/all_to_all | solution.py:323
  14.4 1.3 %collective-permute-start = (f32[1,16,128]{2,1,0:T(8,128)S(1)}, f32[1,16,128]{2,1,0:T(8,128)S(1)}, u32[]{:S(2)}, u32[]{:S(2)}) collective-permute-start(f32[1,16,128]{2,1,0:T(8,128)S(1)} %get-tuple-element.19), channel_id=1, source_target_pairs={{0,1},{1,0},{2,3},{3,2},{4,5},{5,4},{6,7},{7,6},{8,9},{9,8},{10,11... | collective-permute-start | bytes 24584 | tf_op jit(solution)/shard_map/ppermute | solution.py:328
  15.6 5.2 %collective-permute-start.1 = (f32[2,16,128]{2,1,0:T(8,128)S(1)}, f32[2,16,128]{2,1,0:T(8,128)S(1)}, u32[]{:S(2)}, u32[]{:S(2)}) collective-permute-start(f32[2,16,128]{2,1,0:T(8,128)S(1)} %get-tuple-element.39.near_ref), channel_id=1, source_target_pairs={{0,2},{2,0},{1,3},{3,1},{4,6},{6,4},{5,7},{7,5},{8,10},{10,8},{9,1... | collective-permute-start | bytes 49160 | tf_op jit(solution)/shard_map/ppermute | solution.py:328
  18.7 5.2 %collective-permute-start.3 = (f32[2,16,128]{2,1,0:T(8,128)S(1)}, f32[2,16,128]{2,1,0:T(8,128)S(1)}, u32[]{:S(2)}, u32[]{:S(2)}) collective-permute-start(f32[2,16,128]{2,1,0:T(8,128)S(1)} %get-tuple-element.39.near_ref), channel_id=1, source_target_pairs={{0,18},{2,16},{16,2},{18,0},{1,19},{3,17},{17,3},{19,1},{4,22},{6,... | collective-permute-start | bytes 49160 | tf_op jit(solution)/shard_map/ppermute | solution.py:328
  19.8 4.0 %collective-permute-start.2 = (f32[2,16,128]{2,1,0:T(8,128)S(1)}, f32[2,16,128]{2,1,0:T(8,128)S(1)}, u32[]{:S(2)}, u32[]{:S(2)}) collective-permute-start(f32[2,16,128]{2,1,0:T(8,128)S(1)} %get-tuple-element.39.near_ref), channel_id=1, source_target_pairs={{0,16},{16,0},{1,17},{17,1},{2,18},{18,2},{3,19},{19,3},{4,20},{20... | collective-permute-start | bytes 49160 | tf_op jit(solution)/shard_map/ppermute | solution.py:328
  29.5 1.2 %collective-permute-start.4 = (f32[4,16,128]{2,1,0:T(8,128)S(1)}, f32[4,16,128]{2,1,0:T(8,128)S(1)}, u32[]{:S(2)}, u32[]{:S(2)}) collective-permute-start(f32[4,16,128]{2,1,0:T(8,128)S(1)} %slice_bitcast_fusion), channel_id=1, source_target_pairs={{0,1},{1,0},{2,3},{3,2},{4,5},{5,4},{6,7},{7,6},{8,9},{9,8},{10,11... | collective-permute-start | bytes 98312 | tf_op jit(solution)/shard_map/ppermute | solution.py:328
  30.7 5.2 %collective-permute-start.7 = (f32[1,16,128]{2,1,0:T(8,128)S(1)}, f32[1,16,128]{2,1,0:T(8,128)S(1)}, u32[]{:S(2)}, u32[]{:S(2)}) collective-permute-start(f32[1,16,128]{2,1,0:T(8,128)S(1)} %get-tuple-element.34), channel_id=1, source_target_pairs={{0,2},{2,0},{1,3},{3,1},{4,6},{6,4},{5,7},{7,5},{8,10},{10,8},{9,1... | collective-permute-start | bytes 24584 | tf_op jit(solution)/shard_map/ppermute | solution.py:328
  33.8 3.7 %collective-permute-start.6 = (f32[1,16,128]{2,1,0:T(8,128)S(1)}, f32[1,16,128]{2,1,0:T(8,128)S(1)}, u32[]{:S(2)}, u32[]{:S(2)}) collective-permute-start(f32[1,16,128]{2,1,0:T(8,128)S(1)} %get-tuple-element.35), channel_id=1, source_target_pairs={{0,16},{16,0},{1,17},{17,1},{2,18},{18,2},{3,19},{19,3},{4,20},{20... | collective-permute-start | bytes 24584 | tf_op jit(solution)/shard_map/ppermute | solution.py:328
  34.4 4.9 %collective-permute-start.5 = (f32[1,16,128]{2,1,0:T(8,128)S(1)}, f32[1,16,128]{2,1,0:T(8,128)S(1)}, u32[]{:S(2)}, u32[]{:S(2)}) collective-permute-start(f32[1,16,128]{2,1,0:T(8,128)S(1)} %get-tuple-element.36), channel_id=1, source_target_pairs={{0,18},{2,16},{16,2},{18,0},{1,19},{3,17},{17,3},{19,1},{4,22},{6,... | collective-permute-start | bytes 24584 | tf_op jit(solution)/shard_map/ppermute | solution.py:328
  56.4 1.3 %collective-permute-start.8 = (f32[80,128]{1,0:T(8,128)S(1)}, f32[80,128]{1,0:T(8,128)S(1)}, u32[]{:S(2)}, u32[]{:S(2)}) collective-permute-start(f32[80,128]{1,0:T(8,128)S(1)} %get-tuple-element.30.ours_ref), channel_id=1, source_target_pairs={{0,1},{1,0},{2,3},{3,2},{4,5},{5,4},{6,7},{7,6},{8,9},{9,8},{10,11... | collective-permute-start | bytes 122888 | tf_op jit(solution)/shard_map/ppermute | solution.py:328
  57.7 6.0 %collective-permute-start.11 = (f32[88,128]{1,0:T(8,128)S(1)}, f32[88,128]{1,0:T(8,128)S(1)}, u32[]{:S(2)}, u32[]{:S(2)}) collective-permute-start(f32[88,128]{1,0:T(8,128)S(1)} %core_sum.1.own_part), channel_id=1, source_target_pairs={{0,2},{2,0},{1,3},{3,1},{4,6},{6,4},{5,7},{7,5},{8,10},{10,8},{9,1... | collective-permute-start | bytes 135176 | tf_op jit(solution)/shard_map/ppermute | solution.py:328
  58.7 5.0 %collective-permute-start.10 = (f32[88,128]{1,0:T(8,128)S(1)}, f32[88,128]{1,0:T(8,128)S(1)}, u32[]{:S(2)}, u32[]{:S(2)}) collective-permute-start(f32[88,128]{1,0:T(8,128)S(1)} %core_sum.1.own_part), channel_id=1, source_target_pairs={{0,16},{16,0},{1,17},{17,1},{2,18},{18,2},{3,19},{19,3},{4,20},{20... | collective-permute-start | bytes 135176 | tf_op jit(solution)/shard_map/ppermute | solution.py:328
  59.5 5.3 %collective-permute-start.9 = (f32[88,128]{1,0:T(8,128)S(1)}, f32[88,128]{1,0:T(8,128)S(1)}, u32[]{:S(2)}, u32[]{:S(2)}) collective-permute-start(f32[88,128]{1,0:T(8,128)S(1)} %core_sum.1.own_part), channel_id=1, source_target_pairs={{0,18},{2,16},{16,2},{18,0},{1,19},{3,17},{17,3},{19,1},{4,22},{6,... | collective-permute-start | bytes 135176 | tf_op jit(solution)/shard_map/ppermute | solution.py:328
